TPU v7x, 32 devices: a whole 2x2x4 slice. The times are simulated.
32 devices in a mesh: freq: 2 (over y), clus: 4 (over z), rows: 4 (over x, core).
Axes of the slice: x: 2, y: 2, z: 4, core: 2. Of those that a mesh axis runs over, the one named last changes fastest.
Arguments:
- excitation: bfloat16 [8192, 2, 128], P(('freq', 'clus', 'rows')), parts along dimension 0, may hold values from -6 to 6
- leaf_factor: bfloat16 [4, 4, 4, 32, 1024], P('freq', 'clus', None, 'rows'), parts along dimension 0, may hold values from -0.125 to 0.125
- coupling: bfloat16 [4, 4, 4, 32, 1024], P('freq', 'clus', None, 'rows'), parts along dimension 0, may hold values from -0.375 to 0.375
- ranks: int32 [8, 4], P('freq'), parts along dimension 0, may hold values from 8 to 32, as said below
Outputs:
- field: bfloat16 [8192, 2, 128], P(('freq', 'clus', 'rows')), parts along dimension 0
There are 2 independent parts, one for each index of `freq`. A program takes and returns all parts, laid end to end along the dimension named above; each array names one. Nothing has to cross between parts.
Inputs may be any that keep to these rules, and one draw needn't show every extreme that they name: `ranks`: each block's rank.
All inputs are finite; a program needn't handle non-finite values.
Results may differ from a plain program's by a relative error of at most 0.0076.
Values may be sent and summed in bfloat16 or wider, within the bound.
No kernel may reach another device: no remote copies, remote signals or barrier semaphores. Data moves between devices by JAX's collectives and lax.ppermute only.
A program may use at most 64 MiB of HBM per device.

v0:
```python
import jax
import jax.numpy as jnp
from jax import lax
from jax.sharding import PartitionSpec as P

STEPS = 3


def complex_dot(a_real, a_imag, b_real, b_imag):
    real_part = jnp.dot(a_real, b_real, preferred_element_type=jnp.float32) - jnp.dot(
        a_imag, b_imag, preferred_element_type=jnp.float32
    )
    imag_part = jnp.dot(a_real, b_imag, preferred_element_type=jnp.float32) + jnp.dot(
        a_imag, b_real, preferred_element_type=jnp.float32
    )
    return (real_part, imag_part)


def transposed_dot(columns, skel_flat):
    real_part = jnp.einsum(
        "km,kr->mr", columns[0], skel_flat[0], preferred_element_type=jnp.float32
    ) - jnp.einsum("km,kr->mr", columns[1], skel_flat[1], preferred_element_type=jnp.float32)
    imag_part = jnp.einsum(
        "km,kr->mr", columns[0], skel_flat[1], preferred_element_type=jnp.float32
    ) + jnp.einsum("km,kr->mr", columns[1], skel_flat[0], preferred_element_type=jnp.float32)
    return jnp.stack([real_part, imag_part], axis=1)


def apply_once(current, factor, weights, keep_mask, clusters, quarter, leaf_size, angles, part_row):
    gathered = lax.all_gather(current, "rows", axis=0, tiled=True)
    real_part, imag_part = complex_dot(factor[0], factor[1], gathered[:, 0], gathered[:, 1])
    skeleton = (
        jnp.stack([real_part, imag_part]).astype(jnp.bfloat16).reshape(2, clusters, quarter, angles)
    )
    received = lax.all_to_all(skeleton, "clus", split_axis=1, concat_axis=1, tiled=True)
    received = received * keep_mask[None, :, :, None]
    skel_flat = received.reshape(2, clusters * quarter, angles)
    share_rows = leaf_size // lax.axis_size("rows")
    partial_sum = transposed_dot(weights, skel_flat)
    summed = lax.psum(partial_sum, "rows")
    own_rows = lax.dynamic_slice_in_dim(summed, part_row * share_rows, share_rows, 0)
    return own_rows.astype(jnp.bfloat16)


def body(excitation, leaf_factor, coupling, ranks):
    cluster = lax.axis_index("clus")
    part_row = lax.axis_index("rows")
    clusters = leaf_factor.shape[2]
    quarter = leaf_factor.shape[3]
    leaf_size = leaf_factor.shape[4]
    angles = excitation.shape[2]
    factor = leaf_factor.reshape(2, clusters * quarter, leaf_size)
    weights = coupling.reshape(2, clusters * quarter, leaf_size)
    rank_row = lax.dynamic_slice_in_dim(ranks, cluster, 1, 0)[0]
    rank_level = part_row * quarter + jnp.arange(quarter, dtype=jnp.int32)
    keep_mask = (rank_level[None, :] < rank_row[:, None]).astype(jnp.bfloat16)
    current = excitation
    for step in range(STEPS):
        current = apply_once(
            current, factor, weights, keep_mask, clusters, quarter, leaf_size, angles, part_row
        )
    return current


def solution(mesh):
    placed = (
        P(("freq", "clus", "rows"), None, None),
        P("freq", "clus", None, "rows", None),
        P("freq", "clus", None, "rows", None),
        P("freq", None),
    )
    return jax.shard_map(
        body,
        mesh=mesh,
        in_specs=placed,
        out_specs=P(("freq", "clus", "rows"), None, None),
        check_vma=False,
    )
```

profile of v0, /device:TPU:0, one launch (start us, length us, event | category | flops | bytes accessed | tf_op | source)
XLA Modules:
  0.0 134.5 jit_solution(16988357831519295893)
XLA Ops:
  0.0 0.9 copy.8
  1.0 8.8 %all_gather.9 = bf16[1024,2,128]{2,0,1:T(8,128)(2,1)S(1)} all-gather(bf16[256,2,128]{2,0,1:T(8,128)(2,1)S(1)} %copy.8), channel_id=1, replica_groups=mesh['freq'=2,'clus'=4,'rows'=4] {'rows'}, dimensions={0}, use_global_device_ids=true | all-gather | bytes 655360 | tf_op jit(solution)/shard_map/all_gather | solution.py:30
  10.4 0.6 pad_maximum_fusion.3
  11.0 4.9 %all-to-all-start = ((bf16[2,4,8,128]{3,2,0,1:T(8,128)(2,1)}), bf16[2,4,8,128]{3,2,0,1:T(8,128)(2,1)S(1)}, u32[]{:S(2)}, u32[]{:S(2)}) async-start(bf16[2,4,8,128]{3,2,0,1:T(8,128)(2,1)} %pad_maximum_fusion.3), calls=%async_computation | async-start | bytes 32768 | tf_op jit(solution)/shard_map/all_to_all | solution.py:35
  16.0 5.5 %all-to-all-done = bf16[2,4,8,128]{3,2,0,1:T(8,128)(2,1)S(1)} async-done(((bf16[2,4,8,128]{3,2,0,1:T(8,128)(2,1)}), bf16[2,4,8,128]{3,2,0,1:T(8,128)(2,1)S(1)}, u32[]{:S(2)}, u32[]{:S(2)}) %all-to-all-start) | async-done | bytes 16416 | tf_op jit(solution)/shard_map/all_to_all | solution.py:35
  21.6 0.2 fusion.38
  21.8 0.2 fusion.40
  22.1 0.3 fusion.4
  22.3 0.2 fusion.5
  22.7 25.8 %all-reduce.3 = bf16[1024,2,128]{0,2,1:T(8,128)(2,1)S(1)} all-reduce(f32[1024,2,128]{0,2,1:T(8,128)S(1)} %pad_maximum_fusion), channel_id=1, replica_groups=mesh['freq'=2,'clus'=4,'rows'=4] {'rows'}, use_global_device_ids=true, to_apply=%region_0.0 | all-reduce | flops 262144 | bytes 1572864 | tf_op jit(solution)/shard_map/psum | solution.py:40
  48.5 7.3 %all_gather.10 = bf16[1024,2,128]{0,2,1:T(8,128)(2,1)S(1)} all-gather(bf16[256,2,128]{0,2,1:T(8,128)(2,1)S(1)} %dynamic-slice_convert_fusion.2), channel_id=1, replica_groups=mesh['freq'=2,'clus'=4,'rows'=4] {'rows'}, dimensions={0}, use_global_device_ids=true | all-gather | bytes 655360 | tf_op jit(solution)/shard_map/all_gather | solution.py:30
  56.6 8.0 %all_to_all.15 = bf16[2,4,8,128]{3,2,0,1:T(8,128)(2,1)S(1)} all-to-all(bf16[2,4,8,128]{3,2,0,1:T(8,128)(2,1)S(1)} %pad_maximum_fusion.4), channel_id=1, replica_groups=mesh['freq'=2,'clus'=4,'rows'=4] {'clus'}, dimensions={1} | all-to-all | bytes 32768 | tf_op jit(solution)/shard_map/all_to_all | solution.py:35
  64.6 0.2 fusion.34
  64.9 0.2 fusion.36
  65.1 0.3 fusion.2
  65.4 0.2 fusion.3
  65.7 25.5 %all-reduce.4 = bf16[1024,2,128]{0,2,1:T(8,128)(2,1)S(1)} all-reduce(f32[1024,2,128]{0,2,1:T(8,128)S(1)} %pad_maximum_fusion.1), channel_id=1, replica_groups=mesh['freq'=2,'clus'=4,'rows'=4] {'rows'}, use_global_device_ids=true, to_apply=%region_1.0 | all-reduce | flops 262144 | bytes 1572864 | tf_op jit(solution)/shard_map/psum | solution.py:40
  91.2 7.2 %all_gather.11 = bf16[1024,2,128]{0,2,1:T(8,128)(2,1)S(1)} all-gather(bf16[256,2,128]{0,2,1:T(8,128)(2,1)S(1)} %dynamic-slice_convert_fusion.1), channel_id=1, replica_groups=mesh['freq'=2,'clus'=4,'rows'=4] {'rows'}, dimensions={0}, use_global_device_ids=true | all-gather | bytes 655360 | tf_op jit(solution)/shard_map/all_gather | solution.py:30
  99.3 8.0 %all_to_all.16 = bf16[2,4,8,128]{3,2,0,1:T(8,128)(2,1)S(1)} all-to-all(bf16[2,4,8,128]{3,2,0,1:T(8,128)(2,1)S(1)} %pad_maximum_fusion.5), channel_id=1, replica_groups=mesh['freq'=2,'clus'=4,'rows'=4] {'clus'}, dimensions={1} | all-to-all | bytes 32768 | tf_op jit(solution)/shard_map/all_to_all | solution.py:35
  107.3 0.2 fusion.30
  107.6 0.2 fusion.32
  107.8 0.3 fusion
  108.4 25.3 %all-reduce.5 = bf16[1024,2,128]{0,2,1:T(8,128)(2,1)S(1)} all-reduce(f32[1024,2,128]{0,2,1:T(8,128)S(1)} %pad_maximum_fusion.2), channel_id=1, replica_groups=mesh['freq'=2,'clus'=4,'rows'=4] {'rows'}, use_global_device_ids=true, to_apply=%region_2.0 | all-reduce | flops 262144 | bytes 1572864 | tf_op jit(solution)/shard_map/psum | solution.py:40
  133.8 0.8 copy.15
  (33 shorter events, 3.1 us)
Async XLA Ops:
  0.0 15.9 %copy-start = (s32[4,4]{1,0:T(4,128)S(1)}, s32[4,4]{1,0:T(4,128)}, u32[]{:S(2)}) copy-start(s32[4,4]{1,0:T(4,128)} %param.7) | copy-start | bytes 196
  0.9 8.8 %copy-start.2 = (bf16[2,1,4,8,1024]{4,3,2,1,0:T(8,128)(2,1)S(1)}, bf16[2,1,4,8,1024]{4,3,2,1,0:T(8,128)(2,1)}, u32[]{:S(2)}) copy-start(bf16[2,1,4,8,1024]{4,3,2,1,0:T(8,128)(2,1)} %param.5) | copy-start | bytes 393220
  10.4 11.2 %copy-start.1 = (bf16[2,1,4,8,1024]{4,3,2,1,0:T(8,128)(2,1)S(1)}, bf16[2,1,4,8,1024]{4,3,2,1,0:T(8,128)(2,1)}, u32[]{:S(2)}) copy-start(bf16[2,1,4,8,1024]{4,3,2,1,0:T(8,128)(2,1)} %param.6) | copy-start | bytes 393220
  11.0 10.5 %all-to-all-start = ((bf16[2,4,8,128]{3,2,0,1:T(8,128)(2,1)}), bf16[2,4,8,128]{3,2,0,1:T(8,128)(2,1)S(1)}, u32[]{:S(2)}, u32[]{:S(2)}) async-start(bf16[2,4,8,128]{3,2,0,1:T(8,128)(2,1)} %pad_maximum_fusion.3), calls=%async_computation | async-start | bytes 32768 | tf_op jit(solution)/shard_map/all_to_all | solution.py:35
where the time goes:
time: 135 us
  blocking collectives  116 us (86%)
  waiting for transfers between devices  5.51 us (4%)
  matrix products  5.2 us (4%)
  starting transfers between devices  4.87 us (4%)
  local copies, waits for them, and re-layouts  1.82 us (1%)
    psum x3, blocking collectives, apply_once(): summed = lax.psum(partial_sum, 'rows')  76.6 us
    all_gather x3, blocking collectives, apply_once(): gathered = lax.all_gather(current, 'rows', axis=0, tiled=True)  23.2 us
    all_to_all x2, blocking collectives, apply_once(): lax.all_to_all(skeleton, 'clus', split_axis=1, concat_axis=1, tiled=True)  15.9 us
    all_to_all x1, waiting for transfers between devices, apply_once(): lax.all_to_all(skeleton, 'clus', split_axis=1, concat_axis=1, tiled=True)  5.51 us
    all_to_all x1, starting transfers between devices, apply_once(): lax.all_to_all(skeleton, 'clus', split_axis=1, concat_axis=1, tiled=True)  4.87 us
  transfers between devices with their start and end apart: 1, of which 1 were waited for; matrix products, arithmetic and copies ran while one was open for 0% of the time, Pallas kernels for 0%

commit v1 on v0

v1 whole, which is shorter than its diff:
```python
import functools

import jax
import jax.numpy as jnp
from jax import lax
from jax.experimental import pallas as pl
from jax.experimental.pallas import tpu as pltpu
from jax.sharding import PartitionSpec as P

STEPS = 3
F32 = jnp.float32
BF16 = jnp.bfloat16
SMALL_GATHER = 4 << 20


def complex_dot(a_real, a_imag, b_real, b_imag):
    real_part = jnp.dot(a_real, b_real, preferred_element_type=F32) - jnp.dot(
        a_imag, b_imag, preferred_element_type=F32
    )
    imag_part = jnp.dot(a_real, b_imag, preferred_element_type=F32) + jnp.dot(
        a_imag, b_real, preferred_element_type=F32
    )
    return (real_part, imag_part)


def transposed_dot(columns, skel_flat):
    real_part = jnp.einsum(
        "km,kr->mr", columns[0], skel_flat[0], preferred_element_type=F32
    ) - jnp.einsum("km,kr->mr", columns[1], skel_flat[1], preferred_element_type=F32)
    imag_part = jnp.einsum(
        "km,kr->mr", columns[0], skel_flat[1], preferred_element_type=F32
    ) + jnp.einsum("km,kr->mr", columns[1], skel_flat[0], preferred_element_type=F32)
    return jnp.stack([real_part, imag_part], axis=1)


def apply_once(current, factor, weights, keep_mask, clusters, quarter, leaf_size, angles, part_row):
    gathered = lax.all_gather(current, "rows", axis=0, tiled=True)
    real_part, imag_part = complex_dot(factor[0], factor[1], gathered[:, 0], gathered[:, 1])
    skeleton = jnp.stack([real_part, imag_part]).astype(BF16).reshape(2, clusters, quarter, angles)
    received = lax.all_to_all(skeleton, "clus", split_axis=1, concat_axis=1, tiled=True)
    received = received * keep_mask[None, :, :, None]
    skel_flat = received.reshape(2, clusters * quarter, angles)
    share_rows = leaf_size // lax.axis_size("rows")
    partial_sum = transposed_dot(weights, skel_flat)
    summed = lax.psum(partial_sum, "rows")
    own_rows = lax.dynamic_slice_in_dim(summed, part_row * share_rows, share_rows, 0)
    return own_rows.astype(BF16)


def step_body(excitation, leaf_factor, coupling, ranks):
    cluster = lax.axis_index("clus")
    part_row = lax.axis_index("rows")
    clusters = leaf_factor.shape[2]
    quarter = leaf_factor.shape[3]
    leaf_size = leaf_factor.shape[4]
    angles = excitation.shape[2]
    factor = leaf_factor.reshape(2, clusters * quarter, leaf_size)
    weights = coupling.reshape(2, clusters * quarter, leaf_size)
    rank_row = lax.dynamic_slice_in_dim(ranks, cluster, 1, 0)[0]
    rank_level = part_row * quarter + jnp.arange(quarter, dtype=jnp.int32)
    keep_mask = (rank_level[None, :] < rank_row[:, None]).astype(BF16)
    current = excitation
    for step in range(STEPS):
        current = apply_once(
            current, factor, weights, keep_mask, clusters, quarter, leaf_size, angles, part_row
        )
    return current


def aligned(index, step):
    return pl.multiple_of(index, step)


def rows_of(block):
    flat = block.astype(F32).reshape(block.shape[0] * block.shape[1], block.shape[2])
    return flat.astype(BF16)


def combine(product, rows, columns):
    real_part = product[:rows, :columns] - product[rows:, columns:]
    imag_part = product[:rows, columns:] + product[rows:, :columns]
    return real_part, imag_part


def local_kernel(
    clusters, quarter, leaf, share, angles,
    ranks, l_own, l_x, k_own, k_x, k_core, k_diag, x_own, x_x, x_core, x_diag,
    packed, k_mine, l_all, k_all, x_all, x_wide,
):
    row = lax.axis_index("rows")
    cluster = lax.axis_index("clus")
    side, core = row // 2, row % 2
    block = clusters * quarter
    full = 4 * block
    for ref, at in ((l_own, side), (l_x, 1 - side)):
        for part in range(2):
            l_all[pl.ds(aligned(part * 2 * block + at * block, block), block), :] = rows_of(ref[part])
    for ref, at in ((k_own, row), (k_x, row ^ 2), (k_core, row ^ 1), (k_diag, row ^ 3)):
        for part in range(2):
            k_all[pl.ds(aligned(part * full + at * block, block), block), :] = rows_of(ref[part])
    for ref, at in ((x_own, row), (x_x, row ^ 2), (x_core, row ^ 1), (x_diag, row ^ 3)):
        x_wide[...] = ref[...].astype(F32)
        own_rows = pl.ds(aligned(at * share, share), share)
        for part in range(2):
            x_all[own_rows, part * angles : (part + 1) * angles] = x_wide[
                pl.ds(part, share, stride=2), :
            ].astype(BF16)
    skeleton = jnp.dot(l_all[...], x_all[...], preferred_element_type=F32)
    between = lax.dot_general(
        l_all[...], k_all[...], (((1,), (1,)), ((), ())), preferred_element_type=F32
    )
    parts = combine(skeleton, 2 * block, angles) + combine(between, 2 * block, full)
    level = lax.broadcasted_iota(jnp.int32, (quarter, 128), 0)
    for at in range(2):
        base = (2 * at + core) * quarter
        kept = [level + base < ranks[target, cluster] for target in range(clusters)]
        for i, value in enumerate(parts):
            rows = [
                jnp.where(
                    kept[target],
                    value[at * block + target * quarter : at * block + (target + 1) * quarter],
                    0.0,
                )
                for target in range(clusters)
            ]
            packed[at, i] = jnp.concatenate(rows, axis=0).astype(BF16)
    for part in range(2):
        k_mine[part] = k_all[part * full : (part + 1) * full, pl.ds(aligned(row * share, share), share)]


def chain_kernel(clusters, quarter, share, angles, *refs):
    held, swapped = refs[:clusters], refs[clusters : 2 * clusters]
    k_mine, field, between, skeleton, kept, wide = refs[2 * clusters :]
    row = lax.axis_index("rows")
    cluster = lax.axis_index("clus")
    core = row % 2
    block = clusters * quarter
    full = 4 * block
    for j in range(clusters):
        source = cluster ^ j
        for ref, at_core in ((held[j], core), (swapped[j], 1 - core)):
            for at in range(2):
                first = (2 * at + at_core) * block
                for part in range(2):
                    skeleton[source, part, pl.ds(aligned(first, block), block), :] = ref[
                        at, part
                    ].astype(F32)
                    between[source, pl.ds(aligned(part * full + first, block), block), :] = ref[
                        at, 2 + part
                    ]

    def regroup(target):
        columns = []
        for part in range(2):
            rows = [
                skeleton[s, part, pl.ds(aligned(q * block + target * quarter, quarter), quarter), :]
                for q in range(4)
                for s in range(clusters)
            ]
            columns.append(jnp.concatenate(rows, axis=0))
        return jnp.concatenate(columns, axis=1).astype(BF16)

    for step in range(STEPS - 1):
        for target in range(clusters):
            kept[target] = regroup(target)
        for source in range(clusters):
            product = jnp.dot(between[source], kept[source], preferred_element_type=F32)
            skeleton[source, 0], skeleton[source, 1] = combine(product, full, angles)
    last = regroup(cluster)
    contract = (((0,), (0,)), ((), ()))
    with_real = lax.dot_general(k_mine[0], last, contract, preferred_element_type=F32)
    with_imag = lax.dot_general(k_mine[1], last, contract, preferred_element_type=F32)
    wide[pl.ds(0, share, stride=2), :] = with_real[:, :angles] - with_imag[:, angles:]
    wide[pl.ds(1, share, stride=2), :] = with_real[:, angles:] + with_imag[:, :angles]
    field[...] = wide[...].astype(BF16)


def in_vmem(count):
    return [pl.BlockSpec(memory_space=pltpu.VMEM)] * count


def gather_body(excitation, leaf_factor, coupling, ranks):
    clusters, quarter, leaf = leaf_factor.shape[2:]
    share, _, angles = excitation.shape
    block = clusters * quarter
    full = 4 * block

    def across(flip):
        return lambda v: lax.ppermute(v, "rows", [(i, i ^ flip) for i in range(4)])

    to_x, to_core = across(2), across(1)
    own_x = excitation.reshape(2 * share, angles)
    own_l = leaf_factor.reshape(2, clusters, quarter, leaf)
    own_k = coupling.reshape(2, clusters, quarter, leaf)
    l_x, k_x, x_x = to_x(own_l), to_x(own_k), to_x(own_x)
    k_core, x_core = to_core(own_k), to_core(own_x)
    k_diag, x_diag = to_core(k_x), to_core(x_x)
    packed, k_mine = pl.pallas_call(
        functools.partial(local_kernel, clusters, quarter, leaf, share, angles),
        out_shape=(
            jax.ShapeDtypeStruct((2, 4, block, angles), BF16),
            jax.ShapeDtypeStruct((2, full, share), BF16),
        ),
        in_specs=[pl.BlockSpec(memory_space=pltpu.SMEM)] + in_vmem(10),
        out_specs=tuple(in_vmem(2)),
        scratch_shapes=[
            pltpu.VMEM((4 * block, leaf), BF16),
            pltpu.VMEM((2 * full, leaf), BF16),
            pltpu.VMEM((leaf, 2 * angles), BF16),
            pltpu.VMEM((2 * share, angles), F32),
        ],
        compiler_params=pltpu.CompilerParams(vmem_limit_bytes=32 << 20),
        name="local_skeleton",
    )(ranks, own_l, l_x, own_k, k_x, k_core, k_diag, own_x, x_x, x_core, x_diag)
    held = [packed] + [
        lax.ppermute(packed, "clus", [(i, i ^ j) for i in range(clusters)])
        for j in range(1, clusters)
    ]
    swapped = [to_core(v) for v in held]
    field = pl.pallas_call(
        functools.partial(chain_kernel, clusters, quarter, share, angles),
        out_shape=jax.ShapeDtypeStruct((2 * share, angles), BF16),
        in_specs=in_vmem(2 * clusters + 1),
        out_specs=in_vmem(1)[0],
        scratch_shapes=[
            pltpu.VMEM((clusters, 2 * full, full), BF16),
            pltpu.VMEM((clusters, 2, full, angles), F32),
            pltpu.VMEM((clusters, full, 2 * angles), BF16),
            pltpu.VMEM((2 * share, angles), F32),
        ],
        compiler_params=pltpu.CompilerParams(vmem_limit_bytes=32 << 20),
        name="skeleton_chain",
    )(*held, *swapped, k_mine)
    return field.reshape(share, 2, angles)


def body(excitation, leaf_factor, coupling, ranks):
    clusters, quarter, leaf = leaf_factor.shape[2:]
    share, _, angles = excitation.shape
    rows = lax.axis_size("rows")
    full = rows * clusters * quarter
    gathered = 4 * clusters * full * (angles + full)
    fits = (
        rows == 4
        and clusters == lax.axis_size("clus")
        and clusters & (clusters - 1) == 0
        and quarter == 8
        and angles == full == 128
        and share * rows == leaf
        and gathered <= SMALL_GATHER
    )
    plan = gather_body if fits else step_body
    return plan(excitation, leaf_factor, coupling, ranks)


def solution(mesh):
    placed = (
        P(("freq", "clus", "rows"), None, None),
        P("freq", "clus", None, "rows", None),
        P("freq", "clus", None, "rows", None),
        P("freq", None),
    )
    return jax.shard_map(
        body,
        mesh=mesh,
        in_specs=placed,
        out_specs=P(("freq", "clus", "rows"), None, None),
        check_vma=False,
    )
```

time: 135 us -> 28.8 us (0.21)
  blocking collectives: 116 us -> 0 us
  waiting for transfers between devices: 5.51 us -> 12.6 us
  starting transfers between devices: 4.87 us -> 10.5 us
  matrix products: 5.2 us -> 0 us
  Pallas kernels: 0 us -> 2.66 us
    psum x3 -> x0, blocking collectives: 76.6 us -> none  [apply_once(): summed = lax.psum(partial_sum, 'rows')]
    all_gather x3 -> x0, blocking collectives: 23.2 us -> none  [apply_once(): gathered = lax.all_gather(current, 'rows', axis=0, tiled=True)]
    all_to_all x2 -> x0, blocking collectives: 15.9 us -> none  [apply_once(): lax.all_to_all(skeleton, 'clus', split_axis=1, concat_axis=1, tiled=True)]
    ppermute x0 -> x14, waiting for transfers between devices: none -> 12.6 us  [the longest x11 7.68 us: across(): return lambda v: lax.ppermute(v, 'rows', [(i, i ^ flip) for i in range(4)])]
    ppermute x0 -> x14, starting transfers between devices: none -> 10.5 us  [the longest x11 6 us: across(): return lambda v: lax.ppermute(v, 'rows', [(i, i ^ flip) for i in range(4)])]
    all_to_all x1 -> x0, waiting for transfers between devices: 5.51 us -> none  [apply_once(): lax.all_to_all(skeleton, 'clus', split_axis=1, concat_axis=1, tiled=True)]
    dot_general x24 -> x0, matrix products: 5.2 us -> none  [the longest x3 0.76 us: transposed_dot(): jnp.einsum('km,kr->mr', columns[1], skel_flat[0], preferred_element_type=...]
    all_to_all x1 -> x0, starting transfers between devices: 4.87 us -> none  [apply_once(): lax.all_to_all(skeleton, 'clus', split_axis=1, concat_axis=1, tiled=True)]
  transfers between devices with their start and end apart: 1 -> 14, of which waited for: 1 -> 7; matrix products, arithmetic and copies ran while one was open for 0% -> 0% of each run, Pallas kernels for 0% -> 0%
where the time goes in v1:
time: 28.8 us; the launch traced here: 28.6 us
  waiting for transfers between devices  12.6 us (44%)
  starting transfers between devices  10.5 us (36%)
  local copies, waits for them, and re-layouts  2.71 us (9%)
  Pallas kernels  2.66 us (9%)
    ppermute x11, waiting for transfers between devices, across(): return lambda v: lax.ppermute(v, 'rows', [(i, i ^ flip) for i in range(4)])  7.68 us
    ppermute x11, starting transfers between devices, across(): return lambda v: lax.ppermute(v, 'rows', [(i, i ^ flip) for i in range(4)])  6 us
    ppermute x3, waiting for transfers between devices, gather_body(): lax.ppermute(packed, 'clus', [(i, i ^ j) for i in range(clusters)])  4.94 us
    ppermute x3, starting transfers between devices, gather_body(): lax.ppermute(packed, 'clus', [(i, i ^ j) for i in range(clusters)])  4.55 us
    unnamed x8, local copies, waits for them, and re-layouts  2.71 us
    pallas_call x1, Pallas kernels, gather_body(): pl.pallas_call(functools.partial(chain_kernel, clusters, quarter, share,...  1.5 us
    pallas_call x1, Pallas kernels, gather_body(): pl.pallas_call(functools.partial(local_kernel, clusters, quarter, leaf, s...  1.16 us
  transfers between devices with their start and end apart: 14, of which 7 were waited for; matrix products, arithmetic and copies ran while one was open for 0% of the time, Pallas kernels for 0%

profile of v1, /device:TPU:0, one launch (start us, length us, event | category | flops | bytes accessed | tf_op | source)
XLA Modules:
  0.0 28.6 jit_solution(3309560558884206186)
XLA Ops:
  0.0 2.9 %collective-permute-start.4 = (bf16[512,128]{1,0:T(8,128)(2,1)}, bf16[512,128]{1,0:T(8,128)(2,1)S(1)}, u32[]{:S(2)}, u32[]{:S(2)}) collective-permute-start(bf16[512,128]{1,0:T(8,128)(2,1)} %bitcast.9), channel_id=1, source_target_pairs={{0,2},{1,3},{2,0},{3,1},{4,6},{5,7},{6,4},{7,5},{8,10},{9,11},{10,... | collective-permute-start | bytes 393224 | tf_op jit(solution)/shard_map/ppermute | solution.py:189
  2.9 0.1 collective-permute-start.1
  3.0 0.0 collective-permute-start.5
  3.0 0.5 %collective-permute-start.2 = (bf16[2,4,8,1024]{3,2,1,0:T(8,128)(2,1)}, bf16[2,4,8,1024]{3,2,1,0:T(8,128)(2,1)S(1)}, u32[]{:S(2)}, u32[]{:S(2)}) collective-permute-start(bf16[2,4,8,1024]{3,2,1,0:T(8,128)(2,1)} %bitcast.7), channel_id=1, source_target_pairs={{0,1},{1,0},{2,3},{3,2},{4,5},{5,4},{6,7},{7,6},{8,9},{9,8},{10,11... | collective-permute-start | bytes 393224 | tf_op jit(solution)/shard_map/ppermute | solution.py:189
  3.5 2.0 %collective-permute-start = (bf16[2,4,8,1024]{3,2,1,0:T(8,128)(2,1)}, bf16[2,4,8,1024]{3,2,1,0:T(8,128)(2,1)S(1)}, u32[]{:S(2)}, u32[]{:S(2)}) collective-permute-start(bf16[2,4,8,1024]{3,2,1,0:T(8,128)(2,1)} %bitcast.4), channel_id=1, source_target_pairs={{0,2},{1,3},{2,0},{3,1},{4,6},{5,7},{6,4},{7,5},{8,10},{9,11},{10,... | collective-permute-start | bytes 393224 | tf_op jit(solution)/shard_map/ppermute | solution.py:189
  5.5 2.0 %collective-permute-done.4.x_x = bf16[512,128]{1,0:T(8,128)(2,1)S(1)} collective-permute-done((bf16[512,128]{1,0:T(8,128)(2,1)}, bf16[512,128]{1,0:T(8,128)(2,1)S(1)}, u32[]{:S(2)}, u32[]{:S(2)}) %collective-permute-start.4) | collective-permute-done | bytes 131104 | tf_op jit(solution)/shard_map/ppermute | solution.py:189
  7.5 2.8 %collective-permute-done.1.k_x = bf16[2,4,8,1024]{3,2,1,0:T(8,128)(2,1)S(1)} collective-permute-done((bf16[2,4,8,1024]{3,2,1,0:T(8,128)(2,1)}, bf16[2,4,8,1024]{3,2,1,0:T(8,128)(2,1)S(1)}, u32[]{:S(2)}, u32[]{:S(2)}) %collective-permute-start.1) | collective-permute-done | bytes 131104 | tf_op jit(solution)/shard_map/ppermute | solution.py:189
  10.3 0.0 collective-permute-start.3
  10.3 2.0 %collective-permute-done.l_x = bf16[2,4,8,1024]{3,2,1,0:T(8,128)(2,1)S(1)} collective-permute-done((bf16[2,4,8,1024]{3,2,1,0:T(8,128)(2,1)}, bf16[2,4,8,1024]{3,2,1,0:T(8,128)(2,1)S(1)}, u32[]{:S(2)}, u32[]{:S(2)}) %collective-permute-start) | collective-permute-done | bytes 131104 | tf_op jit(solution)/shard_map/ppermute | solution.py:189
  12.3 0.0 collective-permute-done.2.k_core
  12.3 0.0 collective-permute-done.6.x_diag
  12.3 0.0 collective-permute-done.3.k_diag
  12.3 0.9 %copy-done = bf16[2,1,4,8,1024]{4,3,2,1,0:T(8,128)(2,1)S(1)} copy-done((bf16[2,1,4,8,1024]{4,3,2,1,0:T(8,128)(2,1)S(1)}, bf16[2,1,4,8,1024]{4,3,2,1,0:T(8,128)(2,1)}, u32[]{:S(2)}) %copy-start) | copy-done | bytes 131096
  13.2 0.9 %copy-done.1 = bf16[2,1,4,8,1024]{4,3,2,1,0:T(8,128)(2,1)S(1)} copy-done((bf16[2,1,4,8,1024]{4,3,2,1,0:T(8,128)(2,1)S(1)}, bf16[2,1,4,8,1024]{4,3,2,1,0:T(8,128)(2,1)}, u32[]{:S(2)}) %copy-start.1) | copy-done | bytes 131096
  14.1 0.9 %copy-done.2 = bf16[256,2,128]{2,1,0:T(2,128)(2,1)S(1)} copy-done((bf16[256,2,128]{2,1,0:T(2,128)(2,1)S(1)}, bf16[256,2,128]{2,1,0:T(2,128)(2,1)}, u32[]{:S(2)}) %copy-start.2) | copy-done | bytes 131096
  15.0 1.2 %local_skeleton.1 = (bf16[2,4,32,128]{3,2,1,0:T(8,128)(2,1)S(1)}, bf16[2,128,256]{2,1,0:T(8,128)(2,1)S(1)}) custom-call(s32[4,4]{1,0:T(4,128)S(1)} %copy-done.3, bf16[2,4,8,1024]{3,2,1,0:T(8,128)(2,1)S(1)} %bitcast.5, bf16[2,4,8,1024]{3,2,1,0:T(8,128)(2,1)S(1)} %collective-permute-done.l_x, bf16[2,4,8,1024]{3,2,1,0:T(8,128)(2,1)S(1)} %bitcast.8, ...), custom_call_target="tpu_custom_call" | custom-call | tf_op jit(solution)/shard_map/local_skeleton/pallas_call | solution.py:198
  16.2 3.9 %collective-permute-start.9 = (bf16[2,4,32,128]{3,2,1,0:T(8,128)(2,1)S(1)}, bf16[2,4,32,128]{3,2,1,0:T(8,128)(2,1)S(1)}, u32[]{:S(2)}, u32[]{:S(2)}) collective-permute-start(bf16[2,4,32,128]{3,2,1,0:T(8,128)(2,1)S(1)} %get-tuple-element.7.refs_0_), channel_id=1, source_target_pairs={{0,12},{4,8},{8,4},{12,0},{1,13},{5,9},{9,5},{13,1},{2,14},{6,10},... | collective-permute-start | bytes 196616 | tf_op jit(solution)/shard_map/ppermute | solution.py:216
  20.1 0.6 %collective-permute-start.7 = (bf16[2,4,32,128]{3,2,1,0:T(8,128)(2,1)S(1)}, bf16[2,4,32,128]{3,2,1,0:T(8,128)(2,1)S(1)}, u32[]{:S(2)}, u32[]{:S(2)}) collective-permute-start(bf16[2,4,32,128]{3,2,1,0:T(8,128)(2,1)S(1)} %get-tuple-element.7.refs_0_), channel_id=1, source_target_pairs={{0,4},{4,0},{8,12},{12,8},{1,5},{5,1},{9,13},{13,9},{2,6},{6,2},{1... | collective-permute-start | bytes 196616 | tf_op jit(solution)/shard_map/ppermute | solution.py:216
  20.7 2.0 %collective-permute-done.9.refs_3_ = bf16[2,4,32,128]{3,2,1,0:T(8,128)(2,1)S(1)} collective-permute-done((bf16[2,4,32,128]{3,2,1,0:T(8,128)(2,1)S(1)}, bf16[2,4,32,128]{3,2,1,0:T(8,128)(2,1)S(1)}, u32[]{:S(2)}, u32[]{:S(2)}) %collective-permute-start.9) | collective-permute-done | bytes 65568 | tf_op jit(solution)/shard_map/ppermute | solution.py:216
  22.7 3.0 %collective-permute-done.8.refs_2_ = bf16[2,4,32,128]{3,2,1,0:T(8,128)(2,1)S(1)} collective-permute-done((bf16[2,4,32,128]{3,2,1,0:T(8,128)(2,1)S(1)}, bf16[2,4,32,128]{3,2,1,0:T(8,128)(2,1)S(1)}, u32[]{:S(2)}, u32[]{:S(2)}) %collective-permute-start.8) | collective-permute-done | bytes 65568 | tf_op jit(solution)/shard_map/ppermute | solution.py:216
  25.7 0.5 %collective-permute-start.11 = (bf16[2,4,32,128]{3,2,1,0:T(8,128)(2,1)S(1)}, bf16[2,4,32,128]{3,2,1,0:T(8,128)(2,1)S(1)}, u32[]{:S(2)}, u32[]{:S(2)}) collective-permute-start(bf16[2,4,32,128]{3,2,1,0:T(8,128)(2,1)S(1)} %collective-permute-done.7.refs_1_), channel_id=1, source_target_pairs={{0,1},{1,0},{2,3},{3,2},{4,5},{5,4},{6,7},{7,6},{8,9},{9,8},{10,11... | collective-permute-start | bytes 196616 | tf_op jit(solution)/shard_map/ppermute | solution.py:189
  26.2 0.7 %collective-permute-done.12.refs_6_ = bf16[2,4,32,128]{3,2,1,0:T(8,128)(2,1)S(1)} collective-permute-done((bf16[2,4,32,128]{3,2,1,0:T(8,128)(2,1)S(1)}, bf16[2,4,32,128]{3,2,1,0:T(8,128)(2,1)S(1)}, u32[]{:S(2)}, u32[]{:S(2)}) %collective-permute-start.12) | collective-permute-done | bytes 65568 | tf_op jit(solution)/shard_map/ppermute | solution.py:189
  26.9 0.2 collective-permute-done.11.refs_5_
  27.1 1.5 %skeleton_chain.1 = bf16[512,128]{1,0:T(8,128)(2,1)} custom-call(bf16[2,4,32,128]{3,2,1,0:T(8,128)(2,1)S(1)} %get-tuple-element.7.refs_0_, bf16[2,4,32,128]{3,2,1,0:T(8,128)(2,1)S(1)} %collective-permute-done.7.refs_1_, bf16[2,4,32,128]{3,2,1,0:T(8,128)(2,1)S(1)} %collective-permute-done.8.refs_2_, ...), custom_call_target="tpu_custom_call" | custom-call | tf_op jit(solution)/shard_map/skeleton_chain/pallas_call | solution.py:220
  (14 shorter events, 0.0 us)
Async XLA Ops:
  0.0 12.3 %copy-start.3 = (s32[4,4]{1,0:T(4,128)S(1)}, s32[4,4]{1,0:T(4,128)}, u32[]{:S(2)}) copy-start(s32[4,4]{1,0:T(4,128)} %ranks.1) | copy-start | bytes 196
  0.0 7.5 %collective-permute-start.4 = (bf16[512,128]{1,0:T(8,128)(2,1)}, bf16[512,128]{1,0:T(8,128)(2,1)S(1)}, u32[]{:S(2)}, u32[]{:S(2)}) collective-permute-start(bf16[512,128]{1,0:T(8,128)(2,1)} %bitcast.9), channel_id=1, source_target_pairs={{0,2},{1,3},{2,0},{3,1},{4,6},{5,7},{6,4},{7,5},{8,10},{9,11},{10,... | collective-permute-start | bytes 393224 | tf_op jit(solution)/shard_map/ppermute | solution.py:189
  2.9 7.3 %collective-permute-start.1 = (bf16[2,4,8,1024]{3,2,1,0:T(8,128)(2,1)}, bf16[2,4,8,1024]{3,2,1,0:T(8,128)(2,1)S(1)}, u32[]{:S(2)}, u32[]{:S(2)}) collective-permute-start(bf16[2,4,8,1024]{3,2,1,0:T(8,128)(2,1)} %bitcast.6), channel_id=1, source_target_pairs={{0,2},{1,3},{2,0},{3,1},{4,6},{5,7},{6,4},{7,5},{8,10},{9,11},{10,... | collective-permute-start | bytes 393224 | tf_op jit(solution)/shard_map/ppermute | solution.py:189
  3.0 7.3 %collective-permute-start.5 = (bf16[512,128]{1,0:T(8,128)(2,1)}, bf16[512,128]{1,0:T(8,128)(2,1)S(1)}, u32[]{:S(2)}, u32[]{:S(2)}) collective-permute-start(bf16[512,128]{1,0:T(8,128)(2,1)} %bitcast.10), channel_id=1, source_target_pairs={{0,1},{1,0},{2,3},{3,2},{4,5},{5,4},{6,7},{7,6},{8,9},{9,8},{10,11... | collective-permute-start | bytes 393224 | tf_op jit(solution)/shard_map/ppermute | solution.py:189
  3.0 9.3 %collective-permute-start.2 = (bf16[2,4,8,1024]{3,2,1,0:T(8,128)(2,1)}, bf16[2,4,8,1024]{3,2,1,0:T(8,128)(2,1)S(1)}, u32[]{:S(2)}, u32[]{:S(2)}) collective-permute-start(bf16[2,4,8,1024]{3,2,1,0:T(8,128)(2,1)} %bitcast.7), channel_id=1, source_target_pairs={{0,1},{1,0},{2,3},{3,2},{4,5},{5,4},{6,7},{7,6},{8,9},{9,8},{10,11... | collective-permute-start | bytes 393224 | tf_op jit(solution)/shard_map/ppermute | solution.py:189
  3.5 8.7 %collective-permute-start = (bf16[2,4,8,1024]{3,2,1,0:T(8,128)(2,1)}, bf16[2,4,8,1024]{3,2,1,0:T(8,128)(2,1)S(1)}, u32[]{:S(2)}, u32[]{:S(2)}) collective-permute-start(bf16[2,4,8,1024]{3,2,1,0:T(8,128)(2,1)} %bitcast.4), channel_id=1, source_target_pairs={{0,2},{1,3},{2,0},{3,1},{4,6},{5,7},{6,4},{7,5},{8,10},{9,11},{10,... | collective-permute-start | bytes 393224 | tf_op jit(solution)/shard_map/ppermute | solution.py:189
  7.5 4.8 %collective-permute-start.6 = (bf16[512,128]{1,0:T(8,128)(2,1)S(1)}, bf16[512,128]{1,0:T(8,128)(2,1)S(1)}, u32[]{:S(2)}, u32[]{:S(2)}) collective-permute-start(bf16[512,128]{1,0:T(8,128)(2,1)S(1)} %collective-permute-done.4.x_x), channel_id=1, source_target_pairs={{0,1},{1,0},{2,3},{3,2},{4,5},{5,4},{6,7},{7,6},{8,9},{9,8},{10,11... | collective-permute-start | bytes 393224 | tf_op jit(solution)/shard_map/ppermute | solution.py:189
  10.3 2.0 %collective-permute-start.3 = (bf16[2,4,8,1024]{3,2,1,0:T(8,128)(2,1)S(1)}, bf16[2,4,8,1024]{3,2,1,0:T(8,128)(2,1)S(1)}, u32[]{:S(2)}, u32[]{:S(2)}) collective-permute-start(bf16[2,4,8,1024]{3,2,1,0:T(8,128)(2,1)S(1)} %collective-permute-done.1.k_x), channel_id=1, source_target_pairs={{0,1},{1,0},{2,3},{3,2},{4,5},{5,4},{6,7},{7,6},{8,9},{9,8},{10,11... | collective-permute-start | bytes 393224 | tf_op jit(solution)/shard_map/ppermute | solution.py:189
  12.3 0.9 %copy-start = (bf16[2,1,4,8,1024]{4,3,2,1,0:T(8,128)(2,1)S(1)}, bf16[2,1,4,8,1024]{4,3,2,1,0:T(8,128)(2,1)}, u32[]{:S(2)}) copy-start(bf16[2,1,4,8,1024]{4,3,2,1,0:T(8,128)(2,1)} %param.5) | copy-start | bytes 393220
  13.2 0.9 %copy-start.1 = (bf16[2,1,4,8,1024]{4,3,2,1,0:T(8,128)(2,1)S(1)}, bf16[2,1,4,8,1024]{4,3,2,1,0:T(8,128)(2,1)}, u32[]{:S(2)}) copy-start(bf16[2,1,4,8,1024]{4,3,2,1,0:T(8,128)(2,1)} %param.6) | copy-start | bytes 393220
  14.1 0.9 %copy-start.2 = (bf16[256,2,128]{2,1,0:T(2,128)(2,1)S(1)}, bf16[256,2,128]{2,1,0:T(2,128)(2,1)}, u32[]{:S(2)}) copy-start(bf16[256,2,128]{2,1,0:T(2,128)(2,1)} %param.4) | copy-start | bytes 393220
  16.2 6.5 %collective-permute-start.9 = (bf16[2,4,32,128]{3,2,1,0:T(8,128)(2,1)S(1)}, bf16[2,4,32,128]{3,2,1,0:T(8,128)(2,1)S(1)}, u32[]{:S(2)}, u32[]{:S(2)}) collective-permute-start(bf16[2,4,32,128]{3,2,1,0:T(8,128)(2,1)S(1)} %get-tuple-element.7.refs_0_), channel_id=1, source_target_pairs={{0,12},{4,8},{8,4},{12,0},{1,13},{5,9},{9,5},{13,1},{2,14},{6,10},... | collective-permute-start | bytes 196616 | tf_op jit(solution)/shard_map/ppermute | solution.py:216
  20.1 5.6 %collective-permute-start.8 = (bf16[2,4,32,128]{3,2,1,0:T(8,128)(2,1)S(1)}, bf16[2,4,32,128]{3,2,1,0:T(8,128)(2,1)S(1)}, u32[]{:S(2)}, u32[]{:S(2)}) collective-permute-start(bf16[2,4,32,128]{3,2,1,0:T(8,128)(2,1)S(1)} %get-tuple-element.7.refs_0_), channel_id=1, source_target_pairs={{0,8},{4,12},{8,0},{12,4},{1,9},{5,13},{9,1},{13,5},{2,10},{6,14},... | collective-permute-start | bytes 196616 | tf_op jit(solution)/shard_map/ppermute | solution.py:216
  20.1 5.6 %collective-permute-start.7 = (bf16[2,4,32,128]{3,2,1,0:T(8,128)(2,1)S(1)}, bf16[2,4,32,128]{3,2,1,0:T(8,128)(2,1)S(1)}, u32[]{:S(2)}, u32[]{:S(2)}) collective-permute-start(bf16[2,4,32,128]{3,2,1,0:T(8,128)(2,1)S(1)} %get-tuple-element.7.refs_0_), channel_id=1, source_target_pairs={{0,4},{4,0},{8,12},{12,8},{1,5},{5,1},{9,13},{13,9},{2,6},{6,2},{1... | collective-permute-start | bytes 196616 | tf_op jit(solution)/shard_map/ppermute | solution.py:216
  20.7 5.5 %collective-permute-start.10 = (bf16[2,4,32,128]{3,2,1,0:T(8,128)(2,1)S(1)}, bf16[2,4,32,128]{3,2,1,0:T(8,128)(2,1)S(1)}, u32[]{:S(2)}, u32[]{:S(2)}) collective-permute-start(bf16[2,4,32,128]{3,2,1,0:T(8,128)(2,1)S(1)} %get-tuple-element.7.refs_0_), channel_id=1, source_target_pairs={{0,1},{1,0},{2,3},{3,2},{4,5},{5,4},{6,7},{7,6},{8,9},{9,8},{10,11... | collective-permute-start | bytes 196616 | tf_op jit(solution)/shard_map/ppermute | solution.py:189
  22.7 3.5 %collective-permute-start.13 = (bf16[2,4,32,128]{3,2,1,0:T(8,128)(2,1)S(1)}, bf16[2,4,32,128]{3,2,1,0:T(8,128)(2,1)S(1)}, u32[]{:S(2)}, u32[]{:S(2)}) collective-permute-start(bf16[2,4,32,128]{3,2,1,0:T(8,128)(2,1)S(1)} %collective-permute-done.9.refs_3_), channel_id=1, source_target_pairs={{0,1},{1,0},{2,3},{3,2},{4,5},{5,4},{6,7},{7,6},{8,9},{9,8},{10,11... | collective-permute-start | bytes 196616 | tf_op jit(solution)/shard_map/ppermute | solution.py:189
  25.7 1.3 %collective-permute-start.12 = (bf16[2,4,32,128]{3,2,1,0:T(8,128)(2,1)S(1)}, bf16[2,4,32,128]{3,2,1,0:T(8,128)(2,1)S(1)}, u32[]{:S(2)}, u32[]{:S(2)}) collective-permute-start(bf16[2,4,32,128]{3,2,1,0:T(8,128)(2,1)S(1)} %collective-permute-done.8.refs_2_), channel_id=1, source_target_pairs={{0,1},{1,0},{2,3},{3,2},{4,5},{5,4},{6,7},{7,6},{8,9},{9,8},{10,11... | collective-permute-start | bytes 196616 | tf_op jit(solution)/shard_map/ppermute | solution.py:189
  25.7 1.4 %collective-permute-start.11 = (bf16[2,4,32,128]{3,2,1,0:T(8,128)(2,1)S(1)}, bf16[2,4,32,128]{3,2,1,0:T(8,128)(2,1)S(1)}, u32[]{:S(2)}, u32[]{:S(2)}) collective-permute-start(bf16[2,4,32,128]{3,2,1,0:T(8,128)(2,1)S(1)} %collective-permute-done.7.refs_1_), channel_id=1, source_target_pairs={{0,1},{1,0},{2,3},{3,2},{4,5},{5,4},{6,7},{7,6},{8,9},{9,8},{10,11... | collective-permute-start | bytes 196616 | tf_op jit(solution)/shard_map/ppermute | solution.py:189

commit v2 on v1

--- a/solution.py
+++ b/solution.py
@@ -67,93 +67,120 @@
     return current
 
 
-def aligned(index, step):
-    return pl.multiple_of(index, step)
-
-
-def rows_of(block):
-    flat = block.astype(F32).reshape(block.shape[0] * block.shape[1], block.shape[2])
-    return flat.astype(BF16)
-
-
 def combine(product, rows, columns):
     real_part = product[:rows, :columns] - product[rows:, columns:]
     imag_part = product[:rows, columns:] + product[rows:, :columns]
     return real_part, imag_part
 
 
-def local_kernel(
-    clusters, quarter, leaf, share, angles,
-    ranks, l_own, l_x, k_own, k_x, k_core, k_diag, x_own, x_x, x_core, x_diag,
-    packed, k_mine, l_all, k_all, x_all, x_wide,
+def load_kernel(
+    share, angles, quarter, ranks, l_hbm, k_hbm, x_hbm, x_near,
+    l_own, k_own, x_own, x_core, keep, x_flat, x_wide, sems,
 ):
+    copies = [
+        pltpu.make_async_copy(source, target, sems.at[i])
+        for i, (source, target) in enumerate(((x_hbm, x_flat), (l_hbm, l_own), (k_hbm, k_own)))
+    ]
+    for copy in copies:
+        copy.start()
     row = lax.axis_index("rows")
     cluster = lax.axis_index("clus")
-    side, core = row // 2, row % 2
+    level = lax.broadcasted_iota(jnp.int32, (quarter, angles), 0)
+    for at, flip in enumerate((0, 2, 1, 3)):
+        base = (row ^ flip) * quarter
+        for target in range(keep.shape[1] // quarter):
+            below = level + base < ranks[target, cluster]
+            keep[at, target * quarter : (target + 1) * quarter, :] = below.astype(F32)
+    copies[0].wait()
+    for source, target in ((x_flat, x_own), (x_near, x_core)):
+        x_wide[...] = source[...].astype(F32)
+        for part in range(2):
+            target[:, part * angles : (part + 1) * angles] = x_wide[
+                pl.ds(part, share, stride=2), :
+            ].astype(BF16)
+    copies[1].wait()
+    copies[2].wait()
+
+
+def side_kernel(share, angles, l_own, l_x, x_own, x_core, partial, kept_partial, l_all):
+    row = lax.axis_index("rows")
+    block = l_own.shape[1]
+    for part in range(2):
+        for at, ref in enumerate((l_own, l_x)):
+            first = (2 * part + at) * block
+            l_all[first : first + block, :] = ref[part]
+    total = None
+    for ref, quarter in ((x_own, row), (x_core, row ^ 1)):
+        columns = l_all[:, pl.ds(pl.multiple_of(quarter * share, share), share)]
+        term = jnp.dot(columns, ref[...], preferred_element_type=F32)
+        total = term if total is None else total + term
+    for part, value in enumerate(combine(total, 2 * block, angles)):
+        for at in range(2):
+            rows = value[at * block : (at + 1) * block]
+            kept_partial[at, part] = rows
+            partial[at, part] = rows.astype(BF16)
+
+
+def operator_columns(l_all, k_refs, k_rows):
+    block = k_refs[0].shape[1]
+    for part in range(2):
+        for at, ref in enumerate(k_refs):
+            first = (2 * part + at) * block
+            k_rows[first : first + block, :] = ref[part]
+    product = lax.dot_general(
+        l_all[...], k_rows[...], (((1,), (1,)), ((), ())), preferred_element_type=F32
+    )
+    return combine(product, 2 * block, 2 * block)
+
+
+def near_kernel(l_all, k_own, k_core, near, k_rows):
+    near[0], near[1] = operator_columns(l_all, (k_own, k_core), k_rows)
+
+
+def between_kernel(partial, partial_x, near, keep, l_all, k_x, k_diag, packed, k_rows):
+    block = keep.shape[1]
+    parts = []
+    for part, far in enumerate(operator_columns(l_all, (k_x, k_diag), k_rows)):
+        value = near[part]
+        columns = [value[:, :block], far[:, :block], value[:, block:], far[:, block:]]
+        parts.append(jnp.concatenate(columns, axis=1))
+    for at in range(2):
+        values = [partial[at, part] + partial_x[1 - at, part].astype(F32) for part in range(2)]
+        values += [value[at * block : (at + 1) * block] for value in parts]
+        for i, value in enumerate(values):
+            packed[at, i] = (value * keep[at]).astype(BF16)
+
+
+def chain_kernel(clusters, quarter, share, angles, *refs):
+    pieces, k_quarters = refs[: 2 * clusters], refs[2 * clusters : 2 * clusters + 4]
+    field, between, skeleton, kept, wide, k_mine = refs[2 * clusters + 4 :]
+    row = lax.axis_index("rows")
+    cluster = lax.axis_index("clus")
     block = clusters * quarter
     full = 4 * block
-    for ref, at in ((l_own, side), (l_x, 1 - side)):
+    for at in range(4):
         for part in range(2):
-            l_all[pl.ds(aligned(part * 2 * block + at * block, block), block), :] = rows_of(ref[part])
-    for ref, at in ((k_own, row), (k_x, row ^ 2), (k_core, row ^ 1), (k_diag, row ^ 3)):
-        for part in range(2):
-            k_all[pl.ds(aligned(part * full + at * block, block), block), :] = rows_of(ref[part])
-    for ref, at in ((x_own, row), (x_x, row ^ 2), (x_core, row ^ 1), (x_diag, row ^ 3)):
-        x_wide[...] = ref[...].astype(F32)
-        own_rows = pl.ds(aligned(at * share, share), share)
-        for part in range(2):
-            x_all[own_rows, part * angles : (part + 1) * angles] = x_wide[
-                pl.ds(part, share, stride=2), :
-            ].astype(BF16)
-    skeleton = jnp.dot(l_all[...], x_all[...], preferred_element_type=F32)
-    between = lax.dot_general(
-        l_all[...], k_all[...], (((1,), (1,)), ((), ())), preferred_element_type=F32
-    )
-    parts = combine(skeleton, 2 * block, angles) + combine(between, 2 * block, full)
-    level = lax.broadcasted_iota(jnp.int32, (quarter, 128), 0)
-    for at in range(2):
-        base = (2 * at + core) * quarter
-        kept = [level + base < ranks[target, cluster] for target in range(clusters)]
-        for i, value in enumerate(parts):
-            rows = [
-                jnp.where(
-                    kept[target],
-                    value[at * block + target * quarter : at * block + (target + 1) * quarter],
-                    0.0,
-                )
-                for target in range(clusters)
+            k_mine[part, at * block : (at + 1) * block, :] = k_quarters[at][
+                part, :, pl.ds(pl.multiple_of(row * share, share), share)
             ]
-            packed[at, i] = jnp.concatenate(rows, axis=0).astype(BF16)
-    for part in range(2):
-        k_mine[part] = k_all[part * full : (part + 1) * full, pl.ds(aligned(row * share, share), share)]
-
-
-def chain_kernel(clusters, quarter, share, angles, *refs):
-    held, swapped = refs[:clusters], refs[clusters : 2 * clusters]
-    k_mine, field, between, skeleton, kept, wide = refs[2 * clusters :]
-    row = lax.axis_index("rows")
-    cluster = lax.axis_index("clus")
-    core = row % 2
-    block = clusters * quarter
-    full = 4 * block
     for j in range(clusters):
         source = cluster ^ j
-        for ref, at_core in ((held[j], core), (swapped[j], 1 - core)):
+        for core in range(2):
+            ref = pieces[2 * j + core]
             for at in range(2):
-                first = (2 * at + at_core) * block
+                first = (2 * core + at) * block
                 for part in range(2):
-                    skeleton[source, part, pl.ds(aligned(first, block), block), :] = ref[
-                        at, part
-                    ].astype(F32)
-                    between[source, pl.ds(aligned(part * full + first, block), block), :] = ref[
-                        at, 2 + part
-                    ]
+                    skeleton[source, part, first : first + block, :] = ref[at, part].astype(F32)
+                    value = ref[at, 2 + part]
+                    if core:
+                        value = pltpu.roll(value.astype(F32), full // 2, 1).astype(BF16)
+                    between[source, part * full + first : part * full + first + block, :] = value
 
     def regroup(target):
         columns = []
         for part in range(2):
             rows = [
-                skeleton[s, part, pl.ds(aligned(q * block + target * quarter, quarter), quarter), :]
+                skeleton[s, part, pl.ds(pl.multiple_of(q * block + target * quarter, quarter), quarter), :]
                 for q in range(4)
                 for s in range(clusters)
             ]
@@ -184,53 +211,92 @@
     share, _, angles = excitation.shape
     block = clusters * quarter
     full = 4 * block
+    params = pltpu.CompilerParams(vmem_limit_bytes=32 << 20)
 
     def across(flip):
         return lambda v: lax.ppermute(v, "rows", [(i, i ^ flip) for i in range(4)])
 
     to_x, to_core = across(2), across(1)
-    own_x = excitation.reshape(2 * share, angles)
-    own_l = leaf_factor.reshape(2, clusters, quarter, leaf)
-    own_k = coupling.reshape(2, clusters, quarter, leaf)
-    l_x, k_x, x_x = to_x(own_l), to_x(own_k), to_x(own_x)
-    k_core, x_core = to_core(own_k), to_core(own_x)
-    k_diag, x_diag = to_core(k_x), to_core(x_x)
-    packed, k_mine = pl.pallas_call(
-        functools.partial(local_kernel, clusters, quarter, leaf, share, angles),
+    factor = leaf_factor.reshape(2, block, leaf)
+    weights = coupling.reshape(2, block, leaf)
+    l_x, k_x = to_x(factor), to_x(weights)
+    current = excitation.reshape(2 * share, angles)
+    x_near = to_core(current)
+    k_core = to_core(weights)
+    l_own, k_own, x_own, x_core, keep = pl.pallas_call(
+        functools.partial(load_kernel, share, angles, quarter),
         out_shape=(
-            jax.ShapeDtypeStruct((2, 4, block, angles), BF16),
-            jax.ShapeDtypeStruct((2, full, share), BF16),
+            jax.ShapeDtypeStruct(factor.shape, BF16),
+            jax.ShapeDtypeStruct(weights.shape, BF16),
+            jax.ShapeDtypeStruct((share, 2 * angles), BF16),
+            jax.ShapeDtypeStruct((share, 2 * angles), BF16),
+            jax.ShapeDtypeStruct((4, block, angles), F32),
         ),
-        in_specs=[pl.BlockSpec(memory_space=pltpu.SMEM)] + in_vmem(10),
-        out_specs=tuple(in_vmem(2)),
+        in_specs=[pl.BlockSpec(memory_space=pltpu.SMEM)]
+        + [pl.BlockSpec(memory_space=pl.ANY)] * 3
+        + in_vmem(1),
+        out_specs=tuple(in_vmem(5)),
         scratch_shapes=[
-            pltpu.VMEM((4 * block, leaf), BF16),
-            pltpu.VMEM((2 * full, leaf), BF16),
-            pltpu.VMEM((leaf, 2 * angles), BF16),
+            pltpu.VMEM((2 * share, angles), BF16),
             pltpu.VMEM((2 * share, angles), F32),
+            pltpu.SemaphoreType.DMA((3,)),
         ],
-        compiler_params=pltpu.CompilerParams(vmem_limit_bytes=32 << 20),
-        name="local_skeleton",
-    )(ranks, own_l, l_x, own_k, k_x, k_core, k_diag, own_x, x_x, x_core, x_diag)
-    held = [packed] + [
-        lax.ppermute(packed, "clus", [(i, i ^ j) for i in range(clusters)])
-        for j in range(1, clusters)
-    ]
-    swapped = [to_core(v) for v in held]
+        compiler_params=params,
+        name="load_own",
+    )(ranks, factor, weights, current, x_near)
+    partial, kept_partial, l_all = pl.pallas_call(
+        functools.partial(side_kernel, share, angles),
+        out_shape=(
+            jax.ShapeDtypeStruct((2, 2, block, angles), BF16),
+            jax.ShapeDtypeStruct((2, 2, block, angles), F32),
+            jax.ShapeDtypeStruct((4 * block, leaf), BF16),
+        ),
+        in_specs=in_vmem(4),
+        out_specs=tuple(in_vmem(3)),
+        compiler_params=params,
+        cost_estimate=pl.CostEstimate(flops=1 << 30, bytes_accessed=16 << 20, transcendentals=0),
+        name="side_skeleton",
+    )(l_own, l_x, x_own, x_core)
+    partial_x = to_x(partial)
+    near = pl.pallas_call(
+        near_kernel,
+        out_shape=jax.ShapeDtypeStruct((2, 2 * block, 2 * block), F32),
+        in_specs=in_vmem(3),
+        out_specs=in_vmem(1)[0],
+        scratch_shapes=[pltpu.VMEM((4 * block, leaf), BF16)],
+        compiler_params=params,
+        cost_estimate=pl.CostEstimate(flops=20 << 30, bytes_accessed=16 << 20, transcendentals=0),
+        name="near_columns",
+    )(l_all, k_own, k_core)
+    k_diag = to_core(k_x)
+    packed = pl.pallas_call(
+        between_kernel,
+        out_shape=jax.ShapeDtypeStruct((2, 4, block, angles), BF16),
+        in_specs=in_vmem(7),
+        out_specs=in_vmem(1)[0],
+        scratch_shapes=[pltpu.VMEM((4 * block, leaf), BF16)],
+        compiler_params=params,
+        name="between_skeletons",
+    )(kept_partial, partial_x, near, keep, l_all, k_x, k_diag)
+    pieces = []
+    for j in range(clusters):
+        held = lax.ppermute(packed, "clus", [(i, i ^ j) for i in range(clusters)]) if j else packed
+        pieces += [held, to_core(held)]
     field = pl.pallas_call(
         functools.partial(chain_kernel, clusters, quarter, share, angles),
         out_shape=jax.ShapeDtypeStruct((2 * share, angles), BF16),
-        in_specs=in_vmem(2 * clusters + 1),
+        in_specs=in_vmem(2 * clusters + 4),
         out_specs=in_vmem(1)[0],
         scratch_shapes=[
             pltpu.VMEM((clusters, 2 * full, full), BF16),
             pltpu.VMEM((clusters, 2, full, angles), F32),
             pltpu.VMEM((clusters, full, 2 * angles), BF16),
             pltpu.VMEM((2 * share, angles), F32),
+            pltpu.VMEM((2, full, share), BF16),
         ],
-        compiler_params=pltpu.CompilerParams(vmem_limit_bytes=32 << 20),
+        compiler_params=params,
         name="skeleton_chain",
-    )(*held, *swapped, k_mine)
+    )(*pieces, k_own, k_x, k_core, k_diag)
     return field.reshape(share, 2, angles)
 
 

time: 28.8 us -> 24.6 us (0.85)
  waiting for transfers between devices: 12.6 us -> 7.65 us
  Pallas kernels: 2.66 us -> 3.67 us
    ppermute x11 -> x10, waiting for transfers between devices: 7.68 us -> 2.92 us  [across(): return lambda v: lax.ppermute(v, 'rows', [(i, i ^ flip) for i in range(4)])]
    pallas_call x1 -> x4, Pallas kernels: 1.16 us -> 2.15 us  [the longest x1 1.21 us: gather_body(): pl.pallas_call(functools.partial(load_kernel, share, angles, quarter), ou...]
    ppermute x11 -> x10, starting transfers between devices: 6 us -> 5.66 us  [across(): return lambda v: lax.ppermute(v, 'rows', [(i, i ^ flip) for i in range(4)])]
  transfers between devices with their start and end apart: 14 -> 13, of which waited for: 7 -> 8; matrix products, arithmetic and copies ran while one was open for 0% -> 0% of each run, Pallas kernels for 0% -> 7%
where the time goes in v2:
time: 24.6 us; the launch traced here: 24.4 us
  starting transfers between devices  10.3 us (42%)
  waiting for transfers between devices  7.65 us (31%)
  Pallas kernels  3.67 us (15%)
  local copies, waits for them, and re-layouts  2.72 us (11%)
    ppermute x10, starting transfers between devices, across(): return lambda v: lax.ppermute(v, 'rows', [(i, i ^ flip) for i in range(4)])  5.66 us
    ppermute x3, waiting for transfers between devices, gather_body(): lax.ppermute(packed, 'clus', [(i, i ^ j) for i in range(clusters)])  4.73 us
    ppermute x3, starting transfers between devices, gather_body(): lax.ppermute(packed, 'clus', [(i, i ^ j) for i in range(clusters)])  4.69 us
    ppermute x10, waiting for transfers between devices, across(): return lambda v: lax.ppermute(v, 'rows', [(i, i ^ flip) for i in range(4)])  2.92 us
    unnamed x8, local copies, waits for them, and re-layouts  2.72 us
    pallas_call x1, Pallas kernels, gather_body(): pl.pallas_call(functools.partial(chain_kernel, clusters, quarter, share,...  1.53 us
    pallas_call x1, Pallas kernels, gather_body(): pl.pallas_call(functools.partial(load_kernel, share, angles, quarter), ou...  1.21 us
  transfers between devices with their start and end apart: 13, of which 8 were waited for; matrix products, arithmetic and copies ran while one was open for 0% of the time, Pallas kernels for 7%

profile of v2, /device:TPU:0, one launch (start us, length us, event | category | flops | bytes accessed | tf_op | source)
XLA Modules:
  0.0 24.4 jit_solution(18258734762316195474)
XLA Ops:
  0.0 0.5 %collective-permute-start = (bf16[512,128]{1,0:T(8,128)(2,1)}, bf16[512,128]{1,0:T(8,128)(2,1)S(1)}, u32[]{:S(2)}, u32[]{:S(2)}) collective-permute-start(bf16[512,128]{1,0:T(8,128)(2,1)} %bitcast.4), channel_id=1, source_target_pairs={{0,1},{1,0},{2,3},{3,2},{4,5},{5,4},{6,7},{7,6},{8,9},{9,8},{10,11... | collective-permute-start | bytes 393224 | tf_op jit(solution)/shard_map/ppermute | solution.py:217
  0.5 2.5 %collective-permute-start.1 = (bf16[2,32,1024]{2,1,0:T(8,128)(2,1)}, bf16[2,32,1024]{2,1,0:T(8,128)(2,1)S(1)}, u32[]{:S(2)}, u32[]{:S(2)}) collective-permute-start(bf16[2,32,1024]{2,1,0:T(8,128)(2,1)} %bitcast.6), channel_id=1, source_target_pairs={{0,2},{1,3},{2,0},{3,1},{4,6},{5,7},{6,4},{7,5},{8,10},{9,11},{10,... | collective-permute-start | bytes 393224 | tf_op jit(solution)/shard_map/ppermute | solution.py:217
  3.0 0.1 collective-permute-start.4
  3.1 0.1 collective-permute-start.3
  3.2 0.9 %copy-done = bf16[256,2,128]{2,1,0:T(2,128)(2,1)S(1)} copy-done((bf16[256,2,128]{2,1,0:T(2,128)(2,1)S(1)}, bf16[256,2,128]{2,1,0:T(2,128)(2,1)}, u32[]{:S(2)}) %copy-start) | copy-done | bytes 131096
  4.1 0.9 %copy-done.1 = bf16[2,1,4,8,1024]{4,3,2,1,0:T(8,128)(2,1)S(1)} copy-done((bf16[2,1,4,8,1024]{4,3,2,1,0:T(8,128)(2,1)S(1)}, bf16[2,1,4,8,1024]{4,3,2,1,0:T(8,128)(2,1)}, u32[]{:S(2)}) %copy-start.1) | copy-done | bytes 131096
  5.0 0.9 %copy-done.2 = bf16[2,1,4,8,1024]{4,3,2,1,0:T(8,128)(2,1)S(1)} copy-done((bf16[2,1,4,8,1024]{4,3,2,1,0:T(8,128)(2,1)S(1)}, bf16[2,1,4,8,1024]{4,3,2,1,0:T(8,128)(2,1)}, u32[]{:S(2)}) %copy-start.2) | copy-done | bytes 131096
  5.9 1.2 %load_own.1 = (bf16[2,32,1024]{2,1,0:T(8,128)(2,1)S(1)}, bf16[2,32,1024]{2,1,0:T(8,128)(2,1)S(1)}, bf16[256,256]{1,0:T(8,128)(2,1)S(1)}, bf16[256,256]{1,0:T(8,128)(2,1)S(1)}, f32[4,32,128]{2,1,0:T(8,128)S(1)}) custom-call(s32[4,4]{1,0:T(4,128)S(1)} %copy-done.3, bf16[2,32,1024]{2,1,0:T(8,128)(2,1)S(1)} %bitcast.7, bf16[2,32,1024]{2,1,0:T(8,128)(2,1)S(1)} %bitcast.10, ...), custom_call_target="tpu_custom_call" | custom-call | tf_op jit(solution)/shard_map/load_own/pallas_call | solution.py:226
  7.1 0.4 %collective-permute-done.1.l_x = bf16[2,32,1024]{2,1,0:T(8,128)(2,1)S(1)} collective-permute-done((bf16[2,32,1024]{2,1,0:T(8,128)(2,1)}, bf16[2,32,1024]{2,1,0:T(8,128)(2,1)S(1)}, u32[]{:S(2)}, u32[]{:S(2)}) %collective-permute-start.1) | collective-permute-done | bytes 131104 | tf_op jit(solution)/shard_map/ppermute | solution.py:217
  7.6 0.2 side_skeleton.1
  7.8 2.0 %collective-permute-start.2 = (bf16[2,2,32,128]{3,2,1,0:T(8,128)(2,1)S(1)}, bf16[2,2,32,128]{3,2,1,0:T(8,128)(2,1)S(1)}, u32[]{:S(2)}, u32[]{:S(2)}) collective-permute-start(bf16[2,2,32,128]{3,2,1,0:T(8,128)(2,1)S(1)} %get-tuple-element.17), channel_id=1, source_target_pairs={{0,2},{1,3},{2,0},{3,1},{4,6},{5,7},{6,4},{7,5},{8,10},{9,11},{10,... | collective-permute-start | bytes 98312 | tf_op jit(solution)/shard_map/ppermute | solution.py:217
  9.8 0.3 %collective-permute-done.4.k_x.refs_9_ = bf16[2,32,1024]{2,1,0:T(8,128)(2,1)S(1)} collective-permute-done((bf16[2,32,1024]{2,1,0:T(8,128)(2,1)}, bf16[2,32,1024]{2,1,0:T(8,128)(2,1)S(1)}, u32[]{:S(2)}, u32[]{:S(2)}) %collective-permute-start.4) | collective-permute-done | bytes 131104 | tf_op jit(solution)/shard_map/ppermute | solution.py:217
  10.1 0.4 %near_columns.1.near = f32[2,64,64]{2,1,0:T(8,128)S(1)} custom-call(bf16[128,1024]{1,0:T(8,128)(2,1)S(1)} %get-tuple-element.18.l_all, bf16[2,32,1024]{2,1,0:T(8,128)(2,1)S(1)} %get-tuple-element.19.k_own.refs_8_, bf16[2,32,1024]{2,1,0:T(8,128)(2,1)S(1)} %collective-permute-done.3.k_core.refs_10_), custom_call_target="tpu_custom_call" | custom-call | flops 21474836480 | bytes 16777216 | tf_op jit(solution)/shard_map/near_columns/pallas_call | solution.py:261
  10.5 1.2 %collective-permute-done.2.partial_x = bf16[2,2,32,128]{3,2,1,0:T(8,128)(2,1)S(1)} collective-permute-done((bf16[2,2,32,128]{3,2,1,0:T(8,128)(2,1)S(1)}, bf16[2,2,32,128]{3,2,1,0:T(8,128)(2,1)S(1)}, u32[]{:S(2)}, u32[]{:S(2)}) %collective-permute-start.2) | collective-permute-done | bytes 32800 | tf_op jit(solution)/shard_map/ppermute | solution.py:217
  11.7 0.4 %between_skeletons.1.refs_0_ = bf16[2,4,32,128]{3,2,1,0:T(8,128)(2,1)S(1)} custom-call(f32[2,2,32,128]{3,2,1,0:T(8,128)S(1)} %get-tuple-element.16.partial, bf16[2,2,32,128]{3,2,1,0:T(8,128)(2,1)S(1)} %collective-permute-done.2.partial_x, f32[2,64,64]{2,1,0:T(8,128)S(1)} %near_columns.1.near, f32[4,32,128]{2,1,0:T(8,128)S(1)} %get-tuple-element.20.keep, ...), custom_call_target="tpu_custom_call" | custom-call | tf_op jit(solution)/shard_map/between_skeletons/pallas_call | solution.py:272
  12.1 3.1 %collective-permute-start.9 = (bf16[2,4,32,128]{3,2,1,0:T(8,128)(2,1)S(1)}, bf16[2,4,32,128]{3,2,1,0:T(8,128)(2,1)S(1)}, u32[]{:S(2)}, u32[]{:S(2)}) collective-permute-start(bf16[2,4,32,128]{3,2,1,0:T(8,128)(2,1)S(1)} %between_skeletons.1.refs_0_), channel_id=1, source_target_pairs={{0,8},{4,12},{8,0},{12,4},{1,9},{5,13},{9,1},{13,5},{2,10},{6,14},... | collective-permute-start | bytes 196616 | tf_op jit(solution)/shard_map/ppermute | solution.py:283
  15.3 1.3 %collective-permute-start.11 = (bf16[2,4,32,128]{3,2,1,0:T(8,128)(2,1)S(1)}, bf16[2,4,32,128]{3,2,1,0:T(8,128)(2,1)S(1)}, u32[]{:S(2)}, u32[]{:S(2)}) collective-permute-start(bf16[2,4,32,128]{3,2,1,0:T(8,128)(2,1)S(1)} %between_skeletons.1.refs_0_), channel_id=1, source_target_pairs={{0,12},{4,8},{8,4},{12,0},{1,13},{5,9},{9,5},{13,1},{2,14},{6,10},... | collective-permute-start | bytes 196616 | tf_op jit(solution)/shard_map/ppermute | solution.py:283
  16.6 0.2 collective-permute-start.7
  16.8 1.4 %collective-permute-done.9.refs_4_ = bf16[2,4,32,128]{3,2,1,0:T(8,128)(2,1)S(1)} collective-permute-done((bf16[2,4,32,128]{3,2,1,0:T(8,128)(2,1)S(1)}, bf16[2,4,32,128]{3,2,1,0:T(8,128)(2,1)S(1)}, u32[]{:S(2)}, u32[]{:S(2)}) %collective-permute-start.9) | collective-permute-done | bytes 65568 | tf_op jit(solution)/shard_map/ppermute | solution.py:283
  18.2 3.3 %collective-permute-done.11.refs_6_ = bf16[2,4,32,128]{3,2,1,0:T(8,128)(2,1)S(1)} collective-permute-done((bf16[2,4,32,128]{3,2,1,0:T(8,128)(2,1)S(1)}, bf16[2,4,32,128]{3,2,1,0:T(8,128)(2,1)S(1)}, u32[]{:S(2)}, u32[]{:S(2)}) %collective-permute-start.11) | collective-permute-done | bytes 65568 | tf_op jit(solution)/shard_map/ppermute | solution.py:283
  21.6 0.4 %collective-permute-start.8 = (bf16[2,4,32,128]{3,2,1,0:T(8,128)(2,1)S(1)}, bf16[2,4,32,128]{3,2,1,0:T(8,128)(2,1)S(1)}, u32[]{:S(2)}, u32[]{:S(2)}) collective-permute-start(bf16[2,4,32,128]{3,2,1,0:T(8,128)(2,1)S(1)} %collective-permute-done.7.refs_2_), channel_id=1, source_target_pairs={{0,1},{1,0},{2,3},{3,2},{4,5},{5,4},{6,7},{7,6},{8,9},{9,8},{10,11... | collective-permute-start | bytes 196616 | tf_op jit(solution)/shard_map/ppermute | solution.py:217
  22.0 0.7 %collective-permute-done.12.refs_7_ = bf16[2,4,32,128]{3,2,1,0:T(8,128)(2,1)S(1)} collective-permute-done((bf16[2,4,32,128]{3,2,1,0:T(8,128)(2,1)S(1)}, bf16[2,4,32,128]{3,2,1,0:T(8,128)(2,1)S(1)}, u32[]{:S(2)}, u32[]{:S(2)}) %collective-permute-start.12) | collective-permute-done | bytes 65568 | tf_op jit(solution)/shard_map/ppermute | solution.py:217
  22.7 0.2 collective-permute-done.8.refs_3_
  22.9 1.5 %skeleton_chain.1 = bf16[512,128]{1,0:T(8,128)(2,1)} custom-call(bf16[2,4,32,128]{3,2,1,0:T(8,128)(2,1)S(1)} %between_skeletons.1.refs_0_, bf16[2,4,32,128]{3,2,1,0:T(8,128)(2,1)S(1)} %collective-permute-done.6.refs_1_, bf16[2,4,32,128]{3,2,1,0:T(8,128)(2,1)S(1)} %collective-permute-done.7.refs_2_, ...), custom_call_target="tpu_custom_call" | custom-call | tf_op jit(solution)/shard_map/skeleton_chain/pallas_call | solution.py:285
  (15 shorter events, 0.1 us)
Async XLA Ops:
  0.0 3.2 %copy-start.3 = (s32[4,4]{1,0:T(4,128)S(1)}, s32[4,4]{1,0:T(4,128)}, u32[]{:S(2)}) copy-start(s32[4,4]{1,0:T(4,128)} %ranks.1) | copy-start | bytes 196
  0.0 3.2 %collective-permute-start = (bf16[512,128]{1,0:T(8,128)(2,1)}, bf16[512,128]{1,0:T(8,128)(2,1)S(1)}, u32[]{:S(2)}, u32[]{:S(2)}) collective-permute-start(bf16[512,128]{1,0:T(8,128)(2,1)} %bitcast.4), channel_id=1, source_target_pairs={{0,1},{1,0},{2,3},{3,2},{4,5},{5,4},{6,7},{7,6},{8,9},{9,8},{10,11... | collective-permute-start | bytes 393224 | tf_op jit(solution)/shard_map/ppermute | solution.py:217
  0.5 7.1 %collective-permute-start.1 = (bf16[2,32,1024]{2,1,0:T(8,128)(2,1)}, bf16[2,32,1024]{2,1,0:T(8,128)(2,1)S(1)}, u32[]{:S(2)}, u32[]{:S(2)}) collective-permute-start(bf16[2,32,1024]{2,1,0:T(8,128)(2,1)} %bitcast.6), channel_id=1, source_target_pairs={{0,2},{1,3},{2,0},{3,1},{4,6},{5,7},{6,4},{7,5},{8,10},{9,11},{10,... | collective-permute-start | bytes 393224 | tf_op jit(solution)/shard_map/ppermute | solution.py:217
  3.0 7.1 %collective-permute-start.4 = (bf16[2,32,1024]{2,1,0:T(8,128)(2,1)}, bf16[2,32,1024]{2,1,0:T(8,128)(2,1)S(1)}, u32[]{:S(2)}, u32[]{:S(2)}) collective-permute-start(bf16[2,32,1024]{2,1,0:T(8,128)(2,1)} %bitcast.8), channel_id=1, source_target_pairs={{0,2},{1,3},{2,0},{3,1},{4,6},{5,7},{6,4},{7,5},{8,10},{9,11},{10,... | collective-permute-start | bytes 393224 | tf_op jit(solution)/shard_map/ppermute | solution.py:217
  3.1 7.0 %collective-permute-start.3 = (bf16[2,32,1024]{2,1,0:T(8,128)(2,1)}, bf16[2,32,1024]{2,1,0:T(8,128)(2,1)S(1)}, u32[]{:S(2)}, u32[]{:S(2)}) collective-permute-start(bf16[2,32,1024]{2,1,0:T(8,128)(2,1)} %bitcast.9), channel_id=1, source_target_pairs={{0,1},{1,0},{2,3},{3,2},{4,5},{5,4},{6,7},{7,6},{8,9},{9,8},{10,11... | collective-permute-start | bytes 393224 | tf_op jit(solution)/shard_map/ppermute | solution.py:217
  3.2 0.9 %copy-start = (bf16[256,2,128]{2,1,0:T(2,128)(2,1)S(1)}, bf16[256,2,128]{2,1,0:T(2,128)(2,1)}, u32[]{:S(2)}) copy-start(bf16[256,2,128]{2,1,0:T(2,128)(2,1)} %param.4) | copy-start | bytes 393220
  4.1 0.9 %copy-start.1 = (bf16[2,1,4,8,1024]{4,3,2,1,0:T(8,128)(2,1)S(1)}, bf16[2,1,4,8,1024]{4,3,2,1,0:T(8,128)(2,1)}, u32[]{:S(2)}) copy-start(bf16[2,1,4,8,1024]{4,3,2,1,0:T(8,128)(2,1)} %param.5) | copy-start | bytes 393220
  5.0 0.9 %copy-start.2 = (bf16[2,1,4,8,1024]{4,3,2,1,0:T(8,128)(2,1)S(1)}, bf16[2,1,4,8,1024]{4,3,2,1,0:T(8,128)(2,1)}, u32[]{:S(2)}) copy-start(bf16[2,1,4,8,1024]{4,3,2,1,0:T(8,128)(2,1)} %param.6) | copy-start | bytes 393220
  7.8 4.0 %collective-permute-start.2 = (bf16[2,2,32,128]{3,2,1,0:T(8,128)(2,1)S(1)}, bf16[2,2,32,128]{3,2,1,0:T(8,128)(2,1)S(1)}, u32[]{:S(2)}, u32[]{:S(2)}) collective-permute-start(bf16[2,2,32,128]{3,2,1,0:T(8,128)(2,1)S(1)} %get-tuple-element.17), channel_id=1, source_target_pairs={{0,2},{1,3},{2,0},{3,1},{4,6},{5,7},{6,4},{7,5},{8,10},{9,11},{10,... | collective-permute-start | bytes 98312 | tf_op jit(solution)/shard_map/ppermute | solution.py:217
  10.1 1.6 %collective-permute-start.5 = (bf16[2,32,1024]{2,1,0:T(8,128)(2,1)S(1)}, bf16[2,32,1024]{2,1,0:T(8,128)(2,1)S(1)}, u32[]{:S(2)}, u32[]{:S(2)}) collective-permute-start(bf16[2,32,1024]{2,1,0:T(8,128)(2,1)S(1)} %collective-permute-done.4.k_x.refs_9_), channel_id=1, source_target_pairs={{0,1},{1,0},{2,3},{3,2},{4,5},{5,4},{6,7},{7,6},{8,9},{9,8},{10,11... | collective-permute-start | bytes 393224 | tf_op jit(solution)/shard_map/ppermute | solution.py:217
  12.1 6.1 %collective-permute-start.9 = (bf16[2,4,32,128]{3,2,1,0:T(8,128)(2,1)S(1)}, bf16[2,4,32,128]{3,2,1,0:T(8,128)(2,1)S(1)}, u32[]{:S(2)}, u32[]{:S(2)}) collective-permute-start(bf16[2,4,32,128]{3,2,1,0:T(8,128)(2,1)S(1)} %between_skeletons.1.refs_0_), channel_id=1, source_target_pairs={{0,8},{4,12},{8,0},{12,4},{1,9},{5,13},{9,1},{13,5},{2,10},{6,14},... | collective-permute-start | bytes 196616 | tf_op jit(solution)/shard_map/ppermute | solution.py:283
  15.3 6.2 %collective-permute-start.11 = (bf16[2,4,32,128]{3,2,1,0:T(8,128)(2,1)S(1)}, bf16[2,4,32,128]{3,2,1,0:T(8,128)(2,1)S(1)}, u32[]{:S(2)}, u32[]{:S(2)}) collective-permute-start(bf16[2,4,32,128]{3,2,1,0:T(8,128)(2,1)S(1)} %between_skeletons.1.refs_0_), channel_id=1, source_target_pairs={{0,12},{4,8},{8,4},{12,0},{1,13},{5,9},{9,5},{13,1},{2,14},{6,10},... | collective-permute-start | bytes 196616 | tf_op jit(solution)/shard_map/ppermute | solution.py:283
  16.6 5.0 %collective-permute-start.7 = (bf16[2,4,32,128]{3,2,1,0:T(8,128)(2,1)S(1)}, bf16[2,4,32,128]{3,2,1,0:T(8,128)(2,1)S(1)}, u32[]{:S(2)}, u32[]{:S(2)}) collective-permute-start(bf16[2,4,32,128]{3,2,1,0:T(8,128)(2,1)S(1)} %between_skeletons.1.refs_0_), channel_id=1, source_target_pairs={{0,4},{4,0},{8,12},{12,8},{1,5},{5,1},{9,13},{13,9},{2,6},{6,2},{1... | collective-permute-start | bytes 196616 | tf_op jit(solution)/shard_map/ppermute | solution.py:283
  16.8 5.2 %collective-permute-start.6 = (bf16[2,4,32,128]{3,2,1,0:T(8,128)(2,1)S(1)}, bf16[2,4,32,128]{3,2,1,0:T(8,128)(2,1)S(1)}, u32[]{:S(2)}, u32[]{:S(2)}) collective-permute-start(bf16[2,4,32,128]{3,2,1,0:T(8,128)(2,1)S(1)} %between_skeletons.1.refs_0_), channel_id=1, source_target_pairs={{0,1},{1,0},{2,3},{3,2},{4,5},{5,4},{6,7},{7,6},{8,9},{9,8},{10,11... | collective-permute-start | bytes 196616 | tf_op jit(solution)/shard_map/ppermute | solution.py:217
  18.2 3.8 %collective-permute-start.10 = (bf16[2,4,32,128]{3,2,1,0:T(8,128)(2,1)S(1)}, bf16[2,4,32,128]{3,2,1,0:T(8,128)(2,1)S(1)}, u32[]{:S(2)}, u32[]{:S(2)}) collective-permute-start(bf16[2,4,32,128]{3,2,1,0:T(8,128)(2,1)S(1)} %collective-permute-done.9.refs_4_), channel_id=1, source_target_pairs={{0,1},{1,0},{2,3},{3,2},{4,5},{5,4},{6,7},{7,6},{8,9},{9,8},{10,11... | collective-permute-start | bytes 196616 | tf_op jit(solution)/shard_map/ppermute | solution.py:217
  21.5 1.3 %collective-permute-start.12 = (bf16[2,4,32,128]{3,2,1,0:T(8,128)(2,1)S(1)}, bf16[2,4,32,128]{3,2,1,0:T(8,128)(2,1)S(1)}, u32[]{:S(2)}, u32[]{:S(2)}) collective-permute-start(bf16[2,4,32,128]{3,2,1,0:T(8,128)(2,1)S(1)} %collective-permute-done.11.refs_6_), channel_id=1, source_target_pairs={{0,1},{1,0},{2,3},{3,2},{4,5},{5,4},{6,7},{7,6},{8,9},{9,8},{10,11... | collective-permute-start | bytes 196616 | tf_op jit(solution)/shard_map/ppermute | solution.py:217
  21.6 1.3 %collective-permute-start.8 = (bf16[2,4,32,128]{3,2,1,0:T(8,128)(2,1)S(1)}, bf16[2,4,32,128]{3,2,1,0:T(8,128)(2,1)S(1)}, u32[]{:S(2)}, u32[]{:S(2)}) collective-permute-start(bf16[2,4,32,128]{3,2,1,0:T(8,128)(2,1)S(1)} %collective-permute-done.7.refs_2_), channel_id=1, source_target_pairs={{0,1},{1,0},{2,3},{3,2},{4,5},{5,4},{6,7},{7,6},{8,9},{9,8},{10,11... | collective-permute-start | bytes 196616 | tf_op jit(solution)/shard_map/ppermute | solution.py:217

commit v3 on v2

--- a/solution.py
+++ b/solution.py
@@ -137,69 +137,81 @@
     near[0], near[1] = operator_columns(l_all, (k_own, k_core), k_rows)
 
 
-def between_kernel(partial, partial_x, near, keep, l_all, k_x, k_diag, packed, k_rows):
+def far_kernel(near, keep, l_all, k_x, k_diag, between, k_rows):
     block = keep.shape[1]
-    parts = []
     for part, far in enumerate(operator_columns(l_all, (k_x, k_diag), k_rows)):
         value = near[part]
         columns = [value[:, :block], far[:, :block], value[:, block:], far[:, block:]]
-        parts.append(jnp.concatenate(columns, axis=1))
+        value = jnp.concatenate(columns, axis=1)
+        for at in range(2):
+            between[at, part] = (value[at * block : (at + 1) * block] * keep[at]).astype(BF16)
+
+
+def pack_kernel(partial, partial_x, keep, between, packed):
     for at in range(2):
-        values = [partial[at, part] + partial_x[1 - at, part].astype(F32) for part in range(2)]
-        values += [value[at * block : (at + 1) * block] for value in parts]
-        for i, value in enumerate(values):
-            packed[at, i] = (value * keep[at]).astype(BF16)
-
-
-def chain_kernel(clusters, quarter, share, angles, *refs):
-    pieces, k_quarters = refs[: 2 * clusters], refs[2 * clusters : 2 * clusters + 4]
-    field, between, skeleton, kept, wide, k_mine = refs[2 * clusters + 4 :]
+        for part in range(2):
+            value = partial[at, part] + partial_x[1 - at, part].astype(F32)
+            packed[at, part] = (value * keep[at]).astype(BF16)
+            packed[at, 2 + part] = between[at, part]
+
+
+def fold_kernel(share, k_own, k_x, k_core, k_diag, folded, wide):
     row = lax.axis_index("rows")
+    mine = pl.ds(pl.multiple_of(row * share, share), share)
+    real, imag = (
+        jnp.concatenate([k[part, :, mine].astype(F32) for k in (k_own, k_x, k_core, k_diag)], axis=0).T
+        for part in range(2)
+    )
+    full = real.shape[1]
+    even, odd = pl.ds(0, share, stride=2), pl.ds(1, share, stride=2)
+    wide[0, even, :] = real
+    wide[1, even, :] = -imag
+    wide[0, odd, :] = imag
+    wide[1, odd, :] = real
+    folded[:, :full] = wide[0].astype(BF16)
+    folded[:, full:] = wide[1].astype(BF16)
+
+
+def chain_kernel(clusters, quarter, *refs):
+    pieces, folded, field = refs[: 2 * clusters], refs[2 * clusters], refs[2 * clusters + 1]
+    between, skeleton, kept = refs[2 * clusters + 2 :]
     cluster = lax.axis_index("clus")
     block = clusters * quarter
     full = 4 * block
-    for at in range(4):
-        for part in range(2):
-            k_mine[part, at * block : (at + 1) * block, :] = k_quarters[at][
-                part, :, pl.ds(pl.multiple_of(row * share, share), share)
-            ]
     for j in range(clusters):
         source = cluster ^ j
         for core in range(2):
             ref = pieces[2 * j + core]
             for at in range(2):
                 first = (2 * core + at) * block
+                rows = slice(first, first + block)
                 for part in range(2):
-                    skeleton[source, part, first : first + block, :] = ref[at, part].astype(F32)
+                    columns = slice(part * full, (part + 1) * full)
+                    skeleton[source, rows, columns] = ref[at, part].astype(F32)
                     value = ref[at, 2 + part]
                     if core:
                         value = pltpu.roll(value.astype(F32), full // 2, 1).astype(BF16)
-                    between[source, part * full + first : part * full + first + block, :] = value
-
-    def regroup(target):
-        columns = []
-        for part in range(2):
-            rows = [
-                skeleton[s, part, pl.ds(pl.multiple_of(q * block + target * quarter, quarter), quarter), :]
-                for q in range(4)
-                for s in range(clusters)
-            ]
-            columns.append(jnp.concatenate(rows, axis=0))
-        return jnp.concatenate(columns, axis=1).astype(BF16)
+                    between[source, rows, columns] = value
+
+    def gather(target):
+        rows = [
+            skeleton[s, pl.ds(pl.multiple_of(q * block + target * quarter, quarter), quarter), :]
+            for q in range(4)
+            for s in range(clusters)
+        ]
+        return jnp.concatenate(rows, axis=0)
 
     for step in range(STEPS - 1):
         for target in range(clusters):
-            kept[target] = regroup(target)
+            value = gather(target)
+            kept[target, :full, :] = value.astype(BF16)
+            kept[target, full:, :full] = (-value[:, full:]).astype(BF16)
+            kept[target, full:, full:] = value[:, :full].astype(BF16)
         for source in range(clusters):
-            product = jnp.dot(between[source], kept[source], preferred_element_type=F32)
-            skeleton[source, 0], skeleton[source, 1] = combine(product, full, angles)
-    last = regroup(cluster)
-    contract = (((0,), (0,)), ((), ()))
-    with_real = lax.dot_general(k_mine[0], last, contract, preferred_element_type=F32)
-    with_imag = lax.dot_general(k_mine[1], last, contract, preferred_element_type=F32)
-    wide[pl.ds(0, share, stride=2), :] = with_real[:, :angles] - with_imag[:, angles:]
-    wide[pl.ds(1, share, stride=2), :] = with_real[:, angles:] + with_imag[:, :angles]
-    field[...] = wide[...].astype(BF16)
+            skeleton[source] = jnp.dot(between[source], kept[source], preferred_element_type=F32)
+    value = gather(cluster)
+    last = jnp.concatenate([value[:, :full], value[:, full:]], axis=0).astype(BF16)
+    field[...] = jnp.dot(folded[...], last, preferred_element_type=F32).astype(BF16)
 
 
 def in_vmem(count):
@@ -269,34 +281,51 @@
         name="near_columns",
     )(l_all, k_own, k_core)
     k_diag = to_core(k_x)
+    between = pl.pallas_call(
+        far_kernel,
+        out_shape=jax.ShapeDtypeStruct((2, 2, block, full), BF16),
+        in_specs=in_vmem(5),
+        out_specs=in_vmem(1)[0],
+        scratch_shapes=[pltpu.VMEM((4 * block, leaf), BF16)],
+        compiler_params=params,
+        name="far_columns",
+    )(near, keep, l_all, k_x, k_diag)
     packed = pl.pallas_call(
-        between_kernel,
+        pack_kernel,
         out_shape=jax.ShapeDtypeStruct((2, 4, block, angles), BF16),
-        in_specs=in_vmem(7),
-        out_specs=in_vmem(1)[0],
-        scratch_shapes=[pltpu.VMEM((4 * block, leaf), BF16)],
-        compiler_params=params,
-        name="between_skeletons",
-    )(kept_partial, partial_x, near, keep, l_all, k_x, k_diag)
+        in_specs=in_vmem(4),
+        out_specs=in_vmem(1)[0],
+        compiler_params=params,
+        name="pack_rows",
+    )(kept_partial, partial_x, keep, between)
+    folded = pl.pallas_call(
+        functools.partial(fold_kernel, share),
+        out_shape=jax.ShapeDtypeStruct((2 * share, 2 * full), BF16),
+        in_specs=in_vmem(4),
+        out_specs=in_vmem(1)[0],
+        scratch_shapes=[pltpu.VMEM((2, 2 * share, full), F32)],
+        compiler_params=params,
+        name="fold_coupling",
+    )(k_own, k_x, k_core, k_diag)
+    held = {0: packed}
+    for j in range(1, clusters):
+        held[j] = lax.ppermute(packed, "clus", [(i, i ^ j) for i in range(clusters)])
     pieces = []
     for j in range(clusters):
-        held = lax.ppermute(packed, "clus", [(i, i ^ j) for i in range(clusters)]) if j else packed
-        pieces += [held, to_core(held)]
+        pieces += [held[j], to_core(held[j])]
     field = pl.pallas_call(
-        functools.partial(chain_kernel, clusters, quarter, share, angles),
+        functools.partial(chain_kernel, clusters, quarter),
         out_shape=jax.ShapeDtypeStruct((2 * share, angles), BF16),
-        in_specs=in_vmem(2 * clusters + 4),
+        in_specs=in_vmem(2 * clusters + 1),
         out_specs=in_vmem(1)[0],
         scratch_shapes=[
-            pltpu.VMEM((clusters, 2 * full, full), BF16),
-            pltpu.VMEM((clusters, 2, full, angles), F32),
-            pltpu.VMEM((clusters, full, 2 * angles), BF16),
-            pltpu.VMEM((2 * share, angles), F32),
-            pltpu.VMEM((2, full, share), BF16),
+            pltpu.VMEM((clusters, full, 2 * full), BF16),
+            pltpu.VMEM((clusters, full, 2 * angles), F32),
+            pltpu.VMEM((clusters, 2 * full, 2 * angles), BF16),
         ],
         compiler_params=params,
         name="skeleton_chain",
-    )(*pieces, k_own, k_x, k_core, k_diag)
+    )(*pieces, folded)
     return field.reshape(share, 2, angles)
 
 

time: 24.6 us -> 24.2 us (0.984)
  waiting for transfers between devices: 7.65 us -> 7.32 us
    ppermute x10, waiting for transfers between devices: 2.92 us -> 2.47 us  [across(): return lambda v: lax.ppermute(v, 'rows', [(i, i ^ flip) for i in range(4)])]
    pallas_call x2 -> x4, Pallas kernels: 1.91 us -> 2 us  [the longest x1 1.44 us: gather_body(): pl.pallas_call(functools.partial(chain_kernel, clusters, quarter), out_sh...]
  transfers between devices with their start and end apart: 13 -> 13, of which waited for: 8 -> 8; matrix products, arithmetic and copies ran while one was open for 0% -> 0% of each run, Pallas kernels for 7% -> 10%
where the time goes in v3:
time: 24.2 us; the launch traced here: 24.1 us
  starting transfers between devices  10.2 us (42%)
  waiting for transfers between devices  7.32 us (30%)
  Pallas kernels  3.76 us (16%)
  local copies, waits for them, and re-layouts  2.72 us (11%)
    ppermute x10, starting transfers between devices, across(): return lambda v: lax.ppermute(v, 'rows', [(i, i ^ flip) for i in range(4)])  5.65 us
    ppermute x3, waiting for transfers between devices, gather_body(): lax.ppermute(packed, 'clus', [(i, i ^ j) for i in range(clusters)])  4.85 us
    ppermute x3, starting transfers between devices, gather_body(): lax.ppermute(packed, 'clus', [(i, i ^ j) for i in range(clusters)])  4.56 us
    unnamed x8, local copies, waits for them, and re-layouts  2.72 us
    ppermute x10, waiting for transfers between devices, across(): return lambda v: lax.ppermute(v, 'rows', [(i, i ^ flip) for i in range(4)])  2.47 us
    pallas_call x1, Pallas kernels, gather_body(): pl.pallas_call(functools.partial(chain_kernel, clusters, quarter), out_sh...  1.44 us
    pallas_call x1, Pallas kernels, gather_body(): pl.pallas_call(functools.partial(load_kernel, share, angles, quarter), ou...  1.21 us
  transfers between devices with their start and end apart: 13, of which 8 were waited for; matrix products, arithmetic and copies ran while one was open for 0% of the time, Pallas kernels for 10%

profile of v3, /device:TPU:0, one launch (start us, length us, event | category | flops | bytes accessed | tf_op | source)
XLA Modules:
  0.0 24.1 jit_solution(1847013295659149716)
XLA Ops:
  0.0 0.5 %collective-permute-start = (bf16[512,128]{1,0:T(8,128)(2,1)}, bf16[512,128]{1,0:T(8,128)(2,1)S(1)}, u32[]{:S(2)}, u32[]{:S(2)}) collective-permute-start(bf16[512,128]{1,0:T(8,128)(2,1)} %bitcast.4), channel_id=1, source_target_pairs={{0,1},{1,0},{2,3},{3,2},{4,5},{5,4},{6,7},{7,6},{8,9},{9,8},{10,11... | collective-permute-start | bytes 393224 | tf_op jit(solution)/shard_map/ppermute | solution.py:229
  0.5 2.5 %collective-permute-start.1 = (bf16[2,32,1024]{2,1,0:T(8,128)(2,1)}, bf16[2,32,1024]{2,1,0:T(8,128)(2,1)S(1)}, u32[]{:S(2)}, u32[]{:S(2)}) collective-permute-start(bf16[2,32,1024]{2,1,0:T(8,128)(2,1)} %bitcast.6), channel_id=1, source_target_pairs={{0,2},{1,3},{2,0},{3,1},{4,6},{5,7},{6,4},{7,5},{8,10},{9,11},{10,... | collective-permute-start | bytes 393224 | tf_op jit(solution)/shard_map/ppermute | solution.py:229
  3.0 0.1 collective-permute-start.4
  3.2 0.9 %copy-done = bf16[256,2,128]{2,1,0:T(2,128)(2,1)S(1)} copy-done((bf16[256,2,128]{2,1,0:T(2,128)(2,1)S(1)}, bf16[256,2,128]{2,1,0:T(2,128)(2,1)}, u32[]{:S(2)}) %copy-start) | copy-done | bytes 131096
  4.1 0.9 %copy-done.1 = bf16[2,1,4,8,1024]{4,3,2,1,0:T(8,128)(2,1)S(1)} copy-done((bf16[2,1,4,8,1024]{4,3,2,1,0:T(8,128)(2,1)S(1)}, bf16[2,1,4,8,1024]{4,3,2,1,0:T(8,128)(2,1)}, u32[]{:S(2)}) %copy-start.1) | copy-done | bytes 131096
  5.0 0.9 %copy-done.2 = bf16[2,1,4,8,1024]{4,3,2,1,0:T(8,128)(2,1)S(1)} copy-done((bf16[2,1,4,8,1024]{4,3,2,1,0:T(8,128)(2,1)S(1)}, bf16[2,1,4,8,1024]{4,3,2,1,0:T(8,128)(2,1)}, u32[]{:S(2)}) %copy-start.2) | copy-done | bytes 131096
  5.9 1.2 %load_own.1 = (bf16[2,32,1024]{2,1,0:T(8,128)(2,1)S(1)}, bf16[2,32,1024]{2,1,0:T(8,128)(2,1)S(1)}, bf16[256,256]{1,0:T(8,128)(2,1)S(1)}, bf16[256,256]{1,0:T(8,128)(2,1)S(1)}, f32[4,32,128]{2,1,0:T(8,128)S(1)}) custom-call(s32[4,4]{1,0:T(4,128)S(1)} %copy-done.3, bf16[2,32,1024]{2,1,0:T(8,128)(2,1)S(1)} %bitcast.7, bf16[2,32,1024]{2,1,0:T(8,128)(2,1)S(1)} %bitcast.10, ...), custom_call_target="tpu_custom_call" | custom-call | tf_op jit(solution)/shard_map/load_own/pallas_call | solution.py:238
  7.1 0.4 %collective-permute-done.1.l_x = bf16[2,32,1024]{2,1,0:T(8,128)(2,1)S(1)} collective-permute-done((bf16[2,32,1024]{2,1,0:T(8,128)(2,1)}, bf16[2,32,1024]{2,1,0:T(8,128)(2,1)S(1)}, u32[]{:S(2)}, u32[]{:S(2)}) %collective-permute-start.1) | collective-permute-done | bytes 131104 | tf_op jit(solution)/shard_map/ppermute | solution.py:229
  7.6 0.2 side_skeleton.1
  7.8 2.0 %collective-permute-start.2 = (bf16[2,2,32,128]{3,2,1,0:T(8,128)(2,1)S(1)}, bf16[2,2,32,128]{3,2,1,0:T(8,128)(2,1)S(1)}, u32[]{:S(2)}, u32[]{:S(2)}) collective-permute-start(bf16[2,2,32,128]{3,2,1,0:T(8,128)(2,1)S(1)} %get-tuple-element.17), channel_id=1, source_target_pairs={{0,2},{1,3},{2,0},{3,1},{4,6},{5,7},{6,4},{7,5},{8,10},{9,11},{10,... | collective-permute-start | bytes 98312 | tf_op jit(solution)/shard_map/ppermute | solution.py:229
  9.8 0.3 %collective-permute-done.4.k_x = bf16[2,32,1024]{2,1,0:T(8,128)(2,1)S(1)} collective-permute-done((bf16[2,32,1024]{2,1,0:T(8,128)(2,1)}, bf16[2,32,1024]{2,1,0:T(8,128)(2,1)S(1)}, u32[]{:S(2)}, u32[]{:S(2)}) %collective-permute-start.4) | collective-permute-done | bytes 131104 | tf_op jit(solution)/shard_map/ppermute | solution.py:229
  10.1 0.4 %near_columns.1.near = f32[2,64,64]{2,1,0:T(8,128)S(1)} custom-call(bf16[128,1024]{1,0:T(8,128)(2,1)S(1)} %get-tuple-element.19.l_all, bf16[2,32,1024]{2,1,0:T(8,128)(2,1)S(1)} %get-tuple-element.20.k_own, bf16[2,32,1024]{2,1,0:T(8,128)(2,1)S(1)} %collective-permute-done.3.k_core), custom_call_target="tpu_custom_call" | custom-call | flops 21474836480 | bytes 16777216 | tf_op jit(solution)/shard_map/near_columns/pallas_call | solution.py:273
  10.5 1.0 %collective-permute-done.5.k_diag = bf16[2,32,1024]{2,1,0:T(8,128)(2,1)S(1)} collective-permute-done((bf16[2,32,1024]{2,1,0:T(8,128)(2,1)S(1)}, bf16[2,32,1024]{2,1,0:T(8,128)(2,1)S(1)}, u32[]{:S(2)}, u32[]{:S(2)}) %collective-permute-start.5) | collective-permute-done | bytes 131104 | tf_op jit(solution)/shard_map/ppermute | solution.py:229
  11.5 0.4 %far_columns.1.between = bf16[2,2,32,128]{3,2,1,0:T(8,128)(2,1)S(1)} custom-call(f32[2,64,64]{2,1,0:T(8,128)S(1)} %near_columns.1.near, f32[4,32,128]{2,1,0:T(8,128)S(1)} %get-tuple-element.18.keep, bf16[128,1024]{1,0:T(8,128)(2,1)S(1)} %get-tuple-element.19.l_all, bf16[2,32,1024]{2,1,0:T(8,128)(2,1)S(1)} %collective-permute-done.4.k_x, ...), custom_call_target="tpu_custom_call" | custom-call | tf_op jit(solution)/shard_map/far_columns/pallas_call | solution.py:284
  11.9 3.0 %collective-permute-start.9 = (bf16[2,4,32,128]{3,2,1,0:T(8,128)(2,1)S(1)}, bf16[2,4,32,128]{3,2,1,0:T(8,128)(2,1)S(1)}, u32[]{:S(2)}, u32[]{:S(2)}) collective-permute-start(bf16[2,4,32,128]{3,2,1,0:T(8,128)(2,1)S(1)} %pack_rows.1.refs_0_), channel_id=1, source_target_pairs={{0,8},{4,12},{8,0},{12,4},{1,9},{5,13},{9,1},{13,5},{2,10},{6,14},... | collective-permute-start | bytes 196616 | tf_op jit(solution)/shard_map/ppermute | solution.py:312
  14.9 1.3 %collective-permute-start.11 = (bf16[2,4,32,128]{3,2,1,0:T(8,128)(2,1)S(1)}, bf16[2,4,32,128]{3,2,1,0:T(8,128)(2,1)S(1)}, u32[]{:S(2)}, u32[]{:S(2)}) collective-permute-start(bf16[2,4,32,128]{3,2,1,0:T(8,128)(2,1)S(1)} %pack_rows.1.refs_0_), channel_id=1, source_target_pairs={{0,12},{4,8},{8,4},{12,0},{1,13},{5,9},{9,5},{13,1},{2,14},{6,10},... | collective-permute-start | bytes 196616 | tf_op jit(solution)/shard_map/ppermute | solution.py:312
  16.2 0.2 collective-permute-start.7
  16.5 2.3 %collective-permute-done.9.refs_4_ = bf16[2,4,32,128]{3,2,1,0:T(8,128)(2,1)S(1)} collective-permute-done((bf16[2,4,32,128]{3,2,1,0:T(8,128)(2,1)S(1)}, bf16[2,4,32,128]{3,2,1,0:T(8,128)(2,1)S(1)}, u32[]{:S(2)}, u32[]{:S(2)}) %collective-permute-start.9) | collective-permute-done | bytes 65568 | tf_op jit(solution)/shard_map/ppermute | solution.py:312
  18.7 2.5 %collective-permute-done.11.refs_6_ = bf16[2,4,32,128]{3,2,1,0:T(8,128)(2,1)S(1)} collective-permute-done((bf16[2,4,32,128]{3,2,1,0:T(8,128)(2,1)S(1)}, bf16[2,4,32,128]{3,2,1,0:T(8,128)(2,1)S(1)}, u32[]{:S(2)}, u32[]{:S(2)}) %collective-permute-start.11) | collective-permute-done | bytes 65568 | tf_op jit(solution)/shard_map/ppermute | solution.py:312
  21.3 0.4 %collective-permute-start.8 = (bf16[2,4,32,128]{3,2,1,0:T(8,128)(2,1)S(1)}, bf16[2,4,32,128]{3,2,1,0:T(8,128)(2,1)S(1)}, u32[]{:S(2)}, u32[]{:S(2)}) collective-permute-start(bf16[2,4,32,128]{3,2,1,0:T(8,128)(2,1)S(1)} %collective-permute-done.7.refs_2_), channel_id=1, source_target_pairs={{0,1},{1,0},{2,3},{3,2},{4,5},{5,4},{6,7},{7,6},{8,9},{9,8},{10,11... | collective-permute-start | bytes 196616 | tf_op jit(solution)/shard_map/ppermute | solution.py:229
  21.7 0.2 fold_coupling.1.refs_8_
  21.9 0.5 %collective-permute-done.12.refs_7_ = bf16[2,4,32,128]{3,2,1,0:T(8,128)(2,1)S(1)} collective-permute-done((bf16[2,4,32,128]{3,2,1,0:T(8,128)(2,1)S(1)}, bf16[2,4,32,128]{3,2,1,0:T(8,128)(2,1)S(1)}, u32[]{:S(2)}, u32[]{:S(2)}) %collective-permute-start.12) | collective-permute-done | bytes 65568 | tf_op jit(solution)/shard_map/ppermute | solution.py:229
  22.5 0.2 collective-permute-done.8.refs_3_
  22.6 1.4 %skeleton_chain.1 = bf16[512,128]{1,0:T(8,128)(2,1)} custom-call(bf16[2,4,32,128]{3,2,1,0:T(8,128)(2,1)S(1)} %pack_rows.1.refs_0_, bf16[2,4,32,128]{3,2,1,0:T(8,128)(2,1)S(1)} %collective-permute-done.6.refs_1_, bf16[2,4,32,128]{3,2,1,0:T(8,128)(2,1)S(1)} %collective-permute-done.7.refs_2_, bf16[2,4,32,128]{3,2,1,0:T(8,128)(2,1)S(1)} %collective-permute-done.8.refs_3_, ...), custom_call_target="tpu_custom_call" | custom-call | tf_op jit(solution)/shard_map/skeleton_chain/pallas_call | solution.py:316
  (17 shorter events, 0.2 us)
Async XLA Ops:
  0.0 3.2 %copy-start.3 = (s32[4,4]{1,0:T(4,128)S(1)}, s32[4,4]{1,0:T(4,128)}, u32[]{:S(2)}) copy-start(s32[4,4]{1,0:T(4,128)} %ranks.1) | copy-start | bytes 196
  0.0 3.2 %collective-permute-start = (bf16[512,128]{1,0:T(8,128)(2,1)}, bf16[512,128]{1,0:T(8,128)(2,1)S(1)}, u32[]{:S(2)}, u32[]{:S(2)}) collective-permute-start(bf16[512,128]{1,0:T(8,128)(2,1)} %bitcast.4), channel_id=1, source_target_pairs={{0,1},{1,0},{2,3},{3,2},{4,5},{5,4},{6,7},{7,6},{8,9},{9,8},{10,11... | collective-permute-start | bytes 393224 | tf_op jit(solution)/shard_map/ppermute | solution.py:229
  0.5 7.1 %collective-permute-start.1 = (bf16[2,32,1024]{2,1,0:T(8,128)(2,1)}, bf16[2,32,1024]{2,1,0:T(8,128)(2,1)S(1)}, u32[]{:S(2)}, u32[]{:S(2)}) collective-permute-start(bf16[2,32,1024]{2,1,0:T(8,128)(2,1)} %bitcast.6), channel_id=1, source_target_pairs={{0,2},{1,3},{2,0},{3,1},{4,6},{5,7},{6,4},{7,5},{8,10},{9,11},{10,... | collective-permute-start | bytes 393224 | tf_op jit(solution)/shard_map/ppermute | solution.py:229
  3.0 7.1 %collective-permute-start.4 = (bf16[2,32,1024]{2,1,0:T(8,128)(2,1)}, bf16[2,32,1024]{2,1,0:T(8,128)(2,1)S(1)}, u32[]{:S(2)}, u32[]{:S(2)}) collective-permute-start(bf16[2,32,1024]{2,1,0:T(8,128)(2,1)} %bitcast.8), channel_id=1, source_target_pairs={{0,2},{1,3},{2,0},{3,1},{4,6},{5,7},{6,4},{7,5},{8,10},{9,11},{10,... | collective-permute-start | bytes 393224 | tf_op jit(solution)/shard_map/ppermute | solution.py:229
  3.1 7.0 %collective-permute-start.3 = (bf16[2,32,1024]{2,1,0:T(8,128)(2,1)}, bf16[2,32,1024]{2,1,0:T(8,128)(2,1)S(1)}, u32[]{:S(2)}, u32[]{:S(2)}) collective-permute-start(bf16[2,32,1024]{2,1,0:T(8,128)(2,1)} %bitcast.9), channel_id=1, source_target_pairs={{0,1},{1,0},{2,3},{3,2},{4,5},{5,4},{6,7},{7,6},{8,9},{9,8},{10,11... | collective-permute-start | bytes 393224 | tf_op jit(solution)/shard_map/ppermute | solution.py:229
  3.2 0.9 %copy-start = (bf16[256,2,128]{2,1,0:T(2,128)(2,1)S(1)}, bf16[256,2,128]{2,1,0:T(2,128)(2,1)}, u32[]{:S(2)}) copy-start(bf16[256,2,128]{2,1,0:T(2,128)(2,1)} %param.4) | copy-start | bytes 393220
  4.1 0.9 %copy-start.1 = (bf16[2,1,4,8,1024]{4,3,2,1,0:T(8,128)(2,1)S(1)}, bf16[2,1,4,8,1024]{4,3,2,1,0:T(8,128)(2,1)}, u32[]{:S(2)}) copy-start(bf16[2,1,4,8,1024]{4,3,2,1,0:T(8,128)(2,1)} %param.5) | copy-start | bytes 393220
  5.0 0.9 %copy-start.2 = (bf16[2,1,4,8,1024]{4,3,2,1,0:T(8,128)(2,1)S(1)}, bf16[2,1,4,8,1024]{4,3,2,1,0:T(8,128)(2,1)}, u32[]{:S(2)}) copy-start(bf16[2,1,4,8,1024]{4,3,2,1,0:T(8,128)(2,1)} %param.6) | copy-start | bytes 393220
  7.8 4.1 %collective-permute-start.2 = (bf16[2,2,32,128]{3,2,1,0:T(8,128)(2,1)S(1)}, bf16[2,2,32,128]{3,2,1,0:T(8,128)(2,1)S(1)}, u32[]{:S(2)}, u32[]{:S(2)}) collective-permute-start(bf16[2,2,32,128]{3,2,1,0:T(8,128)(2,1)S(1)} %get-tuple-element.17), channel_id=1, source_target_pairs={{0,2},{1,3},{2,0},{3,1},{4,6},{5,7},{6,4},{7,5},{8,10},{9,11},{10,... | collective-permute-start | bytes 98312 | tf_op jit(solution)/shard_map/ppermute | solution.py:229
  10.1 1.3 %collective-permute-start.5 = (bf16[2,32,1024]{2,1,0:T(8,128)(2,1)S(1)}, bf16[2,32,1024]{2,1,0:T(8,128)(2,1)S(1)}, u32[]{:S(2)}, u32[]{:S(2)}) collective-permute-start(bf16[2,32,1024]{2,1,0:T(8,128)(2,1)S(1)} %collective-permute-done.4.k_x), channel_id=1, source_target_pairs={{0,1},{1,0},{2,3},{3,2},{4,5},{5,4},{6,7},{7,6},{8,9},{9,8},{10,11... | collective-permute-start | bytes 393224 | tf_op jit(solution)/shard_map/ppermute | solution.py:229
  11.9 6.8 %collective-permute-start.9 = (bf16[2,4,32,128]{3,2,1,0:T(8,128)(2,1)S(1)}, bf16[2,4,32,128]{3,2,1,0:T(8,128)(2,1)S(1)}, u32[]{:S(2)}, u32[]{:S(2)}) collective-permute-start(bf16[2,4,32,128]{3,2,1,0:T(8,128)(2,1)S(1)} %pack_rows.1.refs_0_), channel_id=1, source_target_pairs={{0,8},{4,12},{8,0},{12,4},{1,9},{5,13},{9,1},{13,5},{2,10},{6,14},... | collective-permute-start | bytes 196616 | tf_op jit(solution)/shard_map/ppermute | solution.py:312
  14.9 6.3 %collective-permute-start.11 = (bf16[2,4,32,128]{3,2,1,0:T(8,128)(2,1)S(1)}, bf16[2,4,32,128]{3,2,1,0:T(8,128)(2,1)S(1)}, u32[]{:S(2)}, u32[]{:S(2)}) collective-permute-start(bf16[2,4,32,128]{3,2,1,0:T(8,128)(2,1)S(1)} %pack_rows.1.refs_0_), channel_id=1, source_target_pairs={{0,12},{4,8},{8,4},{12,0},{1,13},{5,9},{9,5},{13,1},{2,14},{6,10},... | collective-permute-start | bytes 196616 | tf_op jit(solution)/shard_map/ppermute | solution.py:312
  16.2 5.1 %collective-permute-start.7 = (bf16[2,4,32,128]{3,2,1,0:T(8,128)(2,1)S(1)}, bf16[2,4,32,128]{3,2,1,0:T(8,128)(2,1)S(1)}, u32[]{:S(2)}, u32[]{:S(2)}) collective-permute-start(bf16[2,4,32,128]{3,2,1,0:T(8,128)(2,1)S(1)} %pack_rows.1.refs_0_), channel_id=1, source_target_pairs={{0,4},{4,0},{8,12},{12,8},{1,5},{5,1},{9,13},{13,9},{2,6},{6,2},{1... | collective-permute-start | bytes 196616 | tf_op jit(solution)/shard_map/ppermute | solution.py:312
  16.5 5.5 %collective-permute-start.6 = (bf16[2,4,32,128]{3,2,1,0:T(8,128)(2,1)S(1)}, bf16[2,4,32,128]{3,2,1,0:T(8,128)(2,1)S(1)}, u32[]{:S(2)}, u32[]{:S(2)}) collective-permute-start(bf16[2,4,32,128]{3,2,1,0:T(8,128)(2,1)S(1)} %pack_rows.1.refs_0_), channel_id=1, source_target_pairs={{0,1},{1,0},{2,3},{3,2},{4,5},{5,4},{6,7},{7,6},{8,9},{9,8},{10,11... | collective-permute-start | bytes 196616 | tf_op jit(solution)/shard_map/ppermute | solution.py:229
  18.7 3.2 %collective-permute-start.10 = (bf16[2,4,32,128]{3,2,1,0:T(8,128)(2,1)S(1)}, bf16[2,4,32,128]{3,2,1,0:T(8,128)(2,1)S(1)}, u32[]{:S(2)}, u32[]{:S(2)}) collective-permute-start(bf16[2,4,32,128]{3,2,1,0:T(8,128)(2,1)S(1)} %collective-permute-done.9.refs_4_), channel_id=1, source_target_pairs={{0,1},{1,0},{2,3},{3,2},{4,5},{5,4},{6,7},{7,6},{8,9},{9,8},{10,11... | collective-permute-start | bytes 196616 | tf_op jit(solution)/shard_map/ppermute | solution.py:229
  21.2 1.3 %collective-permute-start.12 = (bf16[2,4,32,128]{3,2,1,0:T(8,128)(2,1)S(1)}, bf16[2,4,32,128]{3,2,1,0:T(8,128)(2,1)S(1)}, u32[]{:S(2)}, u32[]{:S(2)}) collective-permute-start(bf16[2,4,32,128]{3,2,1,0:T(8,128)(2,1)S(1)} %collective-permute-done.11.refs_6_), channel_id=1, source_target_pairs={{0,1},{1,0},{2,3},{3,2},{4,5},{5,4},{6,7},{7,6},{8,9},{9,8},{10,11... | collective-permute-start | bytes 196616 | tf_op jit(solution)/shard_map/ppermute | solution.py:229
  21.3 1.3 %collective-permute-start.8 = (bf16[2,4,32,128]{3,2,1,0:T(8,128)(2,1)S(1)}, bf16[2,4,32,128]{3,2,1,0:T(8,128)(2,1)S(1)}, u32[]{:S(2)}, u32[]{:S(2)}) collective-permute-start(bf16[2,4,32,128]{3,2,1,0:T(8,128)(2,1)S(1)} %collective-permute-done.7.refs_2_), channel_id=1, source_target_pairs={{0,1},{1,0},{2,3},{3,2},{4,5},{5,4},{6,7},{7,6},{8,9},{9,8},{10,11... | collective-permute-start | bytes 196616 | tf_op jit(solution)/shard_map/ppermute | solution.py:229

commit v4 on v3

--- a/solution.py
+++ b/solution.py
@@ -11,6 +11,7 @@
 F32 = jnp.float32
 BF16 = jnp.bfloat16
 SMALL_GATHER = 4 << 20
+ROUNDS = ((0, 1, 2, 3), (2, 0, 3, 1), (1, 3, 0, 2), (3, 2, 1, 0))
 
 
 def complex_dot(a_real, a_imag, b_real, b_imag):
@@ -172,6 +173,13 @@
     folded[:, full:] = wide[1].astype(BF16)
 
 
+def sender(targets, cluster):
+    source = jnp.int32(0)
+    for at, target in enumerate(targets):
+        source = jnp.where(cluster == target, at, source)
+    return source
+
+
 def chain_kernel(clusters, quarter, *refs):
     pieces, folded, field = refs[: 2 * clusters], refs[2 * clusters], refs[2 * clusters + 1]
     between, skeleton, kept = refs[2 * clusters + 2 :]
@@ -179,7 +187,7 @@
     block = clusters * quarter
     full = 4 * block
     for j in range(clusters):
-        source = cluster ^ j
+        source = sender(ROUNDS[j], cluster)
         for core in range(2):
             ref = pieces[2 * j + core]
             for at in range(2):
@@ -201,15 +209,36 @@
         ]
         return jnp.concatenate(rows, axis=0)
 
-    for step in range(STEPS - 1):
-        for target in range(clusters):
-            value = gather(target)
-            kept[target, :full, :] = value.astype(BF16)
-            kept[target, full:, :full] = (-value[:, full:]).astype(BF16)
-            kept[target, full:, full:] = value[:, :full].astype(BF16)
+    def embed(target, value):
+        kept[target, :full, :] = value.astype(BF16)
+        kept[target, full:, :full] = (-value[:, full:]).astype(BF16)
+        kept[target, full:, full:] = value[:, :full].astype(BF16)
+
+    def own_target(source):
+        blocks = []
+        for q in range(4):
+            rows = between[source, q * block : (q + 1) * block, :].astype(F32)
+            chosen = rows[:quarter]
+            for target in range(1, clusters):
+                other = rows[target * quarter : (target + 1) * quarter]
+                chosen = jnp.where(cluster == target, other, chosen)
+            blocks.append(chosen)
+        return jnp.concatenate(blocks, axis=0).astype(BF16)
+
+    for target in range(clusters):
+        embed(target, gather(target))
+    for step in range(STEPS - 2):
         for source in range(clusters):
             skeleton[source] = jnp.dot(between[source], kept[source], preferred_element_type=F32)
-    value = gather(cluster)
+        for target in range(clusters):
+            embed(target, gather(target))
+    wanted = [
+        jnp.dot(own_target(source), kept[source], preferred_element_type=F32)
+        for source in range(clusters)
+    ]
+    value = jnp.concatenate(
+        [wanted[s][q * quarter : (q + 1) * quarter] for q in range(4) for s in range(clusters)], axis=0
+    )
     last = jnp.concatenate([value[:, :full], value[:, full:]], axis=0).astype(BF16)
     field[...] = jnp.dot(folded[...], last, preferred_element_type=F32).astype(BF16)
 
@@ -309,7 +338,7 @@
     )(k_own, k_x, k_core, k_diag)
     held = {0: packed}
     for j in range(1, clusters):
-        held[j] = lax.ppermute(packed, "clus", [(i, i ^ j) for i in range(clusters)])
+        held[j] = lax.ppermute(packed, "clus", list(enumerate(ROUNDS[j])))
     pieces = []
     for j in range(clusters):
         pieces += [held[j], to_core(held[j])]
@@ -338,7 +367,7 @@
     fits = (
         rows == 4
         and clusters == lax.axis_size("clus")
-        and clusters & (clusters - 1) == 0
+        and clusters == len(ROUNDS)
         and quarter == 8
         and angles == full == 128
         and share * rows == leaf

time: 24.2 us -> 23.9 us (0.988)
  waiting for transfers between devices: 7.32 us -> 5.26 us
  starting transfers between devices: 10.2 us -> 11.9 us
    ppermute x3, waiting for transfers between devices: 4.85 us -> 2.63 us  [gather_body(): held[j] = lax.ppermute(packed, 'clus', list(enumerate(ROUNDS[j])))]
    ppermute x3, starting transfers between devices: 4.56 us -> 6 us  [gather_body(): held[j] = lax.ppermute(packed, 'clus', list(enumerate(ROUNDS[j])))]
    ppermute x10, starting transfers between devices: 5.65 us -> 5.93 us  [across(): return lambda v: lax.ppermute(v, 'rows', [(i, i ^ flip) for i in range(4)])]
  transfers between devices with their start and end apart: 13 -> 13, of which waited for: 8 -> 7; matrix products, arithmetic and copies ran while one was open for 0% -> 0% of each run, Pallas kernels for 10% -> 10%
where the time goes in v4:
time: 23.9 us; the launch traced here: 23.7 us
  starting transfers between devices  11.9 us (50%)
  waiting for transfers between devices  5.26 us (22%)
  Pallas kernels  3.73 us (16%)
  local copies, waits for them, and re-layouts  2.72 us (11%)
    ppermute x3, starting transfers between devices, gather_body(): held[j] = lax.ppermute(packed, 'clus', list(enumerate(ROUNDS[j])))  6 us
    ppermute x10, starting transfers between devices, across(): return lambda v: lax.ppermute(v, 'rows', [(i, i ^ flip) for i in range(4)])  5.93 us
    unnamed x8, local copies, waits for them, and re-layouts  2.72 us
    ppermute x3, waiting for transfers between devices, gather_body(): held[j] = lax.ppermute(packed, 'clus', list(enumerate(ROUNDS[j])))  2.63 us
    ppermute x10, waiting for transfers between devices, across(): return lambda v: lax.ppermute(v, 'rows', [(i, i ^ flip) for i in range(4)])  2.63 us
    pallas_call x1, Pallas kernels, gather_body(): pl.pallas_call(functools.partial(chain_kernel, clusters, quarter), out_sh...  1.41 us
    pallas_call x1, Pallas kernels, gather_body(): pl.pallas_call(functools.partial(load_kernel, share, angles, quarter), ou...  1.21 us
  transfers between devices with their start and end apart: 13, of which 7 were waited for; matrix products, arithmetic and copies ran while one was open for 0% of the time, Pallas kernels for 10%

profile of v4, /device:TPU:0, one launch (start us, length us, event | category | flops | bytes accessed | tf_op | source)
XLA Modules:
  0.0 23.7 jit_solution(7586678038533449674)
XLA Ops:
  0.0 0.5 %collective-permute-start = (bf16[512,128]{1,0:T(8,128)(2,1)}, bf16[512,128]{1,0:T(8,128)(2,1)S(1)}, u32[]{:S(2)}, u32[]{:S(2)}) collective-permute-start(bf16[512,128]{1,0:T(8,128)(2,1)} %bitcast.4), channel_id=1, source_target_pairs={{0,1},{1,0},{2,3},{3,2},{4,5},{5,4},{6,7},{7,6},{8,9},{9,8},{10,11... | collective-permute-start | bytes 393224 | tf_op jit(solution)/shard_map/ppermute | solution.py:258
  0.5 2.5 %collective-permute-start.1 = (bf16[2,32,1024]{2,1,0:T(8,128)(2,1)}, bf16[2,32,1024]{2,1,0:T(8,128)(2,1)S(1)}, u32[]{:S(2)}, u32[]{:S(2)}) collective-permute-start(bf16[2,32,1024]{2,1,0:T(8,128)(2,1)} %bitcast.6), channel_id=1, source_target_pairs={{0,2},{1,3},{2,0},{3,1},{4,6},{5,7},{6,4},{7,5},{8,10},{9,11},{10,... | collective-permute-start | bytes 393224 | tf_op jit(solution)/shard_map/ppermute | solution.py:258
  3.2 0.9 %copy-done = bf16[256,2,128]{2,1,0:T(2,128)(2,1)S(1)} copy-done((bf16[256,2,128]{2,1,0:T(2,128)(2,1)S(1)}, bf16[256,2,128]{2,1,0:T(2,128)(2,1)}, u32[]{:S(2)}) %copy-start) | copy-done | bytes 131096
  4.1 0.9 %copy-done.1 = bf16[2,1,4,8,1024]{4,3,2,1,0:T(8,128)(2,1)S(1)} copy-done((bf16[2,1,4,8,1024]{4,3,2,1,0:T(8,128)(2,1)S(1)}, bf16[2,1,4,8,1024]{4,3,2,1,0:T(8,128)(2,1)}, u32[]{:S(2)}) %copy-start.1) | copy-done | bytes 131096
  5.0 0.9 %copy-done.2 = bf16[2,1,4,8,1024]{4,3,2,1,0:T(8,128)(2,1)S(1)} copy-done((bf16[2,1,4,8,1024]{4,3,2,1,0:T(8,128)(2,1)S(1)}, bf16[2,1,4,8,1024]{4,3,2,1,0:T(8,128)(2,1)}, u32[]{:S(2)}) %copy-start.2) | copy-done | bytes 131096
  5.9 1.2 %load_own.1 = (bf16[2,32,1024]{2,1,0:T(8,128)(2,1)S(1)}, bf16[2,32,1024]{2,1,0:T(8,128)(2,1)S(1)}, bf16[256,256]{1,0:T(8,128)(2,1)S(1)}, bf16[256,256]{1,0:T(8,128)(2,1)S(1)}, f32[4,32,128]{2,1,0:T(8,128)S(1)}) custom-call(s32[4,4]{1,0:T(4,128)S(1)} %copy-done.3, bf16[2,32,1024]{2,1,0:T(8,128)(2,1)S(1)} %bitcast.7, bf16[2,32,1024]{2,1,0:T(8,128)(2,1)S(1)} %bitcast.10, ...), custom_call_target="tpu_custom_call" | custom-call | tf_op jit(solution)/shard_map/load_own/pallas_call | solution.py:267
  7.1 0.4 %collective-permute-done.1.l_x = bf16[2,32,1024]{2,1,0:T(8,128)(2,1)S(1)} collective-permute-done((bf16[2,32,1024]{2,1,0:T(8,128)(2,1)}, bf16[2,32,1024]{2,1,0:T(8,128)(2,1)S(1)}, u32[]{:S(2)}, u32[]{:S(2)}) %collective-permute-start.1) | collective-permute-done | bytes 131104 | tf_op jit(solution)/shard_map/ppermute | solution.py:258
  7.6 0.2 side_skeleton.1
  7.8 2.0 %collective-permute-start.2 = (bf16[2,2,32,128]{3,2,1,0:T(8,128)(2,1)S(1)}, bf16[2,2,32,128]{3,2,1,0:T(8,128)(2,1)S(1)}, u32[]{:S(2)}, u32[]{:S(2)}) collective-permute-start(bf16[2,2,32,128]{3,2,1,0:T(8,128)(2,1)S(1)} %get-tuple-element.17), channel_id=1, source_target_pairs={{0,2},{1,3},{2,0},{3,1},{4,6},{5,7},{6,4},{7,5},{8,10},{9,11},{10,... | collective-permute-start | bytes 98312 | tf_op jit(solution)/shard_map/ppermute | solution.py:258
  9.8 0.3 %collective-permute-done.4.k_x = bf16[2,32,1024]{2,1,0:T(8,128)(2,1)S(1)} collective-permute-done((bf16[2,32,1024]{2,1,0:T(8,128)(2,1)}, bf16[2,32,1024]{2,1,0:T(8,128)(2,1)S(1)}, u32[]{:S(2)}, u32[]{:S(2)}) %collective-permute-start.4) | collective-permute-done | bytes 131104 | tf_op jit(solution)/shard_map/ppermute | solution.py:258
  10.1 0.4 %near_columns.1.near = f32[2,64,64]{2,1,0:T(8,128)S(1)} custom-call(bf16[128,1024]{1,0:T(8,128)(2,1)S(1)} %get-tuple-element.19.l_all, bf16[2,32,1024]{2,1,0:T(8,128)(2,1)S(1)} %get-tuple-element.20.k_own, bf16[2,32,1024]{2,1,0:T(8,128)(2,1)S(1)} %collective-permute-done.3.k_core), custom_call_target="tpu_custom_call" | custom-call | flops 21474836480 | bytes 16777216 | tf_op jit(solution)/shard_map/near_columns/pallas_call | solution.py:302
  10.5 1.0 %collective-permute-done.5.k_diag = bf16[2,32,1024]{2,1,0:T(8,128)(2,1)S(1)} collective-permute-done((bf16[2,32,1024]{2,1,0:T(8,128)(2,1)S(1)}, bf16[2,32,1024]{2,1,0:T(8,128)(2,1)S(1)}, u32[]{:S(2)}, u32[]{:S(2)}) %collective-permute-start.5) | collective-permute-done | bytes 131104 | tf_op jit(solution)/shard_map/ppermute | solution.py:258
  11.5 0.4 %far_columns.1.between = bf16[2,2,32,128]{3,2,1,0:T(8,128)(2,1)S(1)} custom-call(f32[2,64,64]{2,1,0:T(8,128)S(1)} %near_columns.1.near, f32[4,32,128]{2,1,0:T(8,128)S(1)} %get-tuple-element.18.keep, bf16[128,1024]{1,0:T(8,128)(2,1)S(1)} %get-tuple-element.19.l_all, bf16[2,32,1024]{2,1,0:T(8,128)(2,1)S(1)} %collective-permute-done.4.k_x, ...), custom_call_target="tpu_custom_call" | custom-call | tf_op jit(solution)/shard_map/far_columns/pallas_call | solution.py:313
  11.9 2.0 %collective-permute-start.9 = (bf16[2,4,32,128]{3,2,1,0:T(8,128)(2,1)S(1)}, bf16[2,4,32,128]{3,2,1,0:T(8,128)(2,1)S(1)}, u32[]{:S(2)}, u32[]{:S(2)}) collective-permute-start(bf16[2,4,32,128]{3,2,1,0:T(8,128)(2,1)S(1)} %pack_rows.1.refs_0_), channel_id=1, source_target_pairs={{0,4},{4,12},{8,0},{12,8},{1,5},{5,13},{9,1},{13,9},{2,6},{6,14},{... | collective-permute-start | bytes 196616 | tf_op jit(solution)/shard_map/ppermute | solution.py:341
  13.9 2.5 %collective-permute-start.11 = (bf16[2,4,32,128]{3,2,1,0:T(8,128)(2,1)S(1)}, bf16[2,4,32,128]{3,2,1,0:T(8,128)(2,1)S(1)}, u32[]{:S(2)}, u32[]{:S(2)}) collective-permute-start(bf16[2,4,32,128]{3,2,1,0:T(8,128)(2,1)S(1)} %pack_rows.1.refs_0_), channel_id=1, source_target_pairs={{0,12},{4,8},{8,4},{12,0},{1,13},{5,9},{9,5},{13,1},{2,14},{6,10},... | collective-permute-start | bytes 196616 | tf_op jit(solution)/shard_map/ppermute | solution.py:341
  16.3 1.6 %collective-permute-start.7 = (bf16[2,4,32,128]{3,2,1,0:T(8,128)(2,1)S(1)}, bf16[2,4,32,128]{3,2,1,0:T(8,128)(2,1)S(1)}, u32[]{:S(2)}, u32[]{:S(2)}) collective-permute-start(bf16[2,4,32,128]{3,2,1,0:T(8,128)(2,1)S(1)} %pack_rows.1.refs_0_), channel_id=1, source_target_pairs={{0,8},{4,0},{8,12},{12,4},{1,9},{5,1},{9,13},{13,5},{2,10},{6,2},{... | collective-permute-start | bytes 196616 | tf_op jit(solution)/shard_map/ppermute | solution.py:341
  17.9 0.5 %collective-permute-start.10 = (bf16[2,4,32,128]{3,2,1,0:T(8,128)(2,1)S(1)}, bf16[2,4,32,128]{3,2,1,0:T(8,128)(2,1)S(1)}, u32[]{:S(2)}, u32[]{:S(2)}) collective-permute-start(bf16[2,4,32,128]{3,2,1,0:T(8,128)(2,1)S(1)} %collective-permute-done.9.refs_4_), channel_id=1, source_target_pairs={{0,1},{1,0},{2,3},{3,2},{4,5},{5,4},{6,7},{7,6},{8,9},{9,8},{10,11... | collective-permute-start | bytes 196616 | tf_op jit(solution)/shard_map/ppermute | solution.py:258
  18.4 2.3 %collective-permute-done.11.refs_6_ = bf16[2,4,32,128]{3,2,1,0:T(8,128)(2,1)S(1)} collective-permute-done((bf16[2,4,32,128]{3,2,1,0:T(8,128)(2,1)S(1)}, bf16[2,4,32,128]{3,2,1,0:T(8,128)(2,1)S(1)}, u32[]{:S(2)}, u32[]{:S(2)}) %collective-permute-start.11) | collective-permute-done | bytes 65568 | tf_op jit(solution)/shard_map/ppermute | solution.py:341
  20.7 0.3 %collective-permute-done.7.refs_2_ = bf16[2,4,32,128]{3,2,1,0:T(8,128)(2,1)S(1)} collective-permute-done((bf16[2,4,32,128]{3,2,1,0:T(8,128)(2,1)S(1)}, bf16[2,4,32,128]{3,2,1,0:T(8,128)(2,1)S(1)}, u32[]{:S(2)}, u32[]{:S(2)}) %collective-permute-start.7) | collective-permute-done | bytes 65568 | tf_op jit(solution)/shard_map/ppermute | solution.py:341
  21.1 0.2 collective-permute-start.8
  21.2 0.2 fold_coupling.1.refs_8_
  21.4 0.5 %collective-permute-done.12.refs_7_ = bf16[2,4,32,128]{3,2,1,0:T(8,128)(2,1)S(1)} collective-permute-done((bf16[2,4,32,128]{3,2,1,0:T(8,128)(2,1)S(1)}, bf16[2,4,32,128]{3,2,1,0:T(8,128)(2,1)S(1)}, u32[]{:S(2)}, u32[]{:S(2)}) %collective-permute-start.12) | collective-permute-done | bytes 65568 | tf_op jit(solution)/shard_map/ppermute | solution.py:258
  22.0 0.3 %collective-permute-done.8.refs_3_ = bf16[2,4,32,128]{3,2,1,0:T(8,128)(2,1)S(1)} collective-permute-done((bf16[2,4,32,128]{3,2,1,0:T(8,128)(2,1)S(1)}, bf16[2,4,32,128]{3,2,1,0:T(8,128)(2,1)S(1)}, u32[]{:S(2)}, u32[]{:S(2)}) %collective-permute-start.8) | collective-permute-done | bytes 65568 | tf_op jit(solution)/shard_map/ppermute | solution.py:258
  22.3 1.4 %skeleton_chain.1 = bf16[512,128]{1,0:T(8,128)(2,1)} custom-call(bf16[2,4,32,128]{3,2,1,0:T(8,128)(2,1)S(1)} %pack_rows.1.refs_0_, bf16[2,4,32,128]{3,2,1,0:T(8,128)(2,1)S(1)} %collective-permute-done.6.refs_1_, bf16[2,4,32,128]{3,2,1,0:T(8,128)(2,1)S(1)} %collective-permute-done.7.refs_2_, bf16[2,4,32,128]{3,2,1,0:T(8,128)(2,1)S(1)} %collective-permute-done.8.refs_3_, ...), custom_call_target="tpu_custom_call" | custom-call | tf_op jit(solution)/shard_map/skeleton_chain/pallas_call | solution.py:345
  (17 shorter events, 0.2 us)
Async XLA Ops:
  0.0 3.2 %copy-start.3 = (s32[4,4]{1,0:T(4,128)S(1)}, s32[4,4]{1,0:T(4,128)}, u32[]{:S(2)}) copy-start(s32[4,4]{1,0:T(4,128)} %ranks.1) | copy-start | bytes 196
  0.0 3.2 %collective-permute-start = (bf16[512,128]{1,0:T(8,128)(2,1)}, bf16[512,128]{1,0:T(8,128)(2,1)S(1)}, u32[]{:S(2)}, u32[]{:S(2)}) collective-permute-start(bf16[512,128]{1,0:T(8,128)(2,1)} %bitcast.4), channel_id=1, source_target_pairs={{0,1},{1,0},{2,3},{3,2},{4,5},{5,4},{6,7},{7,6},{8,9},{9,8},{10,11... | collective-permute-start | bytes 393224 | tf_op jit(solution)/shard_map/ppermute | solution.py:258
  0.5 7.1 %collective-permute-start.1 = (bf16[2,32,1024]{2,1,0:T(8,128)(2,1)}, bf16[2,32,1024]{2,1,0:T(8,128)(2,1)S(1)}, u32[]{:S(2)}, u32[]{:S(2)}) collective-permute-start(bf16[2,32,1024]{2,1,0:T(8,128)(2,1)} %bitcast.6), channel_id=1, source_target_pairs={{0,2},{1,3},{2,0},{3,1},{4,6},{5,7},{6,4},{7,5},{8,10},{9,11},{10,... | collective-permute-start | bytes 393224 | tf_op jit(solution)/shard_map/ppermute | solution.py:258
  3.0 7.1 %collective-permute-start.4 = (bf16[2,32,1024]{2,1,0:T(8,128)(2,1)}, bf16[2,32,1024]{2,1,0:T(8,128)(2,1)S(1)}, u32[]{:S(2)}, u32[]{:S(2)}) collective-permute-start(bf16[2,32,1024]{2,1,0:T(8,128)(2,1)} %bitcast.8), channel_id=1, source_target_pairs={{0,2},{1,3},{2,0},{3,1},{4,6},{5,7},{6,4},{7,5},{8,10},{9,11},{10,... | collective-permute-start | bytes 393224 | tf_op jit(solution)/shard_map/ppermute | solution.py:258
  3.1 7.0 %collective-permute-start.3 = (bf16[2,32,1024]{2,1,0:T(8,128)(2,1)}, bf16[2,32,1024]{2,1,0:T(8,128)(2,1)S(1)}, u32[]{:S(2)}, u32[]{:S(2)}) collective-permute-start(bf16[2,32,1024]{2,1,0:T(8,128)(2,1)} %bitcast.9), channel_id=1, source_target_pairs={{0,1},{1,0},{2,3},{3,2},{4,5},{5,4},{6,7},{7,6},{8,9},{9,8},{10,11... | collective-permute-start | bytes 393224 | tf_op jit(solution)/shard_map/ppermute | solution.py:258
  3.2 0.9 %copy-start = (bf16[256,2,128]{2,1,0:T(2,128)(2,1)S(1)}, bf16[256,2,128]{2,1,0:T(2,128)(2,1)}, u32[]{:S(2)}) copy-start(bf16[256,2,128]{2,1,0:T(2,128)(2,1)} %param.4) | copy-start | bytes 393220
  4.1 0.9 %copy-start.1 = (bf16[2,1,4,8,1024]{4,3,2,1,0:T(8,128)(2,1)S(1)}, bf16[2,1,4,8,1024]{4,3,2,1,0:T(8,128)(2,1)}, u32[]{:S(2)}) copy-start(bf16[2,1,4,8,1024]{4,3,2,1,0:T(8,128)(2,1)} %param.5) | copy-start | bytes 393220
  5.0 0.9 %copy-start.2 = (bf16[2,1,4,8,1024]{4,3,2,1,0:T(8,128)(2,1)S(1)}, bf16[2,1,4,8,1024]{4,3,2,1,0:T(8,128)(2,1)}, u32[]{:S(2)}) copy-start(bf16[2,1,4,8,1024]{4,3,2,1,0:T(8,128)(2,1)} %param.6) | copy-start | bytes 393220
  7.8 4.1 %collective-permute-start.2 = (bf16[2,2,32,128]{3,2,1,0:T(8,128)(2,1)S(1)}, bf16[2,2,32,128]{3,2,1,0:T(8,128)(2,1)S(1)}, u32[]{:S(2)}, u32[]{:S(2)}) collective-permute-start(bf16[2,2,32,128]{3,2,1,0:T(8,128)(2,1)S(1)} %get-tuple-element.17), channel_id=1, source_target_pairs={{0,2},{1,3},{2,0},{3,1},{4,6},{5,7},{6,4},{7,5},{8,10},{9,11},{10,... | collective-permute-start | bytes 98312 | tf_op jit(solution)/shard_map/ppermute | solution.py:258
  10.1 1.3 %collective-permute-start.5 = (bf16[2,32,1024]{2,1,0:T(8,128)(2,1)S(1)}, bf16[2,32,1024]{2,1,0:T(8,128)(2,1)S(1)}, u32[]{:S(2)}, u32[]{:S(2)}) collective-permute-start(bf16[2,32,1024]{2,1,0:T(8,128)(2,1)S(1)} %collective-permute-done.4.k_x), channel_id=1, source_target_pairs={{0,1},{1,0},{2,3},{3,2},{4,5},{5,4},{6,7},{7,6},{8,9},{9,8},{10,11... | collective-permute-start | bytes 393224 | tf_op jit(solution)/shard_map/ppermute | solution.py:258
  11.9 6.0 %collective-permute-start.9 = (bf16[2,4,32,128]{3,2,1,0:T(8,128)(2,1)S(1)}, bf16[2,4,32,128]{3,2,1,0:T(8,128)(2,1)S(1)}, u32[]{:S(2)}, u32[]{:S(2)}) collective-permute-start(bf16[2,4,32,128]{3,2,1,0:T(8,128)(2,1)S(1)} %pack_rows.1.refs_0_), channel_id=1, source_target_pairs={{0,4},{4,12},{8,0},{12,8},{1,5},{5,13},{9,1},{13,9},{2,6},{6,14},{... | collective-permute-start | bytes 196616 | tf_op jit(solution)/shard_map/ppermute | solution.py:341
  13.9 6.9 %collective-permute-start.11 = (bf16[2,4,32,128]{3,2,1,0:T(8,128)(2,1)S(1)}, bf16[2,4,32,128]{3,2,1,0:T(8,128)(2,1)S(1)}, u32[]{:S(2)}, u32[]{:S(2)}) collective-permute-start(bf16[2,4,32,128]{3,2,1,0:T(8,128)(2,1)S(1)} %pack_rows.1.refs_0_), channel_id=1, source_target_pairs={{0,12},{4,8},{8,4},{12,0},{1,13},{5,9},{9,5},{13,1},{2,14},{6,10},... | collective-permute-start | bytes 196616 | tf_op jit(solution)/shard_map/ppermute | solution.py:341
  16.3 4.7 %collective-permute-start.7 = (bf16[2,4,32,128]{3,2,1,0:T(8,128)(2,1)S(1)}, bf16[2,4,32,128]{3,2,1,0:T(8,128)(2,1)S(1)}, u32[]{:S(2)}, u32[]{:S(2)}) collective-permute-start(bf16[2,4,32,128]{3,2,1,0:T(8,128)(2,1)S(1)} %pack_rows.1.refs_0_), channel_id=1, source_target_pairs={{0,8},{4,0},{8,12},{12,4},{1,9},{5,1},{9,13},{13,5},{2,10},{6,2},{... | collective-permute-start | bytes 196616 | tf_op jit(solution)/shard_map/ppermute | solution.py:341
  17.9 3.5 %collective-permute-start.6 = (bf16[2,4,32,128]{3,2,1,0:T(8,128)(2,1)S(1)}, bf16[2,4,32,128]{3,2,1,0:T(8,128)(2,1)S(1)}, u32[]{:S(2)}, u32[]{:S(2)}) collective-permute-start(bf16[2,4,32,128]{3,2,1,0:T(8,128)(2,1)S(1)} %pack_rows.1.refs_0_), channel_id=1, source_target_pairs={{0,1},{1,0},{2,3},{3,2},{4,5},{5,4},{6,7},{7,6},{8,9},{9,8},{10,11... | collective-permute-start | bytes 196616 | tf_op jit(solution)/shard_map/ppermute | solution.py:258
  17.9 3.5 %collective-permute-start.10 = (bf16[2,4,32,128]{3,2,1,0:T(8,128)(2,1)S(1)}, bf16[2,4,32,128]{3,2,1,0:T(8,128)(2,1)S(1)}, u32[]{:S(2)}, u32[]{:S(2)}) collective-permute-start(bf16[2,4,32,128]{3,2,1,0:T(8,128)(2,1)S(1)} %collective-permute-done.9.refs_4_), channel_id=1, source_target_pairs={{0,1},{1,0},{2,3},{3,2},{4,5},{5,4},{6,7},{7,6},{8,9},{9,8},{10,11... | collective-permute-start | bytes 196616 | tf_op jit(solution)/shard_map/ppermute | solution.py:258
  20.7 1.3 %collective-permute-start.12 = (bf16[2,4,32,128]{3,2,1,0:T(8,128)(2,1)S(1)}, bf16[2,4,32,128]{3,2,1,0:T(8,128)(2,1)S(1)}, u32[]{:S(2)}, u32[]{:S(2)}) collective-permute-start(bf16[2,4,32,128]{3,2,1,0:T(8,128)(2,1)S(1)} %collective-permute-done.11.refs_6_), channel_id=1, source_target_pairs={{0,1},{1,0},{2,3},{3,2},{4,5},{5,4},{6,7},{7,6},{8,9},{9,8},{10,11... | collective-permute-start | bytes 196616 | tf_op jit(solution)/shard_map/ppermute | solution.py:258
  21.1 1.3 %collective-permute-start.8 = (bf16[2,4,32,128]{3,2,1,0:T(8,128)(2,1)S(1)}, bf16[2,4,32,128]{3,2,1,0:T(8,128)(2,1)S(1)}, u32[]{:S(2)}, u32[]{:S(2)}) collective-permute-start(bf16[2,4,32,128]{3,2,1,0:T(8,128)(2,1)S(1)} %collective-permute-done.7.refs_2_), channel_id=1, source_target_pairs={{0,1},{1,0},{2,3},{3,2},{4,5},{5,4},{6,7},{7,6},{8,9},{9,8},{10,11... | collective-permute-start | bytes 196616 | tf_op jit(solution)/shard_map/ppermute | solution.py:258

commit v5 on v4

--- a/solution.py
+++ b/solution.py
@@ -11,7 +11,10 @@
 F32 = jnp.float32
 BF16 = jnp.bfloat16
 SMALL_GATHER = 4 << 20
-ROUNDS = ((0, 1, 2, 3), (2, 0, 3, 1), (1, 3, 0, 2), (3, 2, 1, 0))
+ROUNDS = (
+    ((0, 1, 2, 3), (2, 0, 3, 1), (1, 3, 0, 2), (3, 2, 1, 0)),
+    ((0, 1, 2, 3), (3, 0, 1, 2), (1, 2, 3, 0), (2, 3, 0, 1)),
+)
 
 
 def complex_dot(a_real, a_imag, b_real, b_imag):
@@ -75,12 +78,12 @@
 
 
 def load_kernel(
-    share, angles, quarter, ranks, l_hbm, k_hbm, x_hbm, x_near,
-    l_own, k_own, x_own, x_core, keep, x_flat, x_wide, sems,
+    share, angles, quarter, ranks, l_hbm, x_hbm, x_near,
+    l_own, x_own, x_core, keep, x_flat, x_wide, sems,
 ):
     copies = [
         pltpu.make_async_copy(source, target, sems.at[i])
-        for i, (source, target) in enumerate(((x_hbm, x_flat), (l_hbm, l_own), (k_hbm, k_own)))
+        for i, (source, target) in enumerate(((x_hbm, x_flat), (l_hbm, l_own)))
     ]
     for copy in copies:
         copy.start()
@@ -100,7 +103,6 @@
                 pl.ds(part, share, stride=2), :
             ].astype(BF16)
     copies[1].wait()
-    copies[2].wait()
 
 
 def side_kernel(share, angles, l_own, l_x, x_own, x_core, partial, kept_partial, l_all):
@@ -183,12 +185,14 @@
 def chain_kernel(clusters, quarter, *refs):
     pieces, folded, field = refs[: 2 * clusters], refs[2 * clusters], refs[2 * clusters + 1]
     between, skeleton, kept = refs[2 * clusters + 2 :]
+    row = lax.axis_index("rows")
     cluster = lax.axis_index("clus")
     block = clusters * quarter
     full = 4 * block
     for j in range(clusters):
-        source = sender(ROUNDS[j], cluster)
+        senders = [sender(rounds[j], cluster) for rounds in ROUNDS]
         for core in range(2):
+            source = jnp.where(row % 2 == core, senders[0], senders[1])
             ref = pieces[2 * j + core]
             for at in range(2):
                 first = (2 * core + at) * block
@@ -260,31 +264,32 @@
     to_x, to_core = across(2), across(1)
     factor = leaf_factor.reshape(2, block, leaf)
     weights = coupling.reshape(2, block, leaf)
-    l_x, k_x = to_x(factor), to_x(weights)
+    l_x = to_x(factor)
     current = excitation.reshape(2 * share, angles)
     x_near = to_core(current)
+    to_send, _ = lax.optimization_barrier((weights, x_near))
+    k_x = to_x(to_send)
     k_core = to_core(weights)
-    l_own, k_own, x_own, x_core, keep = pl.pallas_call(
+    l_own, x_own, x_core, keep = pl.pallas_call(
         functools.partial(load_kernel, share, angles, quarter),
         out_shape=(
             jax.ShapeDtypeStruct(factor.shape, BF16),
-            jax.ShapeDtypeStruct(weights.shape, BF16),
             jax.ShapeDtypeStruct((share, 2 * angles), BF16),
             jax.ShapeDtypeStruct((share, 2 * angles), BF16),
             jax.ShapeDtypeStruct((4, block, angles), F32),
         ),
         in_specs=[pl.BlockSpec(memory_space=pltpu.SMEM)]
-        + [pl.BlockSpec(memory_space=pl.ANY)] * 3
+        + [pl.BlockSpec(memory_space=pl.ANY)] * 2
         + in_vmem(1),
-        out_specs=tuple(in_vmem(5)),
+        out_specs=tuple(in_vmem(4)),
         scratch_shapes=[
             pltpu.VMEM((2 * share, angles), BF16),
             pltpu.VMEM((2 * share, angles), F32),
-            pltpu.SemaphoreType.DMA((3,)),
+            pltpu.SemaphoreType.DMA((2,)),
         ],
         compiler_params=params,
         name="load_own",
-    )(ranks, factor, weights, current, x_near)
+    )(ranks, factor, current, x_near)
     partial, kept_partial, l_all = pl.pallas_call(
         functools.partial(side_kernel, share, angles),
         out_shape=(
@@ -308,7 +313,7 @@
         compiler_params=params,
         cost_estimate=pl.CostEstimate(flops=20 << 30, bytes_accessed=16 << 20, transcendentals=0),
         name="near_columns",
-    )(l_all, k_own, k_core)
+    )(l_all, weights, k_core)
     k_diag = to_core(k_x)
     between = pl.pallas_call(
         far_kernel,
@@ -335,10 +340,13 @@
         scratch_shapes=[pltpu.VMEM((2, 2 * share, full), F32)],
         compiler_params=params,
         name="fold_coupling",
-    )(k_own, k_x, k_core, k_diag)
+    )(weights, k_x, k_core, k_diag)
     held = {0: packed}
     for j in range(1, clusters):
-        held[j] = lax.ppermute(packed, "clus", list(enumerate(ROUNDS[j])))
+        pairs = [
+            (4 * i + row, 4 * ROUNDS[row % 2][j][i] + row) for i in range(clusters) for row in range(4)
+        ]
+        held[j] = lax.ppermute(packed, ("clus", "rows"), pairs)
     pieces = []
     for j in range(clusters):
         pieces += [held[j], to_core(held[j])]
@@ -367,7 +375,7 @@
     fits = (
         rows == 4
         and clusters == lax.axis_size("clus")
-        and clusters == len(ROUNDS)
+        and clusters == len(ROUNDS[0])
         and quarter == 8
         and angles == full == 128
         and share * rows == leaf

time: 23.9 us -> 23.7 us (level)
  starting transfers between devices: 11.9 us -> 13.1 us
  local copies, waits for them, and re-layouts: 2.72 us -> 1.82 us
    ppermute x10, starting transfers between devices: 5.93 us -> 7.05 us  [across(): return lambda v: lax.ppermute(v, 'rows', [(i, i ^ flip) for i in range(4)])]
    unnamed x8, local copies, waits for them, and re-layouts: 2.72 us -> 1.82 us
  transfers between devices with their start and end apart: 13 -> 13, of which waited for: 7 -> 8; matrix products, arithmetic and copies ran while one was open for 0% -> 0% of each run, Pallas kernels for 10% -> 9%
where the time goes in v5:
time: 23.7 us; the launch traced here: 23.6 us
  starting transfers between devices  13.1 us (55%)
  waiting for transfers between devices  5.13 us (22%)
  Pallas kernels  3.53 us (15%)
  local copies, waits for them, and re-layouts  1.82 us (8%)
    ppermute x10, starting transfers between devices, across(): return lambda v: lax.ppermute(v, 'rows', [(i, i ^ flip) for i in range(4)])  7.05 us
    ppermute x3, starting transfers between devices, gather_body(): held[j] = lax.ppermute(packed, ('clus', 'rows'), pairs)  6 us
    ppermute x3, waiting for transfers between devices, gather_body(): held[j] = lax.ppermute(packed, ('clus', 'rows'), pairs)  2.7 us
    ppermute x10, waiting for transfers between devices, across(): return lambda v: lax.ppermute(v, 'rows', [(i, i ^ flip) for i in range(4)])  2.43 us
    unnamed x8, local copies, waits for them, and re-layouts  1.82 us
    pallas_call x1, Pallas kernels, gather_body(): pl.pallas_call(functools.partial(chain_kernel, clusters, quarter), out_sh...  1.39 us
    pallas_call x1, Pallas kernels, gather_body(): pl.pallas_call(functools.partial(load_kernel, share, angles, quarter), ou...  1.03 us
  transfers between devices with their start and end apart: 13, of which 8 were waited for; matrix products, arithmetic and copies ran while one was open for 0% of the time, Pallas kernels for 9%

profile of v5, /device:TPU:0, one launch (start us, length us, event | category | flops | bytes accessed | tf_op | source)
XLA Modules:
  0.0 23.6 jit_solution(10600472527787968123)
XLA Ops:
  0.0 0.5 %collective-permute-start = (bf16[512,128]{1,0:T(8,128)(2,1)}, bf16[512,128]{1,0:T(8,128)(2,1)S(1)}, u32[]{:S(2)}, u32[]{:S(2)}) collective-permute-start(bf16[512,128]{1,0:T(8,128)(2,1)} %bitcast.4), channel_id=1, source_target_pairs={{0,1},{1,0},{2,3},{3,2},{4,5},{5,4},{6,7},{7,6},{8,9},{9,8},{10,11... | collective-permute-start | bytes 393224 | tf_op jit(solution)/shard_map/ppermute | solution.py:262
  0.5 2.5 %collective-permute-start.1 = (bf16[2,32,1024]{2,1,0:T(8,128)(2,1)}, bf16[2,32,1024]{2,1,0:T(8,128)(2,1)S(1)}, u32[]{:S(2)}, u32[]{:S(2)}) collective-permute-start(bf16[2,32,1024]{2,1,0:T(8,128)(2,1)} %bitcast.6), channel_id=1, source_target_pairs={{0,2},{1,3},{2,0},{3,1},{4,6},{5,7},{6,4},{7,5},{8,10},{9,11},{10,... | collective-permute-start | bytes 393224 | tf_op jit(solution)/shard_map/ppermute | solution.py:262
  3.0 1.5 %collective-permute-start.4 = (bf16[2,32,1024]{2,1,0:T(8,128)(2,1)}, bf16[2,32,1024]{2,1,0:T(8,128)(2,1)S(1)}, u32[]{:S(2)}, u32[]{:S(2)}) collective-permute-start(bf16[2,32,1024]{2,1,0:T(8,128)(2,1)} %bitcast.8), channel_id=1, source_target_pairs={{0,2},{1,3},{2,0},{3,1},{4,6},{5,7},{6,4},{7,5},{8,10},{9,11},{10,... | collective-permute-start | bytes 393224 | tf_op jit(solution)/shard_map/ppermute | solution.py:262
  4.5 0.9 %copy-done = bf16[256,2,128]{2,1,0:T(2,128)(2,1)S(1)} copy-done((bf16[256,2,128]{2,1,0:T(2,128)(2,1)S(1)}, bf16[256,2,128]{2,1,0:T(2,128)(2,1)}, u32[]{:S(2)}) %copy-start) | copy-done | bytes 131096
  5.4 0.9 %copy-done.1 = bf16[2,1,4,8,1024]{4,3,2,1,0:T(8,128)(2,1)S(1)} copy-done((bf16[2,1,4,8,1024]{4,3,2,1,0:T(8,128)(2,1)S(1)}, bf16[2,1,4,8,1024]{4,3,2,1,0:T(8,128)(2,1)}, u32[]{:S(2)}) %copy-start.1) | copy-done | bytes 131096
  6.3 1.0 %load_own.1 = (bf16[2,32,1024]{2,1,0:T(8,128)(2,1)S(1)}, bf16[256,256]{1,0:T(8,128)(2,1)S(1)}, bf16[256,256]{1,0:T(8,128)(2,1)S(1)}, f32[4,32,128]{2,1,0:T(8,128)S(1)}) custom-call(s32[4,4]{1,0:T(4,128)S(1)} %copy-done.3, bf16[2,32,1024]{2,1,0:T(8,128)(2,1)S(1)} %bitcast.7, bf16[512,128]{1,0:T(8,128)(2,1)S(1)} %bitcast.5, ...), custom_call_target="tpu_custom_call" | custom-call | tf_op jit(solution)/shard_map/load_own/pallas_call | solution.py:273
  7.4 0.2 collective-permute-done.1.l_x
  7.6 0.2 side_skeleton.1
  7.8 2.0 %collective-permute-start.2 = (bf16[2,2,32,128]{3,2,1,0:T(8,128)(2,1)S(1)}, bf16[2,2,32,128]{3,2,1,0:T(8,128)(2,1)S(1)}, u32[]{:S(2)}, u32[]{:S(2)}) collective-permute-start(bf16[2,2,32,128]{3,2,1,0:T(8,128)(2,1)S(1)} %get-tuple-element.17), channel_id=1, source_target_pairs={{0,2},{1,3},{2,0},{3,1},{4,6},{5,7},{6,4},{7,5},{8,10},{9,11},{10,... | collective-permute-start | bytes 98312 | tf_op jit(solution)/shard_map/ppermute | solution.py:262
  9.8 0.3 %collective-permute-done.4.k_x = bf16[2,32,1024]{2,1,0:T(8,128)(2,1)S(1)} collective-permute-done((bf16[2,32,1024]{2,1,0:T(8,128)(2,1)}, bf16[2,32,1024]{2,1,0:T(8,128)(2,1)S(1)}, u32[]{:S(2)}, u32[]{:S(2)}) %collective-permute-start.4) | collective-permute-done | bytes 131104 | tf_op jit(solution)/shard_map/ppermute | solution.py:262
  10.1 0.4 %near_columns.1.near = f32[2,64,64]{2,1,0:T(8,128)S(1)} custom-call(bf16[128,1024]{1,0:T(8,128)(2,1)S(1)} %get-tuple-element.19.l_all, bf16[2,32,1024]{2,1,0:T(8,128)(2,1)S(1)} %bitcast.10, bf16[2,32,1024]{2,1,0:T(8,128)(2,1)S(1)} %collective-permute-done.3.k_core), custom_call_target="tpu_custom_call" | custom-call | flops 21474836480 | bytes 16777216 | tf_op jit(solution)/shard_map/near_columns/pallas_call | solution.py:307
  10.5 1.0 %collective-permute-done.5.k_diag = bf16[2,32,1024]{2,1,0:T(8,128)(2,1)S(1)} collective-permute-done((bf16[2,32,1024]{2,1,0:T(8,128)(2,1)S(1)}, bf16[2,32,1024]{2,1,0:T(8,128)(2,1)S(1)}, u32[]{:S(2)}, u32[]{:S(2)}) %collective-permute-start.5) | collective-permute-done | bytes 131104 | tf_op jit(solution)/shard_map/ppermute | solution.py:262
  11.5 0.4 %far_columns.1.between = bf16[2,2,32,128]{3,2,1,0:T(8,128)(2,1)S(1)} custom-call(f32[2,64,64]{2,1,0:T(8,128)S(1)} %near_columns.1.near, f32[4,32,128]{2,1,0:T(8,128)S(1)} %get-tuple-element.18.keep, bf16[128,1024]{1,0:T(8,128)(2,1)S(1)} %get-tuple-element.19.l_all, bf16[2,32,1024]{2,1,0:T(8,128)(2,1)S(1)} %collective-permute-done.4.k_x, ...), custom_call_target="tpu_custom_call" | custom-call | tf_op jit(solution)/shard_map/far_columns/pallas_call | solution.py:318
  11.9 2.0 %collective-permute-start.9 = (bf16[2,4,32,128]{3,2,1,0:T(8,128)(2,1)S(1)}, bf16[2,4,32,128]{3,2,1,0:T(8,128)(2,1)S(1)}, u32[]{:S(2)}, u32[]{:S(2)}) collective-permute-start(bf16[2,4,32,128]{3,2,1,0:T(8,128)(2,1)S(1)} %pack_rows.1.refs_0_), channel_id=1, source_target_pairs={{0,4},{1,5},{2,6},{3,7},{4,12},{5,9},{6,14},{7,11},{8,0},{9,13},{1... | collective-permute-start | bytes 196616 | tf_op jit(solution)/shard_map/ppermute | solution.py:349
  13.9 2.5 %collective-permute-start.11 = (bf16[2,4,32,128]{3,2,1,0:T(8,128)(2,1)S(1)}, bf16[2,4,32,128]{3,2,1,0:T(8,128)(2,1)S(1)}, u32[]{:S(2)}, u32[]{:S(2)}) collective-permute-start(bf16[2,4,32,128]{3,2,1,0:T(8,128)(2,1)S(1)} %pack_rows.1.refs_0_), channel_id=1, source_target_pairs={{0,12},{1,9},{2,14},{3,11},{4,8},{5,13},{6,10},{7,15},{8,4},{9,1},... | collective-permute-start | bytes 196616 | tf_op jit(solution)/shard_map/ppermute | solution.py:349
  16.3 1.6 %collective-permute-start.7 = (bf16[2,4,32,128]{3,2,1,0:T(8,128)(2,1)S(1)}, bf16[2,4,32,128]{3,2,1,0:T(8,128)(2,1)S(1)}, u32[]{:S(2)}, u32[]{:S(2)}) collective-permute-start(bf16[2,4,32,128]{3,2,1,0:T(8,128)(2,1)S(1)} %pack_rows.1.refs_0_), channel_id=1, source_target_pairs={{0,8},{1,13},{2,10},{3,15},{4,0},{5,1},{6,2},{7,3},{8,12},{9,5},{1... | collective-permute-start | bytes 196616 | tf_op jit(solution)/shard_map/ppermute | solution.py:349
  18.1 0.3 %collective-permute-start.10 = (bf16[2,4,32,128]{3,2,1,0:T(8,128)(2,1)S(1)}, bf16[2,4,32,128]{3,2,1,0:T(8,128)(2,1)S(1)}, u32[]{:S(2)}, u32[]{:S(2)}) collective-permute-start(bf16[2,4,32,128]{3,2,1,0:T(8,128)(2,1)S(1)} %collective-permute-done.9.refs_4_), channel_id=1, source_target_pairs={{0,1},{1,0},{2,3},{3,2},{4,5},{5,4},{6,7},{7,6},{8,9},{9,8},{10,11... | collective-permute-start | bytes 196616 | tf_op jit(solution)/shard_map/ppermute | solution.py:262
  18.4 2.2 %collective-permute-done.11.refs_6_ = bf16[2,4,32,128]{3,2,1,0:T(8,128)(2,1)S(1)} collective-permute-done((bf16[2,4,32,128]{3,2,1,0:T(8,128)(2,1)S(1)}, bf16[2,4,32,128]{3,2,1,0:T(8,128)(2,1)S(1)}, u32[]{:S(2)}, u32[]{:S(2)}) %collective-permute-start.11) | collective-permute-done | bytes 65568 | tf_op jit(solution)/shard_map/ppermute | solution.py:349
  20.6 0.3 %collective-permute-done.7.refs_2_ = bf16[2,4,32,128]{3,2,1,0:T(8,128)(2,1)S(1)} collective-permute-done((bf16[2,4,32,128]{3,2,1,0:T(8,128)(2,1)S(1)}, bf16[2,4,32,128]{3,2,1,0:T(8,128)(2,1)S(1)}, u32[]{:S(2)}, u32[]{:S(2)}) %collective-permute-start.7) | collective-permute-done | bytes 65568 | tf_op jit(solution)/shard_map/ppermute | solution.py:349
  21.0 0.2 collective-permute-start.8
  21.1 0.2 fold_coupling.1.refs_8_
  21.3 0.5 %collective-permute-done.12.refs_7_ = bf16[2,4,32,128]{3,2,1,0:T(8,128)(2,1)S(1)} collective-permute-done((bf16[2,4,32,128]{3,2,1,0:T(8,128)(2,1)S(1)}, bf16[2,4,32,128]{3,2,1,0:T(8,128)(2,1)S(1)}, u32[]{:S(2)}, u32[]{:S(2)}) %collective-permute-start.12) | collective-permute-done | bytes 65568 | tf_op jit(solution)/shard_map/ppermute | solution.py:262
  21.9 0.3 %collective-permute-done.8.refs_3_ = bf16[2,4,32,128]{3,2,1,0:T(8,128)(2,1)S(1)} collective-permute-done((bf16[2,4,32,128]{3,2,1,0:T(8,128)(2,1)S(1)}, bf16[2,4,32,128]{3,2,1,0:T(8,128)(2,1)S(1)}, u32[]{:S(2)}, u32[]{:S(2)}) %collective-permute-start.8) | collective-permute-done | bytes 65568 | tf_op jit(solution)/shard_map/ppermute | solution.py:262
  22.2 1.4 %skeleton_chain.1 = bf16[512,128]{1,0:T(8,128)(2,1)} custom-call(bf16[2,4,32,128]{3,2,1,0:T(8,128)(2,1)S(1)} %pack_rows.1.refs_0_, bf16[2,4,32,128]{3,2,1,0:T(8,128)(2,1)S(1)} %collective-permute-done.6.refs_1_, bf16[2,4,32,128]{3,2,1,0:T(8,128)(2,1)S(1)} %collective-permute-done.7.refs_2_, bf16[2,4,32,128]{3,2,1,0:T(8,128)(2,1)S(1)} %collective-permute-done.8.refs_3_, ...), custom_call_target="tpu_custom_call" | custom-call | tf_op jit(solution)/shard_map/skeleton_chain/pallas_call | solution.py:353
  (17 shorter events, 0.2 us)
Async XLA Ops:
  0.0 4.5 %copy-start.3 = (s32[4,4]{1,0:T(4,128)S(1)}, s32[4,4]{1,0:T(4,128)}, u32[]{:S(2)}) copy-start(s32[4,4]{1,0:T(4,128)} %ranks.1) | copy-start | bytes 196
  0.0 3.0 %collective-permute-start = (bf16[512,128]{1,0:T(8,128)(2,1)}, bf16[512,128]{1,0:T(8,128)(2,1)S(1)}, u32[]{:S(2)}, u32[]{:S(2)}) collective-permute-start(bf16[512,128]{1,0:T(8,128)(2,1)} %bitcast.4), channel_id=1, source_target_pairs={{0,1},{1,0},{2,3},{3,2},{4,5},{5,4},{6,7},{7,6},{8,9},{9,8},{10,11... | collective-permute-start | bytes 393224 | tf_op jit(solution)/shard_map/ppermute | solution.py:262
  0.5 7.1 %collective-permute-start.1 = (bf16[2,32,1024]{2,1,0:T(8,128)(2,1)}, bf16[2,32,1024]{2,1,0:T(8,128)(2,1)S(1)}, u32[]{:S(2)}, u32[]{:S(2)}) collective-permute-start(bf16[2,32,1024]{2,1,0:T(8,128)(2,1)} %bitcast.6), channel_id=1, source_target_pairs={{0,2},{1,3},{2,0},{3,1},{4,6},{5,7},{6,4},{7,5},{8,10},{9,11},{10,... | collective-permute-start | bytes 393224 | tf_op jit(solution)/shard_map/ppermute | solution.py:262
  3.0 7.1 %collective-permute-start.4 = (bf16[2,32,1024]{2,1,0:T(8,128)(2,1)}, bf16[2,32,1024]{2,1,0:T(8,128)(2,1)S(1)}, u32[]{:S(2)}, u32[]{:S(2)}) collective-permute-start(bf16[2,32,1024]{2,1,0:T(8,128)(2,1)} %bitcast.8), channel_id=1, source_target_pairs={{0,2},{1,3},{2,0},{3,1},{4,6},{5,7},{6,4},{7,5},{8,10},{9,11},{10,... | collective-permute-start | bytes 393224 | tf_op jit(solution)/shard_map/ppermute | solution.py:262
  4.5 5.6 %collective-permute-start.3 = (bf16[2,32,1024]{2,1,0:T(8,128)(2,1)}, bf16[2,32,1024]{2,1,0:T(8,128)(2,1)S(1)}, u32[]{:S(2)}, u32[]{:S(2)}) collective-permute-start(bf16[2,32,1024]{2,1,0:T(8,128)(2,1)} %bitcast.9), channel_id=1, source_target_pairs={{0,1},{1,0},{2,3},{3,2},{4,5},{5,4},{6,7},{7,6},{8,9},{9,8},{10,11... | collective-permute-start | bytes 393224 | tf_op jit(solution)/shard_map/ppermute | solution.py:262
  4.5 0.9 %copy-start = (bf16[256,2,128]{2,1,0:T(2,128)(2,1)S(1)}, bf16[256,2,128]{2,1,0:T(2,128)(2,1)}, u32[]{:S(2)}) copy-start(bf16[256,2,128]{2,1,0:T(2,128)(2,1)} %param.4) | copy-start | bytes 393220
  5.4 0.9 %copy-start.1 = (bf16[2,1,4,8,1024]{4,3,2,1,0:T(8,128)(2,1)S(1)}, bf16[2,1,4,8,1024]{4,3,2,1,0:T(8,128)(2,1)}, u32[]{:S(2)}) copy-start(bf16[2,1,4,8,1024]{4,3,2,1,0:T(8,128)(2,1)} %param.5) | copy-start | bytes 393220
  7.6 2.6 %copy-start.2 = (bf16[2,1,4,8,1024]{4,3,2,1,0:T(8,128)(2,1)S(1)}, bf16[2,1,4,8,1024]{4,3,2,1,0:T(8,128)(2,1)}, u32[]{:S(2)}) copy-start(bf16[2,1,4,8,1024]{4,3,2,1,0:T(8,128)(2,1)} %param.6) | copy-start | bytes 393220
  7.8 4.1 %collective-permute-start.2 = (bf16[2,2,32,128]{3,2,1,0:T(8,128)(2,1)S(1)}, bf16[2,2,32,128]{3,2,1,0:T(8,128)(2,1)S(1)}, u32[]{:S(2)}, u32[]{:S(2)}) collective-permute-start(bf16[2,2,32,128]{3,2,1,0:T(8,128)(2,1)S(1)} %get-tuple-element.17), channel_id=1, source_target_pairs={{0,2},{1,3},{2,0},{3,1},{4,6},{5,7},{6,4},{7,5},{8,10},{9,11},{10,... | collective-permute-start | bytes 98312 | tf_op jit(solution)/shard_map/ppermute | solution.py:262
  10.1 1.3 %collective-permute-start.5 = (bf16[2,32,1024]{2,1,0:T(8,128)(2,1)S(1)}, bf16[2,32,1024]{2,1,0:T(8,128)(2,1)S(1)}, u32[]{:S(2)}, u32[]{:S(2)}) collective-permute-start(bf16[2,32,1024]{2,1,0:T(8,128)(2,1)S(1)} %collective-permute-done.4.k_x), channel_id=1, source_target_pairs={{0,1},{1,0},{2,3},{3,2},{4,5},{5,4},{6,7},{7,6},{8,9},{9,8},{10,11... | collective-permute-start | bytes 393224 | tf_op jit(solution)/shard_map/ppermute | solution.py:262
  11.9 6.2 %collective-permute-start.9 = (bf16[2,4,32,128]{3,2,1,0:T(8,128)(2,1)S(1)}, bf16[2,4,32,128]{3,2,1,0:T(8,128)(2,1)S(1)}, u32[]{:S(2)}, u32[]{:S(2)}) collective-permute-start(bf16[2,4,32,128]{3,2,1,0:T(8,128)(2,1)S(1)} %pack_rows.1.refs_0_), channel_id=1, source_target_pairs={{0,4},{1,5},{2,6},{3,7},{4,12},{5,9},{6,14},{7,11},{8,0},{9,13},{1... | collective-permute-start | bytes 196616 | tf_op jit(solution)/shard_map/ppermute | solution.py:349
  13.9 6.8 %collective-permute-start.11 = (bf16[2,4,32,128]{3,2,1,0:T(8,128)(2,1)S(1)}, bf16[2,4,32,128]{3,2,1,0:T(8,128)(2,1)S(1)}, u32[]{:S(2)}, u32[]{:S(2)}) collective-permute-start(bf16[2,4,32,128]{3,2,1,0:T(8,128)(2,1)S(1)} %pack_rows.1.refs_0_), channel_id=1, source_target_pairs={{0,12},{1,9},{2,14},{3,11},{4,8},{5,13},{6,10},{7,15},{8,4},{9,1},... | collective-permute-start | bytes 196616 | tf_op jit(solution)/shard_map/ppermute | solution.py:349
  16.3 4.6 %collective-permute-start.7 = (bf16[2,4,32,128]{3,2,1,0:T(8,128)(2,1)S(1)}, bf16[2,4,32,128]{3,2,1,0:T(8,128)(2,1)S(1)}, u32[]{:S(2)}, u32[]{:S(2)}) collective-permute-start(bf16[2,4,32,128]{3,2,1,0:T(8,128)(2,1)S(1)} %pack_rows.1.refs_0_), channel_id=1, source_target_pairs={{0,8},{1,13},{2,10},{3,15},{4,0},{5,1},{6,2},{7,3},{8,12},{9,5},{1... | collective-permute-start | bytes 196616 | tf_op jit(solution)/shard_map/ppermute | solution.py:349
  17.9 3.4 %collective-permute-start.6 = (bf16[2,4,32,128]{3,2,1,0:T(8,128)(2,1)S(1)}, bf16[2,4,32,128]{3,2,1,0:T(8,128)(2,1)S(1)}, u32[]{:S(2)}, u32[]{:S(2)}) collective-permute-start(bf16[2,4,32,128]{3,2,1,0:T(8,128)(2,1)S(1)} %pack_rows.1.refs_0_), channel_id=1, source_target_pairs={{0,1},{1,0},{2,3},{3,2},{4,5},{5,4},{6,7},{7,6},{8,9},{9,8},{10,11... | collective-permute-start | bytes 196616 | tf_op jit(solution)/shard_map/ppermute | solution.py:262
  18.1 3.3 %collective-permute-start.10 = (bf16[2,4,32,128]{3,2,1,0:T(8,128)(2,1)S(1)}, bf16[2,4,32,128]{3,2,1,0:T(8,128)(2,1)S(1)}, u32[]{:S(2)}, u32[]{:S(2)}) collective-permute-start(bf16[2,4,32,128]{3,2,1,0:T(8,128)(2,1)S(1)} %collective-permute-done.9.refs_4_), channel_id=1, source_target_pairs={{0,1},{1,0},{2,3},{3,2},{4,5},{5,4},{6,7},{7,6},{8,9},{9,8},{10,11... | collective-permute-start | bytes 196616 | tf_op jit(solution)/shard_map/ppermute | solution.py:262
  20.6 1.3 %collective-permute-start.12 = (bf16[2,4,32,128]{3,2,1,0:T(8,128)(2,1)S(1)}, bf16[2,4,32,128]{3,2,1,0:T(8,128)(2,1)S(1)}, u32[]{:S(2)}, u32[]{:S(2)}) collective-permute-start(bf16[2,4,32,128]{3,2,1,0:T(8,128)(2,1)S(1)} %collective-permute-done.11.refs_6_), channel_id=1, source_target_pairs={{0,1},{1,0},{2,3},{3,2},{4,5},{5,4},{6,7},{7,6},{8,9},{9,8},{10,11... | collective-permute-start | bytes 196616 | tf_op jit(solution)/shard_map/ppermute | solution.py:262
  21.0 1.3 %collective-permute-start.8 = (bf16[2,4,32,128]{3,2,1,0:T(8,128)(2,1)S(1)}, bf16[2,4,32,128]{3,2,1,0:T(8,128)(2,1)S(1)}, u32[]{:S(2)}, u32[]{:S(2)}) collective-permute-start(bf16[2,4,32,128]{3,2,1,0:T(8,128)(2,1)S(1)} %collective-permute-done.7.refs_2_), channel_id=1, source_target_pairs={{0,1},{1,0},{2,3},{3,2},{4,5},{5,4},{6,7},{7,6},{8,9},{9,8},{10,11... | collective-permute-start | bytes 196616 | tf_op jit(solution)/shard_map/ppermute | solution.py:262

commit v6 on v5

--- a/solution.py
+++ b/solution.py
@@ -146,6 +146,8 @@
         value = near[part]
         columns = [value[:, :block], far[:, :block], value[:, block:], far[:, block:]]
         value = jnp.concatenate(columns, axis=1)
+        odd = lax.axis_index("rows") % 2 == 1
+        value = jnp.where(odd, pltpu.roll(value, 2 * block, 1), value)
         for at in range(2):
             between[at, part] = (value[at * block : (at + 1) * block] * keep[at]).astype(BF16)
 
@@ -161,8 +163,17 @@
 def fold_kernel(share, k_own, k_x, k_core, k_diag, folded, wide):
     row = lax.axis_index("rows")
     mine = pl.ds(pl.multiple_of(row * share, share), share)
+    odd = row % 2 == 1
+    near, far = (k_own, k_x), (k_core, k_diag)
     real, imag = (
-        jnp.concatenate([k[part, :, mine].astype(F32) for k in (k_own, k_x, k_core, k_diag)], axis=0).T
+        jnp.concatenate(
+            [
+                jnp.where(odd, b[part, :, mine].astype(F32), a[part, :, mine].astype(F32))
+                for first, second in ((near, far), (far, near))
+                for a, b in zip(first, second, strict=True)
+            ],
+            axis=0,
+        ).T
         for part in range(2)
     )
     full = real.shape[1]
@@ -195,15 +206,12 @@
             source = jnp.where(row % 2 == core, senders[0], senders[1])
             ref = pieces[2 * j + core]
             for at in range(2):
-                first = (2 * core + at) * block
-                rows = slice(first, first + block)
+                first = ((row % 2) ^ core) * 2 * block + at * block
+                rows = pl.ds(pl.multiple_of(first, block), block)
                 for part in range(2):
                     columns = slice(part * full, (part + 1) * full)
                     skeleton[source, rows, columns] = ref[at, part].astype(F32)
-                    value = ref[at, 2 + part]
-                    if core:
-                        value = pltpu.roll(value.astype(F32), full // 2, 1).astype(BF16)
-                    between[source, rows, columns] = value
+                    between[source, rows, columns] = ref[at, 2 + part]
 
     def gather(target):
         rows = [

time: 23.7 us -> 23.7 us (level)
  no operation moved by 1% of the time
where the time goes in v6:
time: 23.7 us; the launch traced here: 23.6 us
  starting transfers between devices  12.9 us (54%)
  waiting for transfers between devices  5.19 us (22%)
  Pallas kernels  3.61 us (15%)
  local copies, waits for them, and re-layouts  1.82 us (8%)
    ppermute x10, starting transfers between devices, across(): return lambda v: lax.ppermute(v, 'rows', [(i, i ^ flip) for i in range(4)])  6.97 us
    ppermute x3, starting transfers between devices, gather_body(): held[j] = lax.ppermute(packed, ('clus', 'rows'), pairs)  5.94 us
    ppermute x3, waiting for transfers between devices, gather_body(): held[j] = lax.ppermute(packed, ('clus', 'rows'), pairs)  2.76 us
    ppermute x10, waiting for transfers between devices, across(): return lambda v: lax.ppermute(v, 'rows', [(i, i ^ flip) for i in range(4)])  2.43 us
    unnamed x8, local copies, waits for them, and re-layouts  1.82 us
    pallas_call x1, Pallas kernels, gather_body(): pl.pallas_call(functools.partial(chain_kernel, clusters, quarter), out_sh...  1.39 us
    pallas_call x1, Pallas kernels, gather_body(): pl.pallas_call(functools.partial(load_kernel, share, angles, quarter), ou...  1.03 us
  transfers between devices with their start and end apart: 13, of which 8 were waited for; matrix products, arithmetic and copies ran while one was open for 0% of the time, Pallas kernels for 9%

profile of v6, /device:TPU:0, one launch (start us, length us, event | category | flops | bytes accessed | tf_op | source)
XLA Modules:
  0.0 23.6 jit_solution(2826062720934528224)
XLA Ops:
  0.0 0.5 %collective-permute-start = (bf16[512,128]{1,0:T(8,128)(2,1)}, bf16[512,128]{1,0:T(8,128)(2,1)S(1)}, u32[]{:S(2)}, u32[]{:S(2)}) collective-permute-start(bf16[512,128]{1,0:T(8,128)(2,1)} %bitcast.4), channel_id=1, source_target_pairs={{0,1},{1,0},{2,3},{3,2},{4,5},{5,4},{6,7},{7,6},{8,9},{9,8},{10,11... | collective-permute-start | bytes 393224 | tf_op jit(solution)/shard_map/ppermute | solution.py:270
  0.5 2.5 %collective-permute-start.1 = (bf16[2,32,1024]{2,1,0:T(8,128)(2,1)}, bf16[2,32,1024]{2,1,0:T(8,128)(2,1)S(1)}, u32[]{:S(2)}, u32[]{:S(2)}) collective-permute-start(bf16[2,32,1024]{2,1,0:T(8,128)(2,1)} %bitcast.6), channel_id=1, source_target_pairs={{0,2},{1,3},{2,0},{3,1},{4,6},{5,7},{6,4},{7,5},{8,10},{9,11},{10,... | collective-permute-start | bytes 393224 | tf_op jit(solution)/shard_map/ppermute | solution.py:270
  3.0 1.5 %collective-permute-start.4 = (bf16[2,32,1024]{2,1,0:T(8,128)(2,1)}, bf16[2,32,1024]{2,1,0:T(8,128)(2,1)S(1)}, u32[]{:S(2)}, u32[]{:S(2)}) collective-permute-start(bf16[2,32,1024]{2,1,0:T(8,128)(2,1)} %bitcast.8), channel_id=1, source_target_pairs={{0,2},{1,3},{2,0},{3,1},{4,6},{5,7},{6,4},{7,5},{8,10},{9,11},{10,... | collective-permute-start | bytes 393224 | tf_op jit(solution)/shard_map/ppermute | solution.py:270
  4.5 0.9 %copy-done = bf16[256,2,128]{2,1,0:T(2,128)(2,1)S(1)} copy-done((bf16[256,2,128]{2,1,0:T(2,128)(2,1)S(1)}, bf16[256,2,128]{2,1,0:T(2,128)(2,1)}, u32[]{:S(2)}) %copy-start) | copy-done | bytes 131096
  5.4 0.9 %copy-done.1 = bf16[2,1,4,8,1024]{4,3,2,1,0:T(8,128)(2,1)S(1)} copy-done((bf16[2,1,4,8,1024]{4,3,2,1,0:T(8,128)(2,1)S(1)}, bf16[2,1,4,8,1024]{4,3,2,1,0:T(8,128)(2,1)}, u32[]{:S(2)}) %copy-start.1) | copy-done | bytes 131096
  6.3 1.0 %load_own.1 = (bf16[2,32,1024]{2,1,0:T(8,128)(2,1)S(1)}, bf16[256,256]{1,0:T(8,128)(2,1)S(1)}, bf16[256,256]{1,0:T(8,128)(2,1)S(1)}, f32[4,32,128]{2,1,0:T(8,128)S(1)}) custom-call(s32[4,4]{1,0:T(4,128)S(1)} %copy-done.3, bf16[2,32,1024]{2,1,0:T(8,128)(2,1)S(1)} %bitcast.7, bf16[512,128]{1,0:T(8,128)(2,1)S(1)} %bitcast.5, ...), custom_call_target="tpu_custom_call" | custom-call | tf_op jit(solution)/shard_map/load_own/pallas_call | solution.py:281
  7.4 0.2 collective-permute-done.1.l_x
  7.6 0.2 side_skeleton.1
  7.8 2.0 %collective-permute-start.2 = (bf16[2,2,32,128]{3,2,1,0:T(8,128)(2,1)S(1)}, bf16[2,2,32,128]{3,2,1,0:T(8,128)(2,1)S(1)}, u32[]{:S(2)}, u32[]{:S(2)}) collective-permute-start(bf16[2,2,32,128]{3,2,1,0:T(8,128)(2,1)S(1)} %get-tuple-element.17), channel_id=1, source_target_pairs={{0,2},{1,3},{2,0},{3,1},{4,6},{5,7},{6,4},{7,5},{8,10},{9,11},{10,... | collective-permute-start | bytes 98312 | tf_op jit(solution)/shard_map/ppermute | solution.py:270
  9.8 0.3 %collective-permute-done.4.k_x = bf16[2,32,1024]{2,1,0:T(8,128)(2,1)S(1)} collective-permute-done((bf16[2,32,1024]{2,1,0:T(8,128)(2,1)}, bf16[2,32,1024]{2,1,0:T(8,128)(2,1)S(1)}, u32[]{:S(2)}, u32[]{:S(2)}) %collective-permute-start.4) | collective-permute-done | bytes 131104 | tf_op jit(solution)/shard_map/ppermute | solution.py:270
  10.1 0.4 %near_columns.1.near = f32[2,64,64]{2,1,0:T(8,128)S(1)} custom-call(bf16[128,1024]{1,0:T(8,128)(2,1)S(1)} %get-tuple-element.19.l_all, bf16[2,32,1024]{2,1,0:T(8,128)(2,1)S(1)} %bitcast.10, bf16[2,32,1024]{2,1,0:T(8,128)(2,1)S(1)} %collective-permute-done.3.k_core), custom_call_target="tpu_custom_call" | custom-call | flops 21474836480 | bytes 16777216 | tf_op jit(solution)/shard_map/near_columns/pallas_call | solution.py:315
  10.5 1.0 %collective-permute-done.5.k_diag = bf16[2,32,1024]{2,1,0:T(8,128)(2,1)S(1)} collective-permute-done((bf16[2,32,1024]{2,1,0:T(8,128)(2,1)S(1)}, bf16[2,32,1024]{2,1,0:T(8,128)(2,1)S(1)}, u32[]{:S(2)}, u32[]{:S(2)}) %collective-permute-start.5) | collective-permute-done | bytes 131104 | tf_op jit(solution)/shard_map/ppermute | solution.py:270
  11.5 0.5 %far_columns.1.between = bf16[2,2,32,128]{3,2,1,0:T(8,128)(2,1)S(1)} custom-call(f32[2,64,64]{2,1,0:T(8,128)S(1)} %near_columns.1.near, f32[4,32,128]{2,1,0:T(8,128)S(1)} %get-tuple-element.18.keep, bf16[128,1024]{1,0:T(8,128)(2,1)S(1)} %get-tuple-element.19.l_all, bf16[2,32,1024]{2,1,0:T(8,128)(2,1)S(1)} %collective-permute-done.4.k_x, ...), custom_call_target="tpu_custom_call" | custom-call | tf_op jit(solution)/shard_map/far_columns/pallas_call | solution.py:326
  12.0 1.9 %collective-permute-start.9 = (bf16[2,4,32,128]{3,2,1,0:T(8,128)(2,1)S(1)}, bf16[2,4,32,128]{3,2,1,0:T(8,128)(2,1)S(1)}, u32[]{:S(2)}, u32[]{:S(2)}) collective-permute-start(bf16[2,4,32,128]{3,2,1,0:T(8,128)(2,1)S(1)} %pack_rows.1.refs_0_), channel_id=1, source_target_pairs={{0,4},{1,5},{2,6},{3,7},{4,12},{5,9},{6,14},{7,11},{8,0},{9,13},{1... | collective-permute-start | bytes 196616 | tf_op jit(solution)/shard_map/ppermute | solution.py:357
  13.9 2.5 %collective-permute-start.11 = (bf16[2,4,32,128]{3,2,1,0:T(8,128)(2,1)S(1)}, bf16[2,4,32,128]{3,2,1,0:T(8,128)(2,1)S(1)}, u32[]{:S(2)}, u32[]{:S(2)}) collective-permute-start(bf16[2,4,32,128]{3,2,1,0:T(8,128)(2,1)S(1)} %pack_rows.1.refs_0_), channel_id=1, source_target_pairs={{0,12},{1,9},{2,14},{3,11},{4,8},{5,13},{6,10},{7,15},{8,4},{9,1},... | collective-permute-start | bytes 196616 | tf_op jit(solution)/shard_map/ppermute | solution.py:357
  16.3 1.6 %collective-permute-start.7 = (bf16[2,4,32,128]{3,2,1,0:T(8,128)(2,1)S(1)}, bf16[2,4,32,128]{3,2,1,0:T(8,128)(2,1)S(1)}, u32[]{:S(2)}, u32[]{:S(2)}) collective-permute-start(bf16[2,4,32,128]{3,2,1,0:T(8,128)(2,1)S(1)} %pack_rows.1.refs_0_), channel_id=1, source_target_pairs={{0,8},{1,13},{2,10},{3,15},{4,0},{5,1},{6,2},{7,3},{8,12},{9,5},{1... | collective-permute-start | bytes 196616 | tf_op jit(solution)/shard_map/ppermute | solution.py:357
  17.9 0.2 collective-permute-done.9.refs_4_
  18.1 0.3 %collective-permute-start.10 = (bf16[2,4,32,128]{3,2,1,0:T(8,128)(2,1)S(1)}, bf16[2,4,32,128]{3,2,1,0:T(8,128)(2,1)S(1)}, u32[]{:S(2)}, u32[]{:S(2)}) collective-permute-start(bf16[2,4,32,128]{3,2,1,0:T(8,128)(2,1)S(1)} %collective-permute-done.9.refs_4_), channel_id=1, source_target_pairs={{0,1},{1,0},{2,3},{3,2},{4,5},{5,4},{6,7},{7,6},{8,9},{9,8},{10,11... | collective-permute-start | bytes 196616 | tf_op jit(solution)/shard_map/ppermute | solution.py:270
  18.4 2.2 %collective-permute-done.11.refs_6_ = bf16[2,4,32,128]{3,2,1,0:T(8,128)(2,1)S(1)} collective-permute-done((bf16[2,4,32,128]{3,2,1,0:T(8,128)(2,1)S(1)}, bf16[2,4,32,128]{3,2,1,0:T(8,128)(2,1)S(1)}, u32[]{:S(2)}, u32[]{:S(2)}) %collective-permute-start.11) | collective-permute-done | bytes 65568 | tf_op jit(solution)/shard_map/ppermute | solution.py:357
  20.6 0.3 %collective-permute-done.7.refs_2_ = bf16[2,4,32,128]{3,2,1,0:T(8,128)(2,1)S(1)} collective-permute-done((bf16[2,4,32,128]{3,2,1,0:T(8,128)(2,1)S(1)}, bf16[2,4,32,128]{3,2,1,0:T(8,128)(2,1)S(1)}, u32[]{:S(2)}, u32[]{:S(2)}) %collective-permute-start.7) | collective-permute-done | bytes 65568 | tf_op jit(solution)/shard_map/ppermute | solution.py:357
  21.0 0.2 collective-permute-start.8
  21.3 0.5 %collective-permute-done.12.refs_7_ = bf16[2,4,32,128]{3,2,1,0:T(8,128)(2,1)S(1)} collective-permute-done((bf16[2,4,32,128]{3,2,1,0:T(8,128)(2,1)S(1)}, bf16[2,4,32,128]{3,2,1,0:T(8,128)(2,1)S(1)}, u32[]{:S(2)}, u32[]{:S(2)}) %collective-permute-start.12) | collective-permute-done | bytes 65568 | tf_op jit(solution)/shard_map/ppermute | solution.py:270
  21.9 0.3 %collective-permute-done.8.refs_3_ = bf16[2,4,32,128]{3,2,1,0:T(8,128)(2,1)S(1)} collective-permute-done((bf16[2,4,32,128]{3,2,1,0:T(8,128)(2,1)S(1)}, bf16[2,4,32,128]{3,2,1,0:T(8,128)(2,1)S(1)}, u32[]{:S(2)}, u32[]{:S(2)}) %collective-permute-start.8) | collective-permute-done | bytes 65568 | tf_op jit(solution)/shard_map/ppermute | solution.py:270
  22.2 1.4 %skeleton_chain.1 = bf16[512,128]{1,0:T(8,128)(2,1)} custom-call(bf16[2,4,32,128]{3,2,1,0:T(8,128)(2,1)S(1)} %pack_rows.1.refs_0_, bf16[2,4,32,128]{3,2,1,0:T(8,128)(2,1)S(1)} %collective-permute-done.6.refs_1_, bf16[2,4,32,128]{3,2,1,0:T(8,128)(2,1)S(1)} %collective-permute-done.7.refs_2_, bf16[2,4,32,128]{3,2,1,0:T(8,128)(2,1)S(1)} %collective-permute-done.8.refs_3_, ...), custom_call_target="tpu_custom_call" | custom-call | tf_op jit(solution)/shard_map/skeleton_chain/pallas_call | solution.py:361
  (17 shorter events, 0.2 us)
Async XLA Ops:
  0.0 4.5 %copy-start.3 = (s32[4,4]{1,0:T(4,128)S(1)}, s32[4,4]{1,0:T(4,128)}, u32[]{:S(2)}) copy-start(s32[4,4]{1,0:T(4,128)} %ranks.1) | copy-start | bytes 196
  0.0 3.0 %collective-permute-start = (bf16[512,128]{1,0:T(8,128)(2,1)}, bf16[512,128]{1,0:T(8,128)(2,1)S(1)}, u32[]{:S(2)}, u32[]{:S(2)}) collective-permute-start(bf16[512,128]{1,0:T(8,128)(2,1)} %bitcast.4), channel_id=1, source_target_pairs={{0,1},{1,0},{2,3},{3,2},{4,5},{5,4},{6,7},{7,6},{8,9},{9,8},{10,11... | collective-permute-start | bytes 393224 | tf_op jit(solution)/shard_map/ppermute | solution.py:270
  0.5 7.1 %collective-permute-start.1 = (bf16[2,32,1024]{2,1,0:T(8,128)(2,1)}, bf16[2,32,1024]{2,1,0:T(8,128)(2,1)S(1)}, u32[]{:S(2)}, u32[]{:S(2)}) collective-permute-start(bf16[2,32,1024]{2,1,0:T(8,128)(2,1)} %bitcast.6), channel_id=1, source_target_pairs={{0,2},{1,3},{2,0},{3,1},{4,6},{5,7},{6,4},{7,5},{8,10},{9,11},{10,... | collective-permute-start | bytes 393224 | tf_op jit(solution)/shard_map/ppermute | solution.py:270
  3.0 7.1 %collective-permute-start.4 = (bf16[2,32,1024]{2,1,0:T(8,128)(2,1)}, bf16[2,32,1024]{2,1,0:T(8,128)(2,1)S(1)}, u32[]{:S(2)}, u32[]{:S(2)}) collective-permute-start(bf16[2,32,1024]{2,1,0:T(8,128)(2,1)} %bitcast.8), channel_id=1, source_target_pairs={{0,2},{1,3},{2,0},{3,1},{4,6},{5,7},{6,4},{7,5},{8,10},{9,11},{10,... | collective-permute-start | bytes 393224 | tf_op jit(solution)/shard_map/ppermute | solution.py:270
  4.5 5.6 %collective-permute-start.3 = (bf16[2,32,1024]{2,1,0:T(8,128)(2,1)}, bf16[2,32,1024]{2,1,0:T(8,128)(2,1)S(1)}, u32[]{:S(2)}, u32[]{:S(2)}) collective-permute-start(bf16[2,32,1024]{2,1,0:T(8,128)(2,1)} %bitcast.9), channel_id=1, source_target_pairs={{0,1},{1,0},{2,3},{3,2},{4,5},{5,4},{6,7},{7,6},{8,9},{9,8},{10,11... | collective-permute-start | bytes 393224 | tf_op jit(solution)/shard_map/ppermute | solution.py:270
  4.5 0.9 %copy-start = (bf16[256,2,128]{2,1,0:T(2,128)(2,1)S(1)}, bf16[256,2,128]{2,1,0:T(2,128)(2,1)}, u32[]{:S(2)}) copy-start(bf16[256,2,128]{2,1,0:T(2,128)(2,1)} %param.4) | copy-start | bytes 393220
  5.4 0.9 %copy-start.1 = (bf16[2,1,4,8,1024]{4,3,2,1,0:T(8,128)(2,1)S(1)}, bf16[2,1,4,8,1024]{4,3,2,1,0:T(8,128)(2,1)}, u32[]{:S(2)}) copy-start(bf16[2,1,4,8,1024]{4,3,2,1,0:T(8,128)(2,1)} %param.5) | copy-start | bytes 393220
  7.6 2.6 %copy-start.2 = (bf16[2,1,4,8,1024]{4,3,2,1,0:T(8,128)(2,1)S(1)}, bf16[2,1,4,8,1024]{4,3,2,1,0:T(8,128)(2,1)}, u32[]{:S(2)}) copy-start(bf16[2,1,4,8,1024]{4,3,2,1,0:T(8,128)(2,1)} %param.6) | copy-start | bytes 393220
  7.8 4.2 %collective-permute-start.2 = (bf16[2,2,32,128]{3,2,1,0:T(8,128)(2,1)S(1)}, bf16[2,2,32,128]{3,2,1,0:T(8,128)(2,1)S(1)}, u32[]{:S(2)}, u32[]{:S(2)}) collective-permute-start(bf16[2,2,32,128]{3,2,1,0:T(8,128)(2,1)S(1)} %get-tuple-element.17), channel_id=1, source_target_pairs={{0,2},{1,3},{2,0},{3,1},{4,6},{5,7},{6,4},{7,5},{8,10},{9,11},{10,... | collective-permute-start | bytes 98312 | tf_op jit(solution)/shard_map/ppermute | solution.py:270
  10.1 1.3 %collective-permute-start.5 = (bf16[2,32,1024]{2,1,0:T(8,128)(2,1)S(1)}, bf16[2,32,1024]{2,1,0:T(8,128)(2,1)S(1)}, u32[]{:S(2)}, u32[]{:S(2)}) collective-permute-start(bf16[2,32,1024]{2,1,0:T(8,128)(2,1)S(1)} %collective-permute-done.4.k_x), channel_id=1, source_target_pairs={{0,1},{1,0},{2,3},{3,2},{4,5},{5,4},{6,7},{7,6},{8,9},{9,8},{10,11... | collective-permute-start | bytes 393224 | tf_op jit(solution)/shard_map/ppermute | solution.py:270
  12.0 6.2 %collective-permute-start.9 = (bf16[2,4,32,128]{3,2,1,0:T(8,128)(2,1)S(1)}, bf16[2,4,32,128]{3,2,1,0:T(8,128)(2,1)S(1)}, u32[]{:S(2)}, u32[]{:S(2)}) collective-permute-start(bf16[2,4,32,128]{3,2,1,0:T(8,128)(2,1)S(1)} %pack_rows.1.refs_0_), channel_id=1, source_target_pairs={{0,4},{1,5},{2,6},{3,7},{4,12},{5,9},{6,14},{7,11},{8,0},{9,13},{1... | collective-permute-start | bytes 196616 | tf_op jit(solution)/shard_map/ppermute | solution.py:357
  13.9 6.8 %collective-permute-start.11 = (bf16[2,4,32,128]{3,2,1,0:T(8,128)(2,1)S(1)}, bf16[2,4,32,128]{3,2,1,0:T(8,128)(2,1)S(1)}, u32[]{:S(2)}, u32[]{:S(2)}) collective-permute-start(bf16[2,4,32,128]{3,2,1,0:T(8,128)(2,1)S(1)} %pack_rows.1.refs_0_), channel_id=1, source_target_pairs={{0,12},{1,9},{2,14},{3,11},{4,8},{5,13},{6,10},{7,15},{8,4},{9,1},... | collective-permute-start | bytes 196616 | tf_op jit(solution)/shard_map/ppermute | solution.py:357
  16.3 4.6 %collective-permute-start.7 = (bf16[2,4,32,128]{3,2,1,0:T(8,128)(2,1)S(1)}, bf16[2,4,32,128]{3,2,1,0:T(8,128)(2,1)S(1)}, u32[]{:S(2)}, u32[]{:S(2)}) collective-permute-start(bf16[2,4,32,128]{3,2,1,0:T(8,128)(2,1)S(1)} %pack_rows.1.refs_0_), channel_id=1, source_target_pairs={{0,8},{1,13},{2,10},{3,15},{4,0},{5,1},{6,2},{7,3},{8,12},{9,5},{1... | collective-permute-start | bytes 196616 | tf_op jit(solution)/shard_map/ppermute | solution.py:357
  17.9 3.4 %collective-permute-start.6 = (bf16[2,4,32,128]{3,2,1,0:T(8,128)(2,1)S(1)}, bf16[2,4,32,128]{3,2,1,0:T(8,128)(2,1)S(1)}, u32[]{:S(2)}, u32[]{:S(2)}) collective-permute-start(bf16[2,4,32,128]{3,2,1,0:T(8,128)(2,1)S(1)} %pack_rows.1.refs_0_), channel_id=1, source_target_pairs={{0,1},{1,0},{2,3},{3,2},{4,5},{5,4},{6,7},{7,6},{8,9},{9,8},{10,11... | collective-permute-start | bytes 196616 | tf_op jit(solution)/shard_map/ppermute | solution.py:270
  18.1 3.2 %collective-permute-start.10 = (bf16[2,4,32,128]{3,2,1,0:T(8,128)(2,1)S(1)}, bf16[2,4,32,128]{3,2,1,0:T(8,128)(2,1)S(1)}, u32[]{:S(2)}, u32[]{:S(2)}) collective-permute-start(bf16[2,4,32,128]{3,2,1,0:T(8,128)(2,1)S(1)} %collective-permute-done.9.refs_4_), channel_id=1, source_target_pairs={{0,1},{1,0},{2,3},{3,2},{4,5},{5,4},{6,7},{7,6},{8,9},{9,8},{10,11... | collective-permute-start | bytes 196616 | tf_op jit(solution)/shard_map/ppermute | solution.py:270
  20.6 1.3 %collective-permute-start.12 = (bf16[2,4,32,128]{3,2,1,0:T(8,128)(2,1)S(1)}, bf16[2,4,32,128]{3,2,1,0:T(8,128)(2,1)S(1)}, u32[]{:S(2)}, u32[]{:S(2)}) collective-permute-start(bf16[2,4,32,128]{3,2,1,0:T(8,128)(2,1)S(1)} %collective-permute-done.11.refs_6_), channel_id=1, source_target_pairs={{0,1},{1,0},{2,3},{3,2},{4,5},{5,4},{6,7},{7,6},{8,9},{9,8},{10,11... | collective-permute-start | bytes 196616 | tf_op jit(solution)/shard_map/ppermute | solution.py:270
  21.0 1.3 %collective-permute-start.8 = (bf16[2,4,32,128]{3,2,1,0:T(8,128)(2,1)S(1)}, bf16[2,4,32,128]{3,2,1,0:T(8,128)(2,1)S(1)}, u32[]{:S(2)}, u32[]{:S(2)}) collective-permute-start(bf16[2,4,32,128]{3,2,1,0:T(8,128)(2,1)S(1)} %collective-permute-done.7.refs_2_), channel_id=1, source_target_pairs={{0,1},{1,0},{2,3},{3,2},{4,5},{5,4},{6,7},{7,6},{8,9},{9,8},{10,11... | collective-permute-start | bytes 196616 | tf_op jit(solution)/shard_map/ppermute | solution.py:270

commit v7 on v6

--- a/solution.py
+++ b/solution.py
@@ -149,7 +149,7 @@
         odd = lax.axis_index("rows") % 2 == 1
         value = jnp.where(odd, pltpu.roll(value, 2 * block, 1), value)
         for at in range(2):
-            between[at, part] = (value[at * block : (at + 1) * block] * keep[at]).astype(BF16)
+            between[at, 2 + part] = (value[at * block : (at + 1) * block] * keep[at]).astype(BF16)
 
 
 def pack_kernel(partial, partial_x, keep, between, packed):
@@ -157,7 +157,6 @@
         for part in range(2):
             value = partial[at, part] + partial_x[1 - at, part].astype(F32)
             packed[at, part] = (value * keep[at]).astype(BF16)
-            packed[at, 2 + part] = between[at, part]
 
 
 def fold_kernel(share, k_own, k_x, k_core, k_diag, folded, wide):
@@ -325,7 +324,7 @@
     k_diag = to_core(k_x)
     between = pl.pallas_call(
         far_kernel,
-        out_shape=jax.ShapeDtypeStruct((2, 2, block, full), BF16),
+        out_shape=jax.ShapeDtypeStruct((2, 4, block, full), BF16),
         in_specs=in_vmem(5),
         out_specs=in_vmem(1)[0],
         scratch_shapes=[pltpu.VMEM((4 * block, leaf), BF16)],
@@ -337,6 +336,7 @@
         out_shape=jax.ShapeDtypeStruct((2, 4, block, angles), BF16),
         in_specs=in_vmem(4),
         out_specs=in_vmem(1)[0],
+        input_output_aliases={3: 0},
         compiler_params=params,
         name="pack_rows",
     )(kept_partial, partial_x, keep, between)

time: 23.7 us -> 23.7 us (level)
  no operation moved by 1% of the time
where the time goes in v7:
time: 23.7 us; the launch traced here: 23.6 us
  starting transfers between devices  12.9 us (54%)
  waiting for transfers between devices  5.19 us (22%)
  Pallas kernels  3.61 us (15%)
  local copies, waits for them, and re-layouts  1.82 us (8%)
    ppermute x10, starting transfers between devices, across(): return lambda v: lax.ppermute(v, 'rows', [(i, i ^ flip) for i in range(4)])  6.97 us
    ppermute x3, starting transfers between devices, gather_body(): held[j] = lax.ppermute(packed, ('clus', 'rows'), pairs)  5.94 us
    ppermute x3, waiting for transfers between devices, gather_body(): held[j] = lax.ppermute(packed, ('clus', 'rows'), pairs)  2.76 us
    ppermute x10, waiting for transfers between devices, across(): return lambda v: lax.ppermute(v, 'rows', [(i, i ^ flip) for i in range(4)])  2.43 us
    unnamed x8, local copies, waits for them, and re-layouts  1.82 us
    pallas_call x1, Pallas kernels, gather_body(): pl.pallas_call(functools.partial(chain_kernel, clusters, quarter), out_sh...  1.39 us
    pallas_call x1, Pallas kernels, gather_body(): pl.pallas_call(functools.partial(load_kernel, share, angles, quarter), ou...  1.03 us
  transfers between devices with their start and end apart: 13, of which 8 were waited for; matrix products, arithmetic and copies ran while one was open for 0% of the time, Pallas kernels for 9%

profile of v7, /device:TPU:0, one launch (start us, length us, event | category | flops | bytes accessed | tf_op | source)
XLA Modules:
  0.0 23.6 jit_solution(9106217285779100103)
XLA Ops:
  0.0 0.5 %collective-permute-start = (bf16[512,128]{1,0:T(8,128)(2,1)}, bf16[512,128]{1,0:T(8,128)(2,1)S(1)}, u32[]{:S(2)}, u32[]{:S(2)}) collective-permute-start(bf16[512,128]{1,0:T(8,128)(2,1)} %bitcast.4), channel_id=1, source_target_pairs={{0,1},{1,0},{2,3},{3,2},{4,5},{5,4},{6,7},{7,6},{8,9},{9,8},{10,11... | collective-permute-start | bytes 393224 | tf_op jit(solution)/shard_map/ppermute | solution.py:269
  0.5 2.5 %collective-permute-start.1 = (bf16[2,32,1024]{2,1,0:T(8,128)(2,1)}, bf16[2,32,1024]{2,1,0:T(8,128)(2,1)S(1)}, u32[]{:S(2)}, u32[]{:S(2)}) collective-permute-start(bf16[2,32,1024]{2,1,0:T(8,128)(2,1)} %bitcast.6), channel_id=1, source_target_pairs={{0,2},{1,3},{2,0},{3,1},{4,6},{5,7},{6,4},{7,5},{8,10},{9,11},{10,... | collective-permute-start | bytes 393224 | tf_op jit(solution)/shard_map/ppermute | solution.py:269
  3.0 1.5 %collective-permute-start.4 = (bf16[2,32,1024]{2,1,0:T(8,128)(2,1)}, bf16[2,32,1024]{2,1,0:T(8,128)(2,1)S(1)}, u32[]{:S(2)}, u32[]{:S(2)}) collective-permute-start(bf16[2,32,1024]{2,1,0:T(8,128)(2,1)} %bitcast.8), channel_id=1, source_target_pairs={{0,2},{1,3},{2,0},{3,1},{4,6},{5,7},{6,4},{7,5},{8,10},{9,11},{10,... | collective-permute-start | bytes 393224 | tf_op jit(solution)/shard_map/ppermute | solution.py:269
  4.5 0.9 %copy-done = bf16[256,2,128]{2,1,0:T(2,128)(2,1)S(1)} copy-done((bf16[256,2,128]{2,1,0:T(2,128)(2,1)S(1)}, bf16[256,2,128]{2,1,0:T(2,128)(2,1)}, u32[]{:S(2)}) %copy-start) | copy-done | bytes 131096
  5.4 0.9 %copy-done.1 = bf16[2,1,4,8,1024]{4,3,2,1,0:T(8,128)(2,1)S(1)} copy-done((bf16[2,1,4,8,1024]{4,3,2,1,0:T(8,128)(2,1)S(1)}, bf16[2,1,4,8,1024]{4,3,2,1,0:T(8,128)(2,1)}, u32[]{:S(2)}) %copy-start.1) | copy-done | bytes 131096
  6.3 1.0 %load_own.1 = (bf16[2,32,1024]{2,1,0:T(8,128)(2,1)S(1)}, bf16[256,256]{1,0:T(8,128)(2,1)S(1)}, bf16[256,256]{1,0:T(8,128)(2,1)S(1)}, f32[4,32,128]{2,1,0:T(8,128)S(1)}) custom-call(s32[4,4]{1,0:T(4,128)S(1)} %copy-done.3, bf16[2,32,1024]{2,1,0:T(8,128)(2,1)S(1)} %bitcast.7, bf16[512,128]{1,0:T(8,128)(2,1)S(1)} %bitcast.5, ...), custom_call_target="tpu_custom_call" | custom-call | tf_op jit(solution)/shard_map/load_own/pallas_call | solution.py:280
  7.4 0.2 collective-permute-done.1.l_x
  7.6 0.2 side_skeleton.1
  7.8 2.0 %collective-permute-start.2 = (bf16[2,2,32,128]{3,2,1,0:T(8,128)(2,1)S(1)}, bf16[2,2,32,128]{3,2,1,0:T(8,128)(2,1)S(1)}, u32[]{:S(2)}, u32[]{:S(2)}) collective-permute-start(bf16[2,2,32,128]{3,2,1,0:T(8,128)(2,1)S(1)} %get-tuple-element.17), channel_id=1, source_target_pairs={{0,2},{1,3},{2,0},{3,1},{4,6},{5,7},{6,4},{7,5},{8,10},{9,11},{10,... | collective-permute-start | bytes 98312 | tf_op jit(solution)/shard_map/ppermute | solution.py:269
  9.8 0.3 %collective-permute-done.4.k_x = bf16[2,32,1024]{2,1,0:T(8,128)(2,1)S(1)} collective-permute-done((bf16[2,32,1024]{2,1,0:T(8,128)(2,1)}, bf16[2,32,1024]{2,1,0:T(8,128)(2,1)S(1)}, u32[]{:S(2)}, u32[]{:S(2)}) %collective-permute-start.4) | collective-permute-done | bytes 131104 | tf_op jit(solution)/shard_map/ppermute | solution.py:269
  10.1 0.4 %near_columns.1.near = f32[2,64,64]{2,1,0:T(8,128)S(1)} custom-call(bf16[128,1024]{1,0:T(8,128)(2,1)S(1)} %get-tuple-element.19.l_all, bf16[2,32,1024]{2,1,0:T(8,128)(2,1)S(1)} %bitcast.10, bf16[2,32,1024]{2,1,0:T(8,128)(2,1)S(1)} %collective-permute-done.3.k_core), custom_call_target="tpu_custom_call" | custom-call | flops 21474836480 | bytes 16777216 | tf_op jit(solution)/shard_map/near_columns/pallas_call | solution.py:314
  10.5 1.0 %collective-permute-done.5.k_diag = bf16[2,32,1024]{2,1,0:T(8,128)(2,1)S(1)} collective-permute-done((bf16[2,32,1024]{2,1,0:T(8,128)(2,1)S(1)}, bf16[2,32,1024]{2,1,0:T(8,128)(2,1)S(1)}, u32[]{:S(2)}, u32[]{:S(2)}) %collective-permute-start.5) | collective-permute-done | bytes 131104 | tf_op jit(solution)/shard_map/ppermute | solution.py:269
  11.5 0.5 %far_columns.1.between = bf16[2,4,32,128]{3,2,1,0:T(8,128)(2,1)S(1)} custom-call(f32[2,64,64]{2,1,0:T(8,128)S(1)} %near_columns.1.near, f32[4,32,128]{2,1,0:T(8,128)S(1)} %get-tuple-element.18.keep, bf16[128,1024]{1,0:T(8,128)(2,1)S(1)} %get-tuple-element.19.l_all, bf16[2,32,1024]{2,1,0:T(8,128)(2,1)S(1)} %collective-permute-done.4.k_x, ...), custom_call_target="tpu_custom_call" | custom-call | tf_op jit(solution)/shard_map/far_columns/pallas_call | solution.py:325
  12.0 1.9 %collective-permute-start.9 = (bf16[2,4,32,128]{3,2,1,0:T(8,128)(2,1)S(1)}, bf16[2,4,32,128]{3,2,1,0:T(8,128)(2,1)S(1)}, u32[]{:S(2)}, u32[]{:S(2)}) collective-permute-start(bf16[2,4,32,128]{3,2,1,0:T(8,128)(2,1)S(1)} %pack_rows.1.refs_0_), channel_id=1, source_target_pairs={{0,4},{1,5},{2,6},{3,7},{4,12},{5,9},{6,14},{7,11},{8,0},{9,13},{1... | collective-permute-start | bytes 196616 | tf_op jit(solution)/shard_map/ppermute | solution.py:357
  13.9 2.5 %collective-permute-start.11 = (bf16[2,4,32,128]{3,2,1,0:T(8,128)(2,1)S(1)}, bf16[2,4,32,128]{3,2,1,0:T(8,128)(2,1)S(1)}, u32[]{:S(2)}, u32[]{:S(2)}) collective-permute-start(bf16[2,4,32,128]{3,2,1,0:T(8,128)(2,1)S(1)} %pack_rows.1.refs_0_), channel_id=1, source_target_pairs={{0,12},{1,9},{2,14},{3,11},{4,8},{5,13},{6,10},{7,15},{8,4},{9,1},... | collective-permute-start | bytes 196616 | tf_op jit(solution)/shard_map/ppermute | solution.py:357
  16.3 1.6 %collective-permute-start.7 = (bf16[2,4,32,128]{3,2,1,0:T(8,128)(2,1)S(1)}, bf16[2,4,32,128]{3,2,1,0:T(8,128)(2,1)S(1)}, u32[]{:S(2)}, u32[]{:S(2)}) collective-permute-start(bf16[2,4,32,128]{3,2,1,0:T(8,128)(2,1)S(1)} %pack_rows.1.refs_0_), channel_id=1, source_target_pairs={{0,8},{1,13},{2,10},{3,15},{4,0},{5,1},{6,2},{7,3},{8,12},{9,5},{1... | collective-permute-start | bytes 196616 | tf_op jit(solution)/shard_map/ppermute | solution.py:357
  17.9 0.2 collective-permute-done.9.refs_4_
  18.1 0.3 %collective-permute-start.10 = (bf16[2,4,32,128]{3,2,1,0:T(8,128)(2,1)S(1)}, bf16[2,4,32,128]{3,2,1,0:T(8,128)(2,1)S(1)}, u32[]{:S(2)}, u32[]{:S(2)}) collective-permute-start(bf16[2,4,32,128]{3,2,1,0:T(8,128)(2,1)S(1)} %collective-permute-done.9.refs_4_), channel_id=1, source_target_pairs={{0,1},{1,0},{2,3},{3,2},{4,5},{5,4},{6,7},{7,6},{8,9},{9,8},{10,11... | collective-permute-start | bytes 196616 | tf_op jit(solution)/shard_map/ppermute | solution.py:269
  18.4 2.2 %collective-permute-done.11.refs_6_ = bf16[2,4,32,128]{3,2,1,0:T(8,128)(2,1)S(1)} collective-permute-done((bf16[2,4,32,128]{3,2,1,0:T(8,128)(2,1)S(1)}, bf16[2,4,32,128]{3,2,1,0:T(8,128)(2,1)S(1)}, u32[]{:S(2)}, u32[]{:S(2)}) %collective-permute-start.11) | collective-permute-done | bytes 65568 | tf_op jit(solution)/shard_map/ppermute | solution.py:357
  20.6 0.3 %collective-permute-done.7.refs_2_ = bf16[2,4,32,128]{3,2,1,0:T(8,128)(2,1)S(1)} collective-permute-done((bf16[2,4,32,128]{3,2,1,0:T(8,128)(2,1)S(1)}, bf16[2,4,32,128]{3,2,1,0:T(8,128)(2,1)S(1)}, u32[]{:S(2)}, u32[]{:S(2)}) %collective-permute-start.7) | collective-permute-done | bytes 65568 | tf_op jit(solution)/shard_map/ppermute | solution.py:357
  21.0 0.2 collective-permute-start.8
  21.3 0.5 %collective-permute-done.12.refs_7_ = bf16[2,4,32,128]{3,2,1,0:T(8,128)(2,1)S(1)} collective-permute-done((bf16[2,4,32,128]{3,2,1,0:T(8,128)(2,1)S(1)}, bf16[2,4,32,128]{3,2,1,0:T(8,128)(2,1)S(1)}, u32[]{:S(2)}, u32[]{:S(2)}) %collective-permute-start.12) | collective-permute-done | bytes 65568 | tf_op jit(solution)/shard_map/ppermute | solution.py:269
  21.9 0.3 %collective-permute-done.8.refs_3_ = bf16[2,4,32,128]{3,2,1,0:T(8,128)(2,1)S(1)} collective-permute-done((bf16[2,4,32,128]{3,2,1,0:T(8,128)(2,1)S(1)}, bf16[2,4,32,128]{3,2,1,0:T(8,128)(2,1)S(1)}, u32[]{:S(2)}, u32[]{:S(2)}) %collective-permute-start.8) | collective-permute-done | bytes 65568 | tf_op jit(solution)/shard_map/ppermute | solution.py:269
  22.2 1.4 %skeleton_chain.1 = bf16[512,128]{1,0:T(8,128)(2,1)} custom-call(bf16[2,4,32,128]{3,2,1,0:T(8,128)(2,1)S(1)} %pack_rows.1.refs_0_, bf16[2,4,32,128]{3,2,1,0:T(8,128)(2,1)S(1)} %collective-permute-done.6.refs_1_, bf16[2,4,32,128]{3,2,1,0:T(8,128)(2,1)S(1)} %collective-permute-done.7.refs_2_, bf16[2,4,32,128]{3,2,1,0:T(8,128)(2,1)S(1)} %collective-permute-done.8.refs_3_, ...), custom_call_target="tpu_custom_call" | custom-call | tf_op jit(solution)/shard_map/skeleton_chain/pallas_call | solution.py:361
  (17 shorter events, 0.2 us)
Async XLA Ops:
  0.0 4.5 %copy-start.3 = (s32[4,4]{1,0:T(4,128)S(1)}, s32[4,4]{1,0:T(4,128)}, u32[]{:S(2)}) copy-start(s32[4,4]{1,0:T(4,128)} %ranks.1) | copy-start | bytes 196
  0.0 3.0 %collective-permute-start = (bf16[512,128]{1,0:T(8,128)(2,1)}, bf16[512,128]{1,0:T(8,128)(2,1)S(1)}, u32[]{:S(2)}, u32[]{:S(2)}) collective-permute-start(bf16[512,128]{1,0:T(8,128)(2,1)} %bitcast.4), channel_id=1, source_target_pairs={{0,1},{1,0},{2,3},{3,2},{4,5},{5,4},{6,7},{7,6},{8,9},{9,8},{10,11... | collective-permute-start | bytes 393224 | tf_op jit(solution)/shard_map/ppermute | solution.py:269
  0.5 7.1 %collective-permute-start.1 = (bf16[2,32,1024]{2,1,0:T(8,128)(2,1)}, bf16[2,32,1024]{2,1,0:T(8,128)(2,1)S(1)}, u32[]{:S(2)}, u32[]{:S(2)}) collective-permute-start(bf16[2,32,1024]{2,1,0:T(8,128)(2,1)} %bitcast.6), channel_id=1, source_target_pairs={{0,2},{1,3},{2,0},{3,1},{4,6},{5,7},{6,4},{7,5},{8,10},{9,11},{10,... | collective-permute-start | bytes 393224 | tf_op jit(solution)/shard_map/ppermute | solution.py:269
  3.0 7.1 %collective-permute-start.4 = (bf16[2,32,1024]{2,1,0:T(8,128)(2,1)}, bf16[2,32,1024]{2,1,0:T(8,128)(2,1)S(1)}, u32[]{:S(2)}, u32[]{:S(2)}) collective-permute-start(bf16[2,32,1024]{2,1,0:T(8,128)(2,1)} %bitcast.8), channel_id=1, source_target_pairs={{0,2},{1,3},{2,0},{3,1},{4,6},{5,7},{6,4},{7,5},{8,10},{9,11},{10,... | collective-permute-start | bytes 393224 | tf_op jit(solution)/shard_map/ppermute | solution.py:269
  4.5 5.6 %collective-permute-start.3 = (bf16[2,32,1024]{2,1,0:T(8,128)(2,1)}, bf16[2,32,1024]{2,1,0:T(8,128)(2,1)S(1)}, u32[]{:S(2)}, u32[]{:S(2)}) collective-permute-start(bf16[2,32,1024]{2,1,0:T(8,128)(2,1)} %bitcast.9), channel_id=1, source_target_pairs={{0,1},{1,0},{2,3},{3,2},{4,5},{5,4},{6,7},{7,6},{8,9},{9,8},{10,11... | collective-permute-start | bytes 393224 | tf_op jit(solution)/shard_map/ppermute | solution.py:269
  4.5 0.9 %copy-start = (bf16[256,2,128]{2,1,0:T(2,128)(2,1)S(1)}, bf16[256,2,128]{2,1,0:T(2,128)(2,1)}, u32[]{:S(2)}) copy-start(bf16[256,2,128]{2,1,0:T(2,128)(2,1)} %param.4) | copy-start | bytes 393220
  5.4 0.9 %copy-start.1 = (bf16[2,1,4,8,1024]{4,3,2,1,0:T(8,128)(2,1)S(1)}, bf16[2,1,4,8,1024]{4,3,2,1,0:T(8,128)(2,1)}, u32[]{:S(2)}) copy-start(bf16[2,1,4,8,1024]{4,3,2,1,0:T(8,128)(2,1)} %param.5) | copy-start | bytes 393220
  7.6 2.6 %copy-start.2 = (bf16[2,1,4,8,1024]{4,3,2,1,0:T(8,128)(2,1)S(1)}, bf16[2,1,4,8,1024]{4,3,2,1,0:T(8,128)(2,1)}, u32[]{:S(2)}) copy-start(bf16[2,1,4,8,1024]{4,3,2,1,0:T(8,128)(2,1)} %param.6) | copy-start | bytes 393220
  7.8 4.2 %collective-permute-start.2 = (bf16[2,2,32,128]{3,2,1,0:T(8,128)(2,1)S(1)}, bf16[2,2,32,128]{3,2,1,0:T(8,128)(2,1)S(1)}, u32[]{:S(2)}, u32[]{:S(2)}) collective-permute-start(bf16[2,2,32,128]{3,2,1,0:T(8,128)(2,1)S(1)} %get-tuple-element.17), channel_id=1, source_target_pairs={{0,2},{1,3},{2,0},{3,1},{4,6},{5,7},{6,4},{7,5},{8,10},{9,11},{10,... | collective-permute-start | bytes 98312 | tf_op jit(solution)/shard_map/ppermute | solution.py:269
  10.1 1.3 %collective-permute-start.5 = (bf16[2,32,1024]{2,1,0:T(8,128)(2,1)S(1)}, bf16[2,32,1024]{2,1,0:T(8,128)(2,1)S(1)}, u32[]{:S(2)}, u32[]{:S(2)}) collective-permute-start(bf16[2,32,1024]{2,1,0:T(8,128)(2,1)S(1)} %collective-permute-done.4.k_x), channel_id=1, source_target_pairs={{0,1},{1,0},{2,3},{3,2},{4,5},{5,4},{6,7},{7,6},{8,9},{9,8},{10,11... | collective-permute-start | bytes 393224 | tf_op jit(solution)/shard_map/ppermute | solution.py:269
  12.0 6.2 %collective-permute-start.9 = (bf16[2,4,32,128]{3,2,1,0:T(8,128)(2,1)S(1)}, bf16[2,4,32,128]{3,2,1,0:T(8,128)(2,1)S(1)}, u32[]{:S(2)}, u32[]{:S(2)}) collective-permute-start(bf16[2,4,32,128]{3,2,1,0:T(8,128)(2,1)S(1)} %pack_rows.1.refs_0_), channel_id=1, source_target_pairs={{0,4},{1,5},{2,6},{3,7},{4,12},{5,9},{6,14},{7,11},{8,0},{9,13},{1... | collective-permute-start | bytes 196616 | tf_op jit(solution)/shard_map/ppermute | solution.py:357
  13.9 6.8 %collective-permute-start.11 = (bf16[2,4,32,128]{3,2,1,0:T(8,128)(2,1)S(1)}, bf16[2,4,32,128]{3,2,1,0:T(8,128)(2,1)S(1)}, u32[]{:S(2)}, u32[]{:S(2)}) collective-permute-start(bf16[2,4,32,128]{3,2,1,0:T(8,128)(2,1)S(1)} %pack_rows.1.refs_0_), channel_id=1, source_target_pairs={{0,12},{1,9},{2,14},{3,11},{4,8},{5,13},{6,10},{7,15},{8,4},{9,1},... | collective-permute-start | bytes 196616 | tf_op jit(solution)/shard_map/ppermute | solution.py:357
  16.3 4.6 %collective-permute-start.7 = (bf16[2,4,32,128]{3,2,1,0:T(8,128)(2,1)S(1)}, bf16[2,4,32,128]{3,2,1,0:T(8,128)(2,1)S(1)}, u32[]{:S(2)}, u32[]{:S(2)}) collective-permute-start(bf16[2,4,32,128]{3,2,1,0:T(8,128)(2,1)S(1)} %pack_rows.1.refs_0_), channel_id=1, source_target_pairs={{0,8},{1,13},{2,10},{3,15},{4,0},{5,1},{6,2},{7,3},{8,12},{9,5},{1... | collective-permute-start | bytes 196616 | tf_op jit(solution)/shard_map/ppermute | solution.py:357
  17.9 3.4 %collective-permute-start.6 = (bf16[2,4,32,128]{3,2,1,0:T(8,128)(2,1)S(1)}, bf16[2,4,32,128]{3,2,1,0:T(8,128)(2,1)S(1)}, u32[]{:S(2)}, u32[]{:S(2)}) collective-permute-start(bf16[2,4,32,128]{3,2,1,0:T(8,128)(2,1)S(1)} %pack_rows.1.refs_0_), channel_id=1, source_target_pairs={{0,1},{1,0},{2,3},{3,2},{4,5},{5,4},{6,7},{7,6},{8,9},{9,8},{10,11... | collective-permute-start | bytes 196616 | tf_op jit(solution)/shard_map/ppermute | solution.py:269
  18.1 3.2 %collective-permute-start.10 = (bf16[2,4,32,128]{3,2,1,0:T(8,128)(2,1)S(1)}, bf16[2,4,32,128]{3,2,1,0:T(8,128)(2,1)S(1)}, u32[]{:S(2)}, u32[]{:S(2)}) collective-permute-start(bf16[2,4,32,128]{3,2,1,0:T(8,128)(2,1)S(1)} %collective-permute-done.9.refs_4_), channel_id=1, source_target_pairs={{0,1},{1,0},{2,3},{3,2},{4,5},{5,4},{6,7},{7,6},{8,9},{9,8},{10,11... | collective-permute-start | bytes 196616 | tf_op jit(solution)/shard_map/ppermute | solution.py:269
  20.6 1.3 %collective-permute-start.12 = (bf16[2,4,32,128]{3,2,1,0:T(8,128)(2,1)S(1)}, bf16[2,4,32,128]{3,2,1,0:T(8,128)(2,1)S(1)}, u32[]{:S(2)}, u32[]{:S(2)}) collective-permute-start(bf16[2,4,32,128]{3,2,1,0:T(8,128)(2,1)S(1)} %collective-permute-done.11.refs_6_), channel_id=1, source_target_pairs={{0,1},{1,0},{2,3},{3,2},{4,5},{5,4},{6,7},{7,6},{8,9},{9,8},{10,11... | collective-permute-start | bytes 196616 | tf_op jit(solution)/shard_map/ppermute | solution.py:269
  21.0 1.3 %collective-permute-start.8 = (bf16[2,4,32,128]{3,2,1,0:T(8,128)(2,1)S(1)}, bf16[2,4,32,128]{3,2,1,0:T(8,128)(2,1)S(1)}, u32[]{:S(2)}, u32[]{:S(2)}) collective-permute-start(bf16[2,4,32,128]{3,2,1,0:T(8,128)(2,1)S(1)} %collective-permute-done.7.refs_2_), channel_id=1, source_target_pairs={{0,1},{1,0},{2,3},{3,2},{4,5},{5,4},{6,7},{7,6},{8,9},{9,8},{10,11... | collective-permute-start | bytes 196616 | tf_op jit(solution)/shard_map/ppermute | solution.py:269

commit v8 on v6

--- a/solution.py
+++ b/solution.py
@@ -275,8 +275,7 @@
     l_x = to_x(factor)
     current = excitation.reshape(2 * share, angles)
     x_near = to_core(current)
-    to_send, _ = lax.optimization_barrier((weights, x_near))
-    k_x = to_x(to_send)
+    k_x = to_x(weights)
     k_core = to_core(weights)
     l_own, x_own, x_core, keep = pl.pallas_call(
         functools.partial(load_kernel, share, angles, quarter),

time: 23.7 us -> 24 us (1.013)
  waiting for transfers between devices: 5.19 us -> 6.34 us
  starting transfers between devices: 12.9 us -> 12 us
    ppermute x10, waiting for transfers between devices: 2.43 us -> 3.73 us  [across(): return lambda v: lax.ppermute(v, 'rows', [(i, i ^ flip) for i in range(4)])]
    ppermute x10, starting transfers between devices: 6.97 us -> 5.83 us  [across(): return lambda v: lax.ppermute(v, 'rows', [(i, i ^ flip) for i in range(4)])]
where the time goes in v8:
time: 24 us; the launch traced here: 23.8 us
  starting transfers between devices  12 us (50%)
  waiting for transfers between devices  6.34 us (26%)
  Pallas kernels  3.61 us (15%)
  local copies, waits for them, and re-layouts  1.82 us (8%)
    ppermute x3, starting transfers between devices, gather_body(): held[j] = lax.ppermute(packed, ('clus', 'rows'), pairs)  6.14 us
    ppermute x10, starting transfers between devices, across(): return lambda v: lax.ppermute(v, 'rows', [(i, i ^ flip) for i in range(4)])  5.83 us
    ppermute x10, waiting for transfers between devices, across(): return lambda v: lax.ppermute(v, 'rows', [(i, i ^ flip) for i in range(4)])  3.73 us
    ppermute x3, waiting for transfers between devices, gather_body(): held[j] = lax.ppermute(packed, ('clus', 'rows'), pairs)  2.62 us
    unnamed x8, local copies, waits for them, and re-layouts  1.82 us
    pallas_call x1, Pallas kernels, gather_body(): pl.pallas_call(functools.partial(chain_kernel, clusters, quarter), out_sh...  1.39 us
    pallas_call x1, Pallas kernels, gather_body(): pl.pallas_call(functools.partial(load_kernel, share, angles, quarter), ou...  1.03 us
  transfers between devices with their start and end apart: 13, of which 8 were waited for; matrix products, arithmetic and copies ran while one was open for 0% of the time, Pallas kernels for 9%

profile of v8, /device:TPU:0, one launch (start us, length us, event | category | flops | bytes accessed | tf_op | source)
XLA Modules:
  0.0 23.8 jit_solution(3304198389753994556)
XLA Ops:
  0.0 0.5 %collective-permute-start = (bf16[512,128]{1,0:T(8,128)(2,1)}, bf16[512,128]{1,0:T(8,128)(2,1)S(1)}, u32[]{:S(2)}, u32[]{:S(2)}) collective-permute-start(bf16[512,128]{1,0:T(8,128)(2,1)} %bitcast.4), channel_id=1, source_target_pairs={{0,1},{1,0},{2,3},{3,2},{4,5},{5,4},{6,7},{7,6},{8,9},{9,8},{10,11... | collective-permute-start | bytes 393224 | tf_op jit(solution)/shard_map/ppermute | solution.py:270
  0.5 2.5 %collective-permute-start.1 = (bf16[2,32,1024]{2,1,0:T(8,128)(2,1)}, bf16[2,32,1024]{2,1,0:T(8,128)(2,1)S(1)}, u32[]{:S(2)}, u32[]{:S(2)}) collective-permute-start(bf16[2,32,1024]{2,1,0:T(8,128)(2,1)} %bitcast.6), channel_id=1, source_target_pairs={{0,2},{1,3},{2,0},{3,1},{4,6},{5,7},{6,4},{7,5},{8,10},{9,11},{10,... | collective-permute-start | bytes 393224 | tf_op jit(solution)/shard_map/ppermute | solution.py:270
  3.0 0.1 collective-permute-start.4
  3.2 0.9 %copy-done = bf16[256,2,128]{2,1,0:T(2,128)(2,1)S(1)} copy-done((bf16[256,2,128]{2,1,0:T(2,128)(2,1)S(1)}, bf16[256,2,128]{2,1,0:T(2,128)(2,1)}, u32[]{:S(2)}) %copy-start) | copy-done | bytes 131096
  4.1 0.9 %copy-done.1 = bf16[2,1,4,8,1024]{4,3,2,1,0:T(8,128)(2,1)S(1)} copy-done((bf16[2,1,4,8,1024]{4,3,2,1,0:T(8,128)(2,1)S(1)}, bf16[2,1,4,8,1024]{4,3,2,1,0:T(8,128)(2,1)}, u32[]{:S(2)}) %copy-start.1) | copy-done | bytes 131096
  5.0 1.0 %load_own.1 = (bf16[2,32,1024]{2,1,0:T(8,128)(2,1)S(1)}, bf16[256,256]{1,0:T(8,128)(2,1)S(1)}, bf16[256,256]{1,0:T(8,128)(2,1)S(1)}, f32[4,32,128]{2,1,0:T(8,128)S(1)}) custom-call(s32[4,4]{1,0:T(4,128)S(1)} %copy-done.3, bf16[2,32,1024]{2,1,0:T(8,128)(2,1)S(1)} %bitcast.7, bf16[512,128]{1,0:T(8,128)(2,1)S(1)} %bitcast.5, ...), custom_call_target="tpu_custom_call" | custom-call | tf_op jit(solution)/shard_map/load_own/pallas_call | solution.py:280
  6.1 1.5 %collective-permute-done.1.l_x = bf16[2,32,1024]{2,1,0:T(8,128)(2,1)S(1)} collective-permute-done((bf16[2,32,1024]{2,1,0:T(8,128)(2,1)}, bf16[2,32,1024]{2,1,0:T(8,128)(2,1)S(1)}, u32[]{:S(2)}, u32[]{:S(2)}) %collective-permute-start.1) | collective-permute-done | bytes 131104 | tf_op jit(solution)/shard_map/ppermute | solution.py:270
  7.6 0.2 side_skeleton.1
  7.8 2.0 %collective-permute-start.2 = (bf16[2,2,32,128]{3,2,1,0:T(8,128)(2,1)S(1)}, bf16[2,2,32,128]{3,2,1,0:T(8,128)(2,1)S(1)}, u32[]{:S(2)}, u32[]{:S(2)}) collective-permute-start(bf16[2,2,32,128]{3,2,1,0:T(8,128)(2,1)S(1)} %get-tuple-element.16), channel_id=1, source_target_pairs={{0,2},{1,3},{2,0},{3,1},{4,6},{5,7},{6,4},{7,5},{8,10},{9,11},{10,... | collective-permute-start | bytes 98312 | tf_op jit(solution)/shard_map/ppermute | solution.py:270
  9.8 0.4 %collective-permute-done.4.k_x = bf16[2,32,1024]{2,1,0:T(8,128)(2,1)S(1)} collective-permute-done((bf16[2,32,1024]{2,1,0:T(8,128)(2,1)}, bf16[2,32,1024]{2,1,0:T(8,128)(2,1)S(1)}, u32[]{:S(2)}, u32[]{:S(2)}) %collective-permute-start.4) | collective-permute-done | bytes 131104 | tf_op jit(solution)/shard_map/ppermute | solution.py:270
  10.2 0.4 %near_columns.1.near = f32[2,64,64]{2,1,0:T(8,128)S(1)} custom-call(bf16[128,1024]{1,0:T(8,128)(2,1)S(1)} %get-tuple-element.18.l_all, bf16[2,32,1024]{2,1,0:T(8,128)(2,1)S(1)} %bitcast.10, bf16[2,32,1024]{2,1,0:T(8,128)(2,1)S(1)} %collective-permute-done.3.k_core), custom_call_target="tpu_custom_call" | custom-call | flops 21474836480 | bytes 16777216 | tf_op jit(solution)/shard_map/near_columns/pallas_call | solution.py:314
  10.5 1.0 %collective-permute-done.5.k_diag = bf16[2,32,1024]{2,1,0:T(8,128)(2,1)S(1)} collective-permute-done((bf16[2,32,1024]{2,1,0:T(8,128)(2,1)S(1)}, bf16[2,32,1024]{2,1,0:T(8,128)(2,1)S(1)}, u32[]{:S(2)}, u32[]{:S(2)}) %collective-permute-start.5) | collective-permute-done | bytes 131104 | tf_op jit(solution)/shard_map/ppermute | solution.py:270
  11.5 0.5 %far_columns.1.between = bf16[2,2,32,128]{3,2,1,0:T(8,128)(2,1)S(1)} custom-call(f32[2,64,64]{2,1,0:T(8,128)S(1)} %near_columns.1.near, f32[4,32,128]{2,1,0:T(8,128)S(1)} %get-tuple-element.17.keep, bf16[128,1024]{1,0:T(8,128)(2,1)S(1)} %get-tuple-element.18.l_all, bf16[2,32,1024]{2,1,0:T(8,128)(2,1)S(1)} %collective-permute-done.4.k_x, ...), custom_call_target="tpu_custom_call" | custom-call | tf_op jit(solution)/shard_map/far_columns/pallas_call | solution.py:325
  12.0 2.1 %collective-permute-start.9 = (bf16[2,4,32,128]{3,2,1,0:T(8,128)(2,1)S(1)}, bf16[2,4,32,128]{3,2,1,0:T(8,128)(2,1)S(1)}, u32[]{:S(2)}, u32[]{:S(2)}) collective-permute-start(bf16[2,4,32,128]{3,2,1,0:T(8,128)(2,1)S(1)} %pack_rows.1.refs_0_), channel_id=1, source_target_pairs={{0,4},{1,5},{2,6},{3,7},{4,12},{5,9},{6,14},{7,11},{8,0},{9,13},{1... | collective-permute-start | bytes 196616 | tf_op jit(solution)/shard_map/ppermute | solution.py:356
  14.1 2.5 %collective-permute-start.11 = (bf16[2,4,32,128]{3,2,1,0:T(8,128)(2,1)S(1)}, bf16[2,4,32,128]{3,2,1,0:T(8,128)(2,1)S(1)}, u32[]{:S(2)}, u32[]{:S(2)}) collective-permute-start(bf16[2,4,32,128]{3,2,1,0:T(8,128)(2,1)S(1)} %pack_rows.1.refs_0_), channel_id=1, source_target_pairs={{0,12},{1,9},{2,14},{3,11},{4,8},{5,13},{6,10},{7,15},{8,4},{9,1},... | collective-permute-start | bytes 196616 | tf_op jit(solution)/shard_map/ppermute | solution.py:356
  16.5 1.6 %collective-permute-start.7 = (bf16[2,4,32,128]{3,2,1,0:T(8,128)(2,1)S(1)}, bf16[2,4,32,128]{3,2,1,0:T(8,128)(2,1)S(1)}, u32[]{:S(2)}, u32[]{:S(2)}) collective-permute-start(bf16[2,4,32,128]{3,2,1,0:T(8,128)(2,1)S(1)} %pack_rows.1.refs_0_), channel_id=1, source_target_pairs={{0,8},{1,13},{2,10},{3,15},{4,0},{5,1},{6,2},{7,3},{8,12},{9,5},{1... | collective-permute-start | bytes 196616 | tf_op jit(solution)/shard_map/ppermute | solution.py:356
  18.2 0.4 %collective-permute-start.10 = (bf16[2,4,32,128]{3,2,1,0:T(8,128)(2,1)S(1)}, bf16[2,4,32,128]{3,2,1,0:T(8,128)(2,1)S(1)}, u32[]{:S(2)}, u32[]{:S(2)}) collective-permute-start(bf16[2,4,32,128]{3,2,1,0:T(8,128)(2,1)S(1)} %collective-permute-done.9.refs_4_), channel_id=1, source_target_pairs={{0,1},{1,0},{2,3},{3,2},{4,5},{5,4},{6,7},{7,6},{8,9},{9,8},{10,11... | collective-permute-start | bytes 196616 | tf_op jit(solution)/shard_map/ppermute | solution.py:270
  18.6 2.2 %collective-permute-done.11.refs_6_ = bf16[2,4,32,128]{3,2,1,0:T(8,128)(2,1)S(1)} collective-permute-done((bf16[2,4,32,128]{3,2,1,0:T(8,128)(2,1)S(1)}, bf16[2,4,32,128]{3,2,1,0:T(8,128)(2,1)S(1)}, u32[]{:S(2)}, u32[]{:S(2)}) %collective-permute-start.11) | collective-permute-done | bytes 65568 | tf_op jit(solution)/shard_map/ppermute | solution.py:356
  20.8 0.3 %collective-permute-done.7.refs_2_ = bf16[2,4,32,128]{3,2,1,0:T(8,128)(2,1)S(1)} collective-permute-done((bf16[2,4,32,128]{3,2,1,0:T(8,128)(2,1)S(1)}, bf16[2,4,32,128]{3,2,1,0:T(8,128)(2,1)S(1)}, u32[]{:S(2)}, u32[]{:S(2)}) %collective-permute-start.7) | collective-permute-done | bytes 65568 | tf_op jit(solution)/shard_map/ppermute | solution.py:356
  21.2 0.2 collective-permute-start.8
  21.3 0.2 fold_coupling.1.refs_8_
  21.5 0.5 %collective-permute-done.12.refs_7_ = bf16[2,4,32,128]{3,2,1,0:T(8,128)(2,1)S(1)} collective-permute-done((bf16[2,4,32,128]{3,2,1,0:T(8,128)(2,1)S(1)}, bf16[2,4,32,128]{3,2,1,0:T(8,128)(2,1)S(1)}, u32[]{:S(2)}, u32[]{:S(2)}) %collective-permute-start.12) | collective-permute-done | bytes 65568 | tf_op jit(solution)/shard_map/ppermute | solution.py:270
  22.1 0.3 %collective-permute-done.8.refs_3_ = bf16[2,4,32,128]{3,2,1,0:T(8,128)(2,1)S(1)} collective-permute-done((bf16[2,4,32,128]{3,2,1,0:T(8,128)(2,1)S(1)}, bf16[2,4,32,128]{3,2,1,0:T(8,128)(2,1)S(1)}, u32[]{:S(2)}, u32[]{:S(2)}) %collective-permute-start.8) | collective-permute-done | bytes 65568 | tf_op jit(solution)/shard_map/ppermute | solution.py:270
  22.4 1.4 %skeleton_chain.1 = bf16[512,128]{1,0:T(8,128)(2,1)} custom-call(bf16[2,4,32,128]{3,2,1,0:T(8,128)(2,1)S(1)} %pack_rows.1.refs_0_, bf16[2,4,32,128]{3,2,1,0:T(8,128)(2,1)S(1)} %collective-permute-done.6.refs_1_, bf16[2,4,32,128]{3,2,1,0:T(8,128)(2,1)S(1)} %collective-permute-done.7.refs_2_, bf16[2,4,32,128]{3,2,1,0:T(8,128)(2,1)S(1)} %collective-permute-done.8.refs_3_, ...), custom_call_target="tpu_custom_call" | custom-call | tf_op jit(solution)/shard_map/skeleton_chain/pallas_call | solution.py:360
  (17 shorter events, 0.2 us)
Async XLA Ops:
  0.0 3.2 %copy-start.3 = (s32[4,4]{1,0:T(4,128)S(1)}, s32[4,4]{1,0:T(4,128)}, u32[]{:S(2)}) copy-start(s32[4,4]{1,0:T(4,128)} %ranks.1) | copy-start | bytes 196
  0.0 3.2 %collective-permute-start = (bf16[512,128]{1,0:T(8,128)(2,1)}, bf16[512,128]{1,0:T(8,128)(2,1)S(1)}, u32[]{:S(2)}, u32[]{:S(2)}) collective-permute-start(bf16[512,128]{1,0:T(8,128)(2,1)} %bitcast.4), channel_id=1, source_target_pairs={{0,1},{1,0},{2,3},{3,2},{4,5},{5,4},{6,7},{7,6},{8,9},{9,8},{10,11... | collective-permute-start | bytes 393224 | tf_op jit(solution)/shard_map/ppermute | solution.py:270
  0.5 7.1 %collective-permute-start.1 = (bf16[2,32,1024]{2,1,0:T(8,128)(2,1)}, bf16[2,32,1024]{2,1,0:T(8,128)(2,1)S(1)}, u32[]{:S(2)}, u32[]{:S(2)}) collective-permute-start(bf16[2,32,1024]{2,1,0:T(8,128)(2,1)} %bitcast.6), channel_id=1, source_target_pairs={{0,2},{1,3},{2,0},{3,1},{4,6},{5,7},{6,4},{7,5},{8,10},{9,11},{10,... | collective-permute-start | bytes 393224 | tf_op jit(solution)/shard_map/ppermute | solution.py:270
  3.0 7.1 %collective-permute-start.4 = (bf16[2,32,1024]{2,1,0:T(8,128)(2,1)}, bf16[2,32,1024]{2,1,0:T(8,128)(2,1)S(1)}, u32[]{:S(2)}, u32[]{:S(2)}) collective-permute-start(bf16[2,32,1024]{2,1,0:T(8,128)(2,1)} %bitcast.8), channel_id=1, source_target_pairs={{0,2},{1,3},{2,0},{3,1},{4,6},{5,7},{6,4},{7,5},{8,10},{9,11},{10,... | collective-permute-start | bytes 393224 | tf_op jit(solution)/shard_map/ppermute | solution.py:270
  3.1 7.0 %collective-permute-start.3 = (bf16[2,32,1024]{2,1,0:T(8,128)(2,1)}, bf16[2,32,1024]{2,1,0:T(8,128)(2,1)S(1)}, u32[]{:S(2)}, u32[]{:S(2)}) collective-permute-start(bf16[2,32,1024]{2,1,0:T(8,128)(2,1)} %bitcast.9), channel_id=1, source_target_pairs={{0,1},{1,0},{2,3},{3,2},{4,5},{5,4},{6,7},{7,6},{8,9},{9,8},{10,11... | collective-permute-start | bytes 393224 | tf_op jit(solution)/shard_map/ppermute | solution.py:270
  3.2 0.9 %copy-start = (bf16[256,2,128]{2,1,0:T(2,128)(2,1)S(1)}, bf16[256,2,128]{2,1,0:T(2,128)(2,1)}, u32[]{:S(2)}) copy-start(bf16[256,2,128]{2,1,0:T(2,128)(2,1)} %param.4) | copy-start | bytes 393220
  4.1 0.9 %copy-start.1 = (bf16[2,1,4,8,1024]{4,3,2,1,0:T(8,128)(2,1)S(1)}, bf16[2,1,4,8,1024]{4,3,2,1,0:T(8,128)(2,1)}, u32[]{:S(2)}) copy-start(bf16[2,1,4,8,1024]{4,3,2,1,0:T(8,128)(2,1)} %param.5) | copy-start | bytes 393220
  7.6 2.6 %copy-start.2 = (bf16[2,1,4,8,1024]{4,3,2,1,0:T(8,128)(2,1)S(1)}, bf16[2,1,4,8,1024]{4,3,2,1,0:T(8,128)(2,1)}, u32[]{:S(2)}) copy-start(bf16[2,1,4,8,1024]{4,3,2,1,0:T(8,128)(2,1)} %param.6) | copy-start | bytes 393220
  7.8 4.2 %collective-permute-start.2 = (bf16[2,2,32,128]{3,2,1,0:T(8,128)(2,1)S(1)}, bf16[2,2,32,128]{3,2,1,0:T(8,128)(2,1)S(1)}, u32[]{:S(2)}, u32[]{:S(2)}) collective-permute-start(bf16[2,2,32,128]{3,2,1,0:T(8,128)(2,1)S(1)} %get-tuple-element.16), channel_id=1, source_target_pairs={{0,2},{1,3},{2,0},{3,1},{4,6},{5,7},{6,4},{7,5},{8,10},{9,11},{10,... | collective-permute-start | bytes 98312 | tf_op jit(solution)/shard_map/ppermute | solution.py:270
  10.1 1.3 %collective-permute-start.5 = (bf16[2,32,1024]{2,1,0:T(8,128)(2,1)S(1)}, bf16[2,32,1024]{2,1,0:T(8,128)(2,1)S(1)}, u32[]{:S(2)}, u32[]{:S(2)}) collective-permute-start(bf16[2,32,1024]{2,1,0:T(8,128)(2,1)S(1)} %collective-permute-done.4.k_x), channel_id=1, source_target_pairs={{0,1},{1,0},{2,3},{3,2},{4,5},{5,4},{6,7},{7,6},{8,9},{9,8},{10,11... | collective-permute-start | bytes 393224 | tf_op jit(solution)/shard_map/ppermute | solution.py:270
  12.0 6.2 %collective-permute-start.9 = (bf16[2,4,32,128]{3,2,1,0:T(8,128)(2,1)S(1)}, bf16[2,4,32,128]{3,2,1,0:T(8,128)(2,1)S(1)}, u32[]{:S(2)}, u32[]{:S(2)}) collective-permute-start(bf16[2,4,32,128]{3,2,1,0:T(8,128)(2,1)S(1)} %pack_rows.1.refs_0_), channel_id=1, source_target_pairs={{0,4},{1,5},{2,6},{3,7},{4,12},{5,9},{6,14},{7,11},{8,0},{9,13},{1... | collective-permute-start | bytes 196616 | tf_op jit(solution)/shard_map/ppermute | solution.py:356
  14.1 6.8 %collective-permute-start.11 = (bf16[2,4,32,128]{3,2,1,0:T(8,128)(2,1)S(1)}, bf16[2,4,32,128]{3,2,1,0:T(8,128)(2,1)S(1)}, u32[]{:S(2)}, u32[]{:S(2)}) collective-permute-start(bf16[2,4,32,128]{3,2,1,0:T(8,128)(2,1)S(1)} %pack_rows.1.refs_0_), channel_id=1, source_target_pairs={{0,12},{1,9},{2,14},{3,11},{4,8},{5,13},{6,10},{7,15},{8,4},{9,1},... | collective-permute-start | bytes 196616 | tf_op jit(solution)/shard_map/ppermute | solution.py:356
  16.5 4.6 %collective-permute-start.7 = (bf16[2,4,32,128]{3,2,1,0:T(8,128)(2,1)S(1)}, bf16[2,4,32,128]{3,2,1,0:T(8,128)(2,1)S(1)}, u32[]{:S(2)}, u32[]{:S(2)}) collective-permute-start(bf16[2,4,32,128]{3,2,1,0:T(8,128)(2,1)S(1)} %pack_rows.1.refs_0_), channel_id=1, source_target_pairs={{0,8},{1,13},{2,10},{3,15},{4,0},{5,1},{6,2},{7,3},{8,12},{9,5},{1... | collective-permute-start | bytes 196616 | tf_op jit(solution)/shard_map/ppermute | solution.py:356
  18.1 3.4 %collective-permute-start.6 = (bf16[2,4,32,128]{3,2,1,0:T(8,128)(2,1)S(1)}, bf16[2,4,32,128]{3,2,1,0:T(8,128)(2,1)S(1)}, u32[]{:S(2)}, u32[]{:S(2)}) collective-permute-start(bf16[2,4,32,128]{3,2,1,0:T(8,128)(2,1)S(1)} %pack_rows.1.refs_0_), channel_id=1, source_target_pairs={{0,1},{1,0},{2,3},{3,2},{4,5},{5,4},{6,7},{7,6},{8,9},{9,8},{10,11... | collective-permute-start | bytes 196616 | tf_op jit(solution)/shard_map/ppermute | solution.py:270
  18.2 3.3 %collective-permute-start.10 = (bf16[2,4,32,128]{3,2,1,0:T(8,128)(2,1)S(1)}, bf16[2,4,32,128]{3,2,1,0:T(8,128)(2,1)S(1)}, u32[]{:S(2)}, u32[]{:S(2)}) collective-permute-start(bf16[2,4,32,128]{3,2,1,0:T(8,128)(2,1)S(1)} %collective-permute-done.9.refs_4_), channel_id=1, source_target_pairs={{0,1},{1,0},{2,3},{3,2},{4,5},{5,4},{6,7},{7,6},{8,9},{9,8},{10,11... | collective-permute-start | bytes 196616 | tf_op jit(solution)/shard_map/ppermute | solution.py:270
  20.8 1.3 %collective-permute-start.12 = (bf16[2,4,32,128]{3,2,1,0:T(8,128)(2,1)S(1)}, bf16[2,4,32,128]{3,2,1,0:T(8,128)(2,1)S(1)}, u32[]{:S(2)}, u32[]{:S(2)}) collective-permute-start(bf16[2,4,32,128]{3,2,1,0:T(8,128)(2,1)S(1)} %collective-permute-done.11.refs_6_), channel_id=1, source_target_pairs={{0,1},{1,0},{2,3},{3,2},{4,5},{5,4},{6,7},{7,6},{8,9},{9,8},{10,11... | collective-permute-start | bytes 196616 | tf_op jit(solution)/shard_map/ppermute | solution.py:270
  21.2 1.3 %collective-permute-start.8 = (bf16[2,4,32,128]{3,2,1,0:T(8,128)(2,1)S(1)}, bf16[2,4,32,128]{3,2,1,0:T(8,128)(2,1)S(1)}, u32[]{:S(2)}, u32[]{:S(2)}) collective-permute-start(bf16[2,4,32,128]{3,2,1,0:T(8,128)(2,1)S(1)} %collective-permute-done.7.refs_2_), channel_id=1, source_target_pairs={{0,1},{1,0},{2,3},{3,2},{4,5},{5,4},{6,7},{7,6},{8,9},{9,8},{10,11... | collective-permute-start | bytes 196616 | tf_op jit(solution)/shard_map/ppermute | solution.py:270

commit v9 on v6

--- a/solution.py
+++ b/solution.py
@@ -105,7 +105,7 @@
     copies[1].wait()
 
 
-def side_kernel(share, angles, l_own, l_x, x_own, x_core, partial, kept_partial, l_all):
+def side_kernel(share, angles, l_own, l_x, x_own, x_core, keep, partial, kept_partial, l_all):
     row = lax.axis_index("rows")
     block = l_own.shape[1]
     for part in range(2):
@@ -119,7 +119,7 @@
         total = term if total is None else total + term
     for part, value in enumerate(combine(total, 2 * block, angles)):
         for at in range(2):
-            rows = value[at * block : (at + 1) * block]
+            rows = value[at * block : (at + 1) * block] * keep[at]
             kept_partial[at, part] = rows
             partial[at, part] = rows.astype(BF16)
 
@@ -152,11 +152,11 @@
             between[at, part] = (value[at * block : (at + 1) * block] * keep[at]).astype(BF16)
 
 
-def pack_kernel(partial, partial_x, keep, between, packed):
+def pack_kernel(partial, partial_x, between, packed):
     for at in range(2):
         for part in range(2):
             value = partial[at, part] + partial_x[1 - at, part].astype(F32)
-            packed[at, part] = (value * keep[at]).astype(BF16)
+            packed[at, part] = value.astype(BF16)
             packed[at, 2 + part] = between[at, part]
 
 
@@ -305,12 +305,12 @@
             jax.ShapeDtypeStruct((2, 2, block, angles), F32),
             jax.ShapeDtypeStruct((4 * block, leaf), BF16),
         ),
-        in_specs=in_vmem(4),
+        in_specs=in_vmem(5),
         out_specs=tuple(in_vmem(3)),
         compiler_params=params,
         cost_estimate=pl.CostEstimate(flops=1 << 30, bytes_accessed=16 << 20, transcendentals=0),
         name="side_skeleton",
-    )(l_own, l_x, x_own, x_core)
+    )(l_own, l_x, x_own, x_core, keep)
     partial_x = to_x(partial)
     near = pl.pallas_call(
         near_kernel,
@@ -335,11 +335,11 @@
     packed = pl.pallas_call(
         pack_kernel,
         out_shape=jax.ShapeDtypeStruct((2, 4, block, angles), BF16),
-        in_specs=in_vmem(4),
+        in_specs=in_vmem(3),
         out_specs=in_vmem(1)[0],
         compiler_params=params,
         name="pack_rows",
-    )(kept_partial, partial_x, keep, between)
+    )(kept_partial, partial_x, between)
     folded = pl.pallas_call(
         functools.partial(fold_kernel, share),
         out_shape=jax.ShapeDtypeStruct((2 * share, 2 * full), BF16),

time: 23.7 us -> 23.7 us (level)
  no operation moved by 1% of the time
where the time goes in v9:
time: 23.7 us; the launch traced here: 23.6 us
  starting transfers between devices  12.9 us (54%)
  waiting for transfers between devices  5.19 us (22%)
  Pallas kernels  3.6 us (15%)
  local copies, waits for them, and re-layouts  1.82 us (8%)
    ppermute x10, starting transfers between devices, across(): return lambda v: lax.ppermute(v, 'rows', [(i, i ^ flip) for i in range(4)])  6.98 us
    ppermute x3, starting transfers between devices, gather_body(): held[j] = lax.ppermute(packed, ('clus', 'rows'), pairs)  5.94 us
    ppermute x3, waiting for transfers between devices, gather_body(): held[j] = lax.ppermute(packed, ('clus', 'rows'), pairs)  2.76 us
    ppermute x10, waiting for transfers between devices, across(): return lambda v: lax.ppermute(v, 'rows', [(i, i ^ flip) for i in range(4)])  2.43 us
    unnamed x8, local copies, waits for them, and re-layouts  1.82 us
    pallas_call x1, Pallas kernels, gather_body(): pl.pallas_call(functools.partial(chain_kernel, clusters, quarter), out_sh...  1.39 us
    pallas_call x1, Pallas kernels, gather_body(): pl.pallas_call(functools.partial(load_kernel, share, angles, quarter), ou...  1.03 us
  transfers between devices with their start and end apart: 13, of which 8 were waited for; matrix products, arithmetic and copies ran while one was open for 0% of the time, Pallas kernels for 9%

profile of v9, /device:TPU:0, one launch (start us, length us, event | category | flops | bytes accessed | tf_op | source)
XLA Modules:
  0.0 23.6 jit_solution(7670760185026735374)
XLA Ops:
  0.0 0.5 %collective-permute-start = (bf16[512,128]{1,0:T(8,128)(2,1)}, bf16[512,128]{1,0:T(8,128)(2,1)S(1)}, u32[]{:S(2)}, u32[]{:S(2)}) collective-permute-start(bf16[512,128]{1,0:T(8,128)(2,1)} %bitcast.4), channel_id=1, source_target_pairs={{0,1},{1,0},{2,3},{3,2},{4,5},{5,4},{6,7},{7,6},{8,9},{9,8},{10,11... | collective-permute-start | bytes 393224 | tf_op jit(solution)/shard_map/ppermute | solution.py:270
  0.5 2.5 %collective-permute-start.1 = (bf16[2,32,1024]{2,1,0:T(8,128)(2,1)}, bf16[2,32,1024]{2,1,0:T(8,128)(2,1)S(1)}, u32[]{:S(2)}, u32[]{:S(2)}) collective-permute-start(bf16[2,32,1024]{2,1,0:T(8,128)(2,1)} %bitcast.6), channel_id=1, source_target_pairs={{0,2},{1,3},{2,0},{3,1},{4,6},{5,7},{6,4},{7,5},{8,10},{9,11},{10,... | collective-permute-start | bytes 393224 | tf_op jit(solution)/shard_map/ppermute | solution.py:270
  3.0 1.5 %collective-permute-start.4 = (bf16[2,32,1024]{2,1,0:T(8,128)(2,1)}, bf16[2,32,1024]{2,1,0:T(8,128)(2,1)S(1)}, u32[]{:S(2)}, u32[]{:S(2)}) collective-permute-start(bf16[2,32,1024]{2,1,0:T(8,128)(2,1)} %bitcast.8), channel_id=1, source_target_pairs={{0,2},{1,3},{2,0},{3,1},{4,6},{5,7},{6,4},{7,5},{8,10},{9,11},{10,... | collective-permute-start | bytes 393224 | tf_op jit(solution)/shard_map/ppermute | solution.py:270
  4.5 0.9 %copy-done = bf16[256,2,128]{2,1,0:T(2,128)(2,1)S(1)} copy-done((bf16[256,2,128]{2,1,0:T(2,128)(2,1)S(1)}, bf16[256,2,128]{2,1,0:T(2,128)(2,1)}, u32[]{:S(2)}) %copy-start) | copy-done | bytes 131096
  5.4 0.9 %copy-done.1 = bf16[2,1,4,8,1024]{4,3,2,1,0:T(8,128)(2,1)S(1)} copy-done((bf16[2,1,4,8,1024]{4,3,2,1,0:T(8,128)(2,1)S(1)}, bf16[2,1,4,8,1024]{4,3,2,1,0:T(8,128)(2,1)}, u32[]{:S(2)}) %copy-start.1) | copy-done | bytes 131096
  6.3 1.0 %load_own.1 = (bf16[2,32,1024]{2,1,0:T(8,128)(2,1)S(1)}, bf16[256,256]{1,0:T(8,128)(2,1)S(1)}, bf16[256,256]{1,0:T(8,128)(2,1)S(1)}, f32[4,32,128]{2,1,0:T(8,128)S(1)}) custom-call(s32[4,4]{1,0:T(4,128)S(1)} %copy-done.3, bf16[2,32,1024]{2,1,0:T(8,128)(2,1)S(1)} %bitcast.7, bf16[512,128]{1,0:T(8,128)(2,1)S(1)} %bitcast.5, ...), custom_call_target="tpu_custom_call" | custom-call | tf_op jit(solution)/shard_map/load_own/pallas_call | solution.py:281
  7.4 0.2 collective-permute-done.1.l_x
  7.6 0.2 side_skeleton.1
  7.8 2.0 %collective-permute-start.2 = (bf16[2,2,32,128]{3,2,1,0:T(8,128)(2,1)S(1)}, bf16[2,2,32,128]{3,2,1,0:T(8,128)(2,1)S(1)}, u32[]{:S(2)}, u32[]{:S(2)}) collective-permute-start(bf16[2,2,32,128]{3,2,1,0:T(8,128)(2,1)S(1)} %get-tuple-element.18), channel_id=1, source_target_pairs={{0,2},{1,3},{2,0},{3,1},{4,6},{5,7},{6,4},{7,5},{8,10},{9,11},{10,... | collective-permute-start | bytes 98312 | tf_op jit(solution)/shard_map/ppermute | solution.py:270
  9.8 0.3 %collective-permute-done.4.k_x = bf16[2,32,1024]{2,1,0:T(8,128)(2,1)S(1)} collective-permute-done((bf16[2,32,1024]{2,1,0:T(8,128)(2,1)}, bf16[2,32,1024]{2,1,0:T(8,128)(2,1)S(1)}, u32[]{:S(2)}, u32[]{:S(2)}) %collective-permute-start.4) | collective-permute-done | bytes 131104 | tf_op jit(solution)/shard_map/ppermute | solution.py:270
  10.1 0.4 %near_columns.1.near = f32[2,64,64]{2,1,0:T(8,128)S(1)} custom-call(bf16[128,1024]{1,0:T(8,128)(2,1)S(1)} %get-tuple-element.19.l_all, bf16[2,32,1024]{2,1,0:T(8,128)(2,1)S(1)} %bitcast.10, bf16[2,32,1024]{2,1,0:T(8,128)(2,1)S(1)} %collective-permute-done.3.k_core), custom_call_target="tpu_custom_call" | custom-call | flops 21474836480 | bytes 16777216 | tf_op jit(solution)/shard_map/near_columns/pallas_call | solution.py:315
  10.5 1.0 %collective-permute-done.5.k_diag = bf16[2,32,1024]{2,1,0:T(8,128)(2,1)S(1)} collective-permute-done((bf16[2,32,1024]{2,1,0:T(8,128)(2,1)S(1)}, bf16[2,32,1024]{2,1,0:T(8,128)(2,1)S(1)}, u32[]{:S(2)}, u32[]{:S(2)}) %collective-permute-start.5) | collective-permute-done | bytes 131104 | tf_op jit(solution)/shard_map/ppermute | solution.py:270
  11.5 0.5 %far_columns.1.between = bf16[2,2,32,128]{3,2,1,0:T(8,128)(2,1)S(1)} custom-call(f32[2,64,64]{2,1,0:T(8,128)S(1)} %near_columns.1.near, f32[4,32,128]{2,1,0:T(8,128)S(1)} %get-tuple-element.16.keep, bf16[128,1024]{1,0:T(8,128)(2,1)S(1)} %get-tuple-element.19.l_all, bf16[2,32,1024]{2,1,0:T(8,128)(2,1)S(1)} %collective-permute-done.4.k_x, ...), custom_call_target="tpu_custom_call" | custom-call | tf_op jit(solution)/shard_map/far_columns/pallas_call | solution.py:326
  12.0 1.9 %collective-permute-start.9 = (bf16[2,4,32,128]{3,2,1,0:T(8,128)(2,1)S(1)}, bf16[2,4,32,128]{3,2,1,0:T(8,128)(2,1)S(1)}, u32[]{:S(2)}, u32[]{:S(2)}) collective-permute-start(bf16[2,4,32,128]{3,2,1,0:T(8,128)(2,1)S(1)} %pack_rows.1.refs_0_), channel_id=1, source_target_pairs={{0,4},{1,5},{2,6},{3,7},{4,12},{5,9},{6,14},{7,11},{8,0},{9,13},{1... | collective-permute-start | bytes 196616 | tf_op jit(solution)/shard_map/ppermute | solution.py:357
  13.9 2.5 %collective-permute-start.11 = (bf16[2,4,32,128]{3,2,1,0:T(8,128)(2,1)S(1)}, bf16[2,4,32,128]{3,2,1,0:T(8,128)(2,1)S(1)}, u32[]{:S(2)}, u32[]{:S(2)}) collective-permute-start(bf16[2,4,32,128]{3,2,1,0:T(8,128)(2,1)S(1)} %pack_rows.1.refs_0_), channel_id=1, source_target_pairs={{0,12},{1,9},{2,14},{3,11},{4,8},{5,13},{6,10},{7,15},{8,4},{9,1},... | collective-permute-start | bytes 196616 | tf_op jit(solution)/shard_map/ppermute | solution.py:357
  16.3 1.6 %collective-permute-start.7 = (bf16[2,4,32,128]{3,2,1,0:T(8,128)(2,1)S(1)}, bf16[2,4,32,128]{3,2,1,0:T(8,128)(2,1)S(1)}, u32[]{:S(2)}, u32[]{:S(2)}) collective-permute-start(bf16[2,4,32,128]{3,2,1,0:T(8,128)(2,1)S(1)} %pack_rows.1.refs_0_), channel_id=1, source_target_pairs={{0,8},{1,13},{2,10},{3,15},{4,0},{5,1},{6,2},{7,3},{8,12},{9,5},{1... | collective-permute-start | bytes 196616 | tf_op jit(solution)/shard_map/ppermute | solution.py:357
  17.9 0.2 collective-permute-done.9.refs_4_
  18.1 0.3 %collective-permute-start.10 = (bf16[2,4,32,128]{3,2,1,0:T(8,128)(2,1)S(1)}, bf16[2,4,32,128]{3,2,1,0:T(8,128)(2,1)S(1)}, u32[]{:S(2)}, u32[]{:S(2)}) collective-permute-start(bf16[2,4,32,128]{3,2,1,0:T(8,128)(2,1)S(1)} %collective-permute-done.9.refs_4_), channel_id=1, source_target_pairs={{0,1},{1,0},{2,3},{3,2},{4,5},{5,4},{6,7},{7,6},{8,9},{9,8},{10,11... | collective-permute-start | bytes 196616 | tf_op jit(solution)/shard_map/ppermute | solution.py:270
  18.4 2.2 %collective-permute-done.11.refs_6_ = bf16[2,4,32,128]{3,2,1,0:T(8,128)(2,1)S(1)} collective-permute-done((bf16[2,4,32,128]{3,2,1,0:T(8,128)(2,1)S(1)}, bf16[2,4,32,128]{3,2,1,0:T(8,128)(2,1)S(1)}, u32[]{:S(2)}, u32[]{:S(2)}) %collective-permute-start.11) | collective-permute-done | bytes 65568 | tf_op jit(solution)/shard_map/ppermute | solution.py:357
  20.6 0.3 %collective-permute-done.7.refs_2_ = bf16[2,4,32,128]{3,2,1,0:T(8,128)(2,1)S(1)} collective-permute-done((bf16[2,4,32,128]{3,2,1,0:T(8,128)(2,1)S(1)}, bf16[2,4,32,128]{3,2,1,0:T(8,128)(2,1)S(1)}, u32[]{:S(2)}, u32[]{:S(2)}) %collective-permute-start.7) | collective-permute-done | bytes 65568 | tf_op jit(solution)/shard_map/ppermute | solution.py:357
  21.0 0.2 collective-permute-start.8
  21.3 0.5 %collective-permute-done.12.refs_7_ = bf16[2,4,32,128]{3,2,1,0:T(8,128)(2,1)S(1)} collective-permute-done((bf16[2,4,32,128]{3,2,1,0:T(8,128)(2,1)S(1)}, bf16[2,4,32,128]{3,2,1,0:T(8,128)(2,1)S(1)}, u32[]{:S(2)}, u32[]{:S(2)}) %collective-permute-start.12) | collective-permute-done | bytes 65568 | tf_op jit(solution)/shard_map/ppermute | solution.py:270
  21.9 0.3 %collective-permute-done.8.refs_3_ = bf16[2,4,32,128]{3,2,1,0:T(8,128)(2,1)S(1)} collective-permute-done((bf16[2,4,32,128]{3,2,1,0:T(8,128)(2,1)S(1)}, bf16[2,4,32,128]{3,2,1,0:T(8,128)(2,1)S(1)}, u32[]{:S(2)}, u32[]{:S(2)}) %collective-permute-start.8) | collective-permute-done | bytes 65568 | tf_op jit(solution)/shard_map/ppermute | solution.py:270
  22.2 1.4 %skeleton_chain.1 = bf16[512,128]{1,0:T(8,128)(2,1)} custom-call(bf16[2,4,32,128]{3,2,1,0:T(8,128)(2,1)S(1)} %pack_rows.1.refs_0_, bf16[2,4,32,128]{3,2,1,0:T(8,128)(2,1)S(1)} %collective-permute-done.6.refs_1_, bf16[2,4,32,128]{3,2,1,0:T(8,128)(2,1)S(1)} %collective-permute-done.7.refs_2_, bf16[2,4,32,128]{3,2,1,0:T(8,128)(2,1)S(1)} %collective-permute-done.8.refs_3_, ...), custom_call_target="tpu_custom_call" | custom-call | tf_op jit(solution)/shard_map/skeleton_chain/pallas_call | solution.py:361
  (17 shorter events, 0.2 us)
Async XLA Ops:
  0.0 4.5 %copy-start.3 = (s32[4,4]{1,0:T(4,128)S(1)}, s32[4,4]{1,0:T(4,128)}, u32[]{:S(2)}) copy-start(s32[4,4]{1,0:T(4,128)} %ranks.1) | copy-start | bytes 196
  0.0 3.0 %collective-permute-start = (bf16[512,128]{1,0:T(8,128)(2,1)}, bf16[512,128]{1,0:T(8,128)(2,1)S(1)}, u32[]{:S(2)}, u32[]{:S(2)}) collective-permute-start(bf16[512,128]{1,0:T(8,128)(2,1)} %bitcast.4), channel_id=1, source_target_pairs={{0,1},{1,0},{2,3},{3,2},{4,5},{5,4},{6,7},{7,6},{8,9},{9,8},{10,11... | collective-permute-start | bytes 393224 | tf_op jit(solution)/shard_map/ppermute | solution.py:270
  0.5 7.1 %collective-permute-start.1 = (bf16[2,32,1024]{2,1,0:T(8,128)(2,1)}, bf16[2,32,1024]{2,1,0:T(8,128)(2,1)S(1)}, u32[]{:S(2)}, u32[]{:S(2)}) collective-permute-start(bf16[2,32,1024]{2,1,0:T(8,128)(2,1)} %bitcast.6), channel_id=1, source_target_pairs={{0,2},{1,3},{2,0},{3,1},{4,6},{5,7},{6,4},{7,5},{8,10},{9,11},{10,... | collective-permute-start | bytes 393224 | tf_op jit(solution)/shard_map/ppermute | solution.py:270
  3.0 7.1 %collective-permute-start.4 = (bf16[2,32,1024]{2,1,0:T(8,128)(2,1)}, bf16[2,32,1024]{2,1,0:T(8,128)(2,1)S(1)}, u32[]{:S(2)}, u32[]{:S(2)}) collective-permute-start(bf16[2,32,1024]{2,1,0:T(8,128)(2,1)} %bitcast.8), channel_id=1, source_target_pairs={{0,2},{1,3},{2,0},{3,1},{4,6},{5,7},{6,4},{7,5},{8,10},{9,11},{10,... | collective-permute-start | bytes 393224 | tf_op jit(solution)/shard_map/ppermute | solution.py:270
  4.5 5.6 %collective-permute-start.3 = (bf16[2,32,1024]{2,1,0:T(8,128)(2,1)}, bf16[2,32,1024]{2,1,0:T(8,128)(2,1)S(1)}, u32[]{:S(2)}, u32[]{:S(2)}) collective-permute-start(bf16[2,32,1024]{2,1,0:T(8,128)(2,1)} %bitcast.9), channel_id=1, source_target_pairs={{0,1},{1,0},{2,3},{3,2},{4,5},{5,4},{6,7},{7,6},{8,9},{9,8},{10,11... | collective-permute-start | bytes 393224 | tf_op jit(solution)/shard_map/ppermute | solution.py:270
  4.5 0.9 %copy-start = (bf16[256,2,128]{2,1,0:T(2,128)(2,1)S(1)}, bf16[256,2,128]{2,1,0:T(2,128)(2,1)}, u32[]{:S(2)}) copy-start(bf16[256,2,128]{2,1,0:T(2,128)(2,1)} %param.4) | copy-start | bytes 393220
  5.4 0.9 %copy-start.1 = (bf16[2,1,4,8,1024]{4,3,2,1,0:T(8,128)(2,1)S(1)}, bf16[2,1,4,8,1024]{4,3,2,1,0:T(8,128)(2,1)}, u32[]{:S(2)}) copy-start(bf16[2,1,4,8,1024]{4,3,2,1,0:T(8,128)(2,1)} %param.5) | copy-start | bytes 393220
  7.6 2.6 %copy-start.2 = (bf16[2,1,4,8,1024]{4,3,2,1,0:T(8,128)(2,1)S(1)}, bf16[2,1,4,8,1024]{4,3,2,1,0:T(8,128)(2,1)}, u32[]{:S(2)}) copy-start(bf16[2,1,4,8,1024]{4,3,2,1,0:T(8,128)(2,1)} %param.6) | copy-start | bytes 393220
  7.8 4.2 %collective-permute-start.2 = (bf16[2,2,32,128]{3,2,1,0:T(8,128)(2,1)S(1)}, bf16[2,2,32,128]{3,2,1,0:T(8,128)(2,1)S(1)}, u32[]{:S(2)}, u32[]{:S(2)}) collective-permute-start(bf16[2,2,32,128]{3,2,1,0:T(8,128)(2,1)S(1)} %get-tuple-element.18), channel_id=1, source_target_pairs={{0,2},{1,3},{2,0},{3,1},{4,6},{5,7},{6,4},{7,5},{8,10},{9,11},{10,... | collective-permute-start | bytes 98312 | tf_op jit(solution)/shard_map/ppermute | solution.py:270
  10.1 1.3 %collective-permute-start.5 = (bf16[2,32,1024]{2,1,0:T(8,128)(2,1)S(1)}, bf16[2,32,1024]{2,1,0:T(8,128)(2,1)S(1)}, u32[]{:S(2)}, u32[]{:S(2)}) collective-permute-start(bf16[2,32,1024]{2,1,0:T(8,128)(2,1)S(1)} %collective-permute-done.4.k_x), channel_id=1, source_target_pairs={{0,1},{1,0},{2,3},{3,2},{4,5},{5,4},{6,7},{7,6},{8,9},{9,8},{10,11... | collective-permute-start | bytes 393224 | tf_op jit(solution)/shard_map/ppermute | solution.py:270
  12.0 6.2 %collective-permute-start.9 = (bf16[2,4,32,128]{3,2,1,0:T(8,128)(2,1)S(1)}, bf16[2,4,32,128]{3,2,1,0:T(8,128)(2,1)S(1)}, u32[]{:S(2)}, u32[]{:S(2)}) collective-permute-start(bf16[2,4,32,128]{3,2,1,0:T(8,128)(2,1)S(1)} %pack_rows.1.refs_0_), channel_id=1, source_target_pairs={{0,4},{1,5},{2,6},{3,7},{4,12},{5,9},{6,14},{7,11},{8,0},{9,13},{1... | collective-permute-start | bytes 196616 | tf_op jit(solution)/shard_map/ppermute | solution.py:357
  13.9 6.8 %collective-permute-start.11 = (bf16[2,4,32,128]{3,2,1,0:T(8,128)(2,1)S(1)}, bf16[2,4,32,128]{3,2,1,0:T(8,128)(2,1)S(1)}, u32[]{:S(2)}, u32[]{:S(2)}) collective-permute-start(bf16[2,4,32,128]{3,2,1,0:T(8,128)(2,1)S(1)} %pack_rows.1.refs_0_), channel_id=1, source_target_pairs={{0,12},{1,9},{2,14},{3,11},{4,8},{5,13},{6,10},{7,15},{8,4},{9,1},... | collective-permute-start | bytes 196616 | tf_op jit(solution)/shard_map/ppermute | solution.py:357
  16.3 4.6 %collective-permute-start.7 = (bf16[2,4,32,128]{3,2,1,0:T(8,128)(2,1)S(1)}, bf16[2,4,32,128]{3,2,1,0:T(8,128)(2,1)S(1)}, u32[]{:S(2)}, u32[]{:S(2)}) collective-permute-start(bf16[2,4,32,128]{3,2,1,0:T(8,128)(2,1)S(1)} %pack_rows.1.refs_0_), channel_id=1, source_target_pairs={{0,8},{1,13},{2,10},{3,15},{4,0},{5,1},{6,2},{7,3},{8,12},{9,5},{1... | collective-permute-start | bytes 196616 | tf_op jit(solution)/shard_map/ppermute | solution.py:357
  17.9 3.4 %collective-permute-start.6 = (bf16[2,4,32,128]{3,2,1,0:T(8,128)(2,1)S(1)}, bf16[2,4,32,128]{3,2,1,0:T(8,128)(2,1)S(1)}, u32[]{:S(2)}, u32[]{:S(2)}) collective-permute-start(bf16[2,4,32,128]{3,2,1,0:T(8,128)(2,1)S(1)} %pack_rows.1.refs_0_), channel_id=1, source_target_pairs={{0,1},{1,0},{2,3},{3,2},{4,5},{5,4},{6,7},{7,6},{8,9},{9,8},{10,11... | collective-permute-start | bytes 196616 | tf_op jit(solution)/shard_map/ppermute | solution.py:270
  18.1 3.2 %collective-permute-start.10 = (bf16[2,4,32,128]{3,2,1,0:T(8,128)(2,1)S(1)}, bf16[2,4,32,128]{3,2,1,0:T(8,128)(2,1)S(1)}, u32[]{:S(2)}, u32[]{:S(2)}) collective-permute-start(bf16[2,4,32,128]{3,2,1,0:T(8,128)(2,1)S(1)} %collective-permute-done.9.refs_4_), channel_id=1, source_target_pairs={{0,1},{1,0},{2,3},{3,2},{4,5},{5,4},{6,7},{7,6},{8,9},{9,8},{10,11... | collective-permute-start | bytes 196616 | tf_op jit(solution)/shard_map/ppermute | solution.py:270
  20.6 1.3 %collective-permute-start.12 = (bf16[2,4,32,128]{3,2,1,0:T(8,128)(2,1)S(1)}, bf16[2,4,32,128]{3,2,1,0:T(8,128)(2,1)S(1)}, u32[]{:S(2)}, u32[]{:S(2)}) collective-permute-start(bf16[2,4,32,128]{3,2,1,0:T(8,128)(2,1)S(1)} %collective-permute-done.11.refs_6_), channel_id=1, source_target_pairs={{0,1},{1,0},{2,3},{3,2},{4,5},{5,4},{6,7},{7,6},{8,9},{9,8},{10,11... | collective-permute-start | bytes 196616 | tf_op jit(solution)/shard_map/ppermute | solution.py:270
  21.0 1.3 %collective-permute-start.8 = (bf16[2,4,32,128]{3,2,1,0:T(8,128)(2,1)S(1)}, bf16[2,4,32,128]{3,2,1,0:T(8,128)(2,1)S(1)}, u32[]{:S(2)}, u32[]{:S(2)}) collective-permute-start(bf16[2,4,32,128]{3,2,1,0:T(8,128)(2,1)S(1)} %collective-permute-done.7.refs_2_), channel_id=1, source_target_pairs={{0,1},{1,0},{2,3},{3,2},{4,5},{5,4},{6,7},{7,6},{8,9},{9,8},{10,11... | collective-permute-start | bytes 196616 | tf_op jit(solution)/shard_map/ppermute | solution.py:270
